TPU v7x, 32 devices: a whole 2x2x4 slice. The times are simulated.
32 devices in a mesh: narrow: 4 (over y, x), wide: 8 (over z, core).
Axes of the slice: x: 2, y: 2, z: 4, core: 2. Of those that a mesh axis runs over, the one named last changes fastest.
Arguments:
- tokens: bfloat16 [8192, 768], P(('narrow', 'wide')), may hold values from -6 to 6
- cotangent: bfloat16 [8192, 768], P(('narrow', 'wide')), may hold values from -6 to 6
- w_query: bfloat16 [768, 768], replicated, may hold values from -0.21875 to 0.21875
- w_key: bfloat16 [768, 768], replicated, may hold values from -0.21875 to 0.21875
- w_value: bfloat16 [768, 768], replicated, may hold values from -0.21875 to 0.21875
- w_output: bfloat16 [768, 768], replicated, may hold values from -1.25 to 1.25
- gain_attn: float32 [768], replicated, may hold values from 0.5 to 1.5
- gain_ffn: float32 [768], replicated, may hold values from 0.5 to 1.5
- w_router: bfloat16 [768, 8], replicated, may hold values from -0.109375 to 0.109375
- bias_table: float32 [32, 12], replicated, may hold values from -4 to 4
- expert_in: bfloat16 [8, 768, 3072], P('wide', None, 'narrow'), may hold values from -0.21875 to 0.21875
- expert_out: bfloat16 [8, 3072, 768], P('wide', 'narrow'), may hold values from -1.75 to 1.75
- choices: int32 [8192, 1], P(('narrow', 'wide')), may hold values from 0 to 7
- router_levels: int32 [8], replicated, may hold values from 0 to 3
- buckets: int32 [511], replicated, may hold values from 0 to 31
Outputs:
- layer_output: bfloat16 [8192, 768], P(('narrow', 'wide'))
- input_grad: bfloat16 [8192, 768], P(('narrow', 'wide'))
- grad_w_query: float32 [768, 768], replicated
- grad_w_key: float32 [768, 768], replicated
- grad_w_value: float32 [768, 768], replicated
- grad_w_output: float32 [768, 768], replicated
- grad_gain_attn: float32 [768], replicated
- grad_gain_ffn: float32 [768], replicated
- grad_w_router: float32 [768, 8], replicated
- grad_bias_table: float32 [32, 12], replicated
- grad_expert_in: float32 [8, 768, 3072], P('wide', None, 'narrow')
- grad_expert_out: float32 [8, 3072, 768], P('wide', 'narrow')
All inputs are finite; a program needn't handle non-finite values.
Results may differ from a plain program's by a relative error of at most 0.018.
Values may be sent and summed in bfloat16 or wider, within the bound.
No kernel may reach another device: no remote copies, remote signals or barrier semaphores. Data moves between devices by JAX's collectives and lax.ppermute only.
A program may use at most 128 MiB of HBM per device.

v0:
```python
import jax
import jax.numpy as jnp
from jax import lax
from jax.sharding import PartitionSpec as P

epsilon = 1e-06


def rms_scale(rows):
    return lax.rsqrt(jnp.mean(rows * rows, axis=-1, keepdims=True) + epsilon)


def expand_bias(table_values, buckets):
    span_len = buckets.shape[0]
    length = (span_len + 1) // 2
    onehot = (
        buckets[:, None] == jnp.arange(table_values.shape[0], dtype=jnp.int32)[None, :]
    ).astype(jnp.float32)
    by_offset = jnp.dot(onehot, table_values, precision=lax.Precision.HIGHEST).T
    shifted = jnp.concatenate(
        [
            by_offset[:, length - 1 :],
            jnp.zeros((by_offset.shape[0], 1), jnp.float32),
            by_offset[:, : length - 1],
        ],
        axis=1,
    )
    tiled_rows = jnp.tile(shifted, (1, length))[:, : length * span_len]
    return tiled_rows.reshape(-1, length, span_len)[:, :, :length]


def local(
    tokens,
    cotangent,
    w_query,
    w_key,
    w_value,
    w_output,
    gain_attn,
    gain_ffn,
    w_router,
    bias_table,
    expert_in,
    expert_out,
    choices,
    router_levels,
    buckets,
):
    length, model_width = tokens.shape
    head_count = bias_table.shape[1]
    head_size = model_width // head_count
    scale = head_size ** (-0.5)
    experts = w_router.shape[1]
    local_experts = expert_in.shape[0]
    slot_count = (5 * length + 4 * experts - 1) // (4 * experts)
    flat_slots = experts * slot_count
    inputs = tokens.astype(jnp.float32)
    scale_one = rms_scale(inputs)
    normed_one = (inputs * scale_one * gain_attn).astype(jnp.bfloat16)
    query_rows = (
        jnp.dot(normed_one, w_query, preferred_element_type=jnp.float32)
        .astype(jnp.bfloat16)
        .reshape(length, head_count, head_size)
    )
    key_rows = (
        jnp.dot(normed_one, w_key, preferred_element_type=jnp.float32)
        .astype(jnp.bfloat16)
        .reshape(length, head_count, head_size)
    )
    value_rows = (
        jnp.dot(normed_one, w_value, preferred_element_type=jnp.float32)
        .astype(jnp.bfloat16)
        .reshape(length, head_count, head_size)
    )

    def bias_of(table_values):
        return expand_bias(table_values, buckets)

    score_bias, bias_pull = jax.vjp(bias_of, bias_table)
    scores = (
        jnp.einsum("ihd,jhd->hij", query_rows, key_rows, preferred_element_type=jnp.float32) * scale
        + score_bias
    )
    row_peak = jnp.max(scores, axis=-1, keepdims=True)
    exp_scores = jnp.exp(scores - row_peak)
    row_total = jnp.sum(exp_scores, axis=-1, keepdims=True)
    log_total = row_peak + jnp.log(row_total)
    attn_probs = exp_scores / row_total
    mixed_heads = jnp.einsum(
        "hij,jhd->ihd",
        attn_probs.astype(jnp.bfloat16),
        value_rows,
        preferred_element_type=jnp.float32,
    )
    mixed_heads = mixed_heads.astype(jnp.bfloat16).reshape(length, model_width)
    residual = inputs + jnp.dot(mixed_heads, w_output, preferred_element_type=jnp.float32)
    scale_two = rms_scale(residual)
    normed_two = (residual * scale_two * gain_ffn).astype(jnp.bfloat16)
    logits = (
        jnp.dot(normed_two, w_router, preferred_element_type=jnp.float32)
        + 0.25 * router_levels.astype(jnp.float32)[None, :]
    )
    logit_exp = jnp.exp(logits - jnp.max(logits, axis=1, keepdims=True))
    router_probs = logit_exp / jnp.sum(logit_exp, axis=1, keepdims=True)
    chosen = choices[:, 0]
    chosen_mask = chosen[:, None] == jnp.arange(experts, dtype=jnp.int32)[None, :]
    gate_value = jnp.sum(jnp.where(chosen_mask, router_probs, 0.0), axis=1)
    counts = jnp.cumsum(chosen_mask.astype(jnp.int32), axis=0)
    position = jnp.sum(jnp.where(chosen_mask, counts, 0), axis=1) - 1
    kept_mask = position < slot_count
    kept_value = kept_mask.astype(jnp.float32)
    slot_of = chosen * slot_count + jnp.minimum(position, slot_count - 1)
    target = jnp.where(kept_mask, slot_of, flat_slots)
    token_of = (
        jnp.zeros((flat_slots,), jnp.int32)
        .at[target]
        .set(jnp.arange(length, dtype=jnp.int32), mode="drop")
    )
    filled = jnp.zeros((flat_slots,), jnp.bfloat16).at[target].set(1, mode="drop")
    outgoing = (jnp.take(normed_two, token_of, axis=0) * filled[:, None]).reshape(
        experts, slot_count, model_width
    )
    arrived = lax.all_to_all(outgoing, "wide", split_axis=0, concat_axis=0, tiled=True).reshape(
        -1, local_experts, slot_count, model_width
    )
    gathered = lax.all_gather(arrived, "narrow", axis=0, tiled=True)
    pre_act = jnp.einsum("recd,edf->recf", gathered, expert_in, preferred_element_type=jnp.float32)
    hidden = jax.nn.gelu(pre_act, approximate=True).astype(jnp.bfloat16)
    partial_out = lax.psum_scatter(
        jnp.einsum("recf,efd->recd", hidden, expert_out, preferred_element_type=jnp.float32).astype(
            jnp.bfloat16
        ),
        "narrow",
        scatter_dimension=0,
        tiled=True,
    )
    full_in, full_out = (expert_in, expert_out)
    expert_result = partial_out.reshape(experts, slot_count, model_width)
    returned = lax.all_to_all(
        expert_result, "wide", split_axis=0, concat_axis=0, tiled=True
    ).reshape(flat_slots, model_width)
    picked = jnp.take(returned, slot_of, axis=0).astype(jnp.float32)
    kept_gate = gate_value * kept_value
    layer_output = (residual + kept_gate[:, None] * picked).astype(jnp.bfloat16)
    upstream = cotangent.astype(jnp.float32)
    grad_gate = jnp.sum(upstream * picked, axis=1) * kept_value
    per_token = kept_gate[:, None] * upstream
    grad_slot = (
        jnp.take(per_token, token_of, axis=0) * filled[:, None].astype(jnp.float32)
    ).astype(jnp.bfloat16)
    grad_slot = grad_slot.reshape(experts, slot_count, model_width)
    grad_arrived = lax.all_to_all(
        grad_slot, "wide", split_axis=0, concat_axis=0, tiled=True
    ).reshape(-1, local_experts, slot_count, model_width)
    grad_rows = lax.all_gather(grad_arrived, "narrow", axis=0, tiled=True)
    pre_again = jnp.einsum("recd,edf->recf", gathered, full_in, preferred_element_type=jnp.float32)
    hidden_value, gelu_pull = jax.vjp(
        lambda values: jax.nn.gelu(values, approximate=True), pre_again
    )
    hidden_again = hidden_value.astype(jnp.bfloat16)
    grad_hidden = jnp.einsum(
        "recd,efd->recf", grad_rows, full_out, preferred_element_type=jnp.float32
    )
    grad_pre = gelu_pull(grad_hidden)[0].astype(jnp.bfloat16)
    grad_out_full = jnp.einsum(
        "recf,recd->efd", hidden_again, grad_rows, preferred_element_type=jnp.float32
    )
    grad_in_full = jnp.einsum(
        "recd,recf->edf", gathered, grad_pre, preferred_element_type=jnp.float32
    )
    grad_back = lax.psum_scatter(
        jnp.einsum("recf,edf->recd", grad_pre, full_in, preferred_element_type=jnp.float32).astype(
            jnp.bfloat16
        ),
        "narrow",
        scatter_dimension=0,
        tiled=True,
    ).astype(jnp.float32)
    grad_expert_in, grad_expert_out = (grad_in_full, grad_out_full)
    grad_back = grad_back.astype(jnp.bfloat16).reshape(experts, slot_count, model_width)
    grad_sent = lax.all_to_all(grad_back, "wide", split_axis=0, concat_axis=0, tiled=True).reshape(
        flat_slots, model_width
    )
    grad_dispatch = jnp.take(grad_sent, slot_of, axis=0).astype(jnp.float32) * kept_value[:, None]
    grad_logits = (
        (grad_gate * gate_value)[:, None] * (chosen_mask.astype(jnp.float32) - router_probs)
    ).astype(jnp.bfloat16)
    grad_w_router = jnp.dot(normed_two.T, grad_logits, preferred_element_type=jnp.float32)
    grad_normed_two = grad_dispatch + jnp.dot(
        grad_logits, w_router.T, preferred_element_type=jnp.float32
    )
    grad_gain_ffn = jnp.sum(grad_normed_two * residual * scale_two, axis=0)
    weighted_two = grad_normed_two * gain_ffn
    grad_residual = (
        upstream
        + scale_two * weighted_two
        - residual * scale_two**3 * jnp.mean(weighted_two * residual, axis=1, keepdims=True)
    )
    grad_attn = grad_residual.astype(jnp.bfloat16)
    grad_w_output = jnp.dot(mixed_heads.T, grad_attn, preferred_element_type=jnp.float32)
    grad_mixed = (
        jnp.dot(grad_attn, w_output.T, preferred_element_type=jnp.float32)
        .astype(jnp.bfloat16)
        .reshape(length, head_count, head_size)
    )
    scores_again = (
        jnp.einsum("ihd,jhd->hij", query_rows, key_rows, preferred_element_type=jnp.float32) * scale
        + score_bias
    )
    probs_again = jnp.exp(scores_again - log_total)
    grad_probs = jnp.einsum(
        "ihd,jhd->hij", grad_mixed, value_rows, preferred_element_type=jnp.float32
    )
    grad_value = jnp.einsum(
        "hij,ihd->jhd",
        probs_again.astype(jnp.bfloat16),
        grad_mixed,
        preferred_element_type=jnp.float32,
    )
    grad_value = grad_value.astype(jnp.bfloat16).reshape(length, model_width)
    grad_scores = (
        probs_again * (grad_probs - jnp.sum(probs_again * grad_probs, axis=-1, keepdims=True))
    ).astype(jnp.bfloat16)
    grad_bias_table = bias_pull(grad_scores.astype(jnp.float32))[0]
    grad_query = (
        (
            jnp.einsum("hij,jhd->ihd", grad_scores, key_rows, preferred_element_type=jnp.float32)
            * scale
        )
        .astype(jnp.bfloat16)
        .reshape(length, model_width)
    )
    grad_key = (
        (
            jnp.einsum("hij,ihd->jhd", grad_scores, query_rows, preferred_element_type=jnp.float32)
            * scale
        )
        .astype(jnp.bfloat16)
        .reshape(length, model_width)
    )
    grad_w_query = jnp.dot(normed_one.T, grad_query, preferred_element_type=jnp.float32)
    grad_w_key = jnp.dot(normed_one.T, grad_key, preferred_element_type=jnp.float32)
    grad_w_value = jnp.dot(normed_one.T, grad_value, preferred_element_type=jnp.float32)
    grad_normed_one = jnp.dot(grad_query, w_query.T, preferred_element_type=jnp.float32)
    grad_normed_one = grad_normed_one + jnp.dot(
        grad_key, w_key.T, preferred_element_type=jnp.float32
    )
    grad_normed_one = grad_normed_one + jnp.dot(
        grad_value, w_value.T, preferred_element_type=jnp.float32
    )
    grad_gain_attn = jnp.sum(grad_normed_one * inputs * scale_one, axis=0)
    weighted_one = grad_normed_one * gain_attn
    input_grad = (
        grad_residual
        + scale_one * weighted_one
        - inputs * scale_one**3 * jnp.mean(weighted_one * inputs, axis=1, keepdims=True)
    )
    summed = lax.psum(
        (
            grad_w_query,
            grad_w_key,
            grad_w_value,
            grad_w_output,
            grad_gain_attn,
            grad_gain_ffn,
            grad_w_router,
            grad_bias_table,
        ),
        ("narrow", "wide"),
    )
    return (
        layer_output,
        input_grad.astype(jnp.bfloat16),
        summed[0],
        summed[1],
        summed[2],
        summed[3],
        summed[4],
        summed[5],
        summed[6],
        summed[7],
        grad_expert_in,
        grad_expert_out,
    )


def solution(mesh):
    in_specs = (
        P(("narrow", "wide"), None),
        P(("narrow", "wide"), None),
        P(),
        P(),
        P(),
        P(),
        P(),
        P(),
        P(),
        P(),
        P("wide", None, "narrow"),
        P("wide", "narrow", None),
        P(("narrow", "wide"), None),
        P(),
        P(),
    )
    out_specs = (
        P(("narrow", "wide"), None),
        P(("narrow", "wide"), None),
        P(),
        P(),
        P(),
        P(),
        P(),
        P(),
        P(),
        P(),
        P("wide", None, "narrow"),
        P("wide", "narrow", None),
    )
    return jax.shard_map(local, mesh=mesh, in_specs=in_specs, out_specs=out_specs, check_vma=False)
```

profile of v0, /device:TPU:1, one launch (start us, length us, event | category | flops | bytes accessed | tf_op | source)
XLA Modules:
  0.0 547.1 jit_solution(12840758614611164670)
XLA Ops:
  23.3 4.9 copy.65
  28.2 3.8 slice.34
  32.0 9.2 %reshape.264 = f32[12,256,511]{2,1,0:T(8,128)} reshape(f32[12,130816]{1,0:T(8,128)} %slice.34) | data formatting | bytes 12558336 | tf_op jit(solution)/shard_map/jvp()/reshape | solution.py:29
  41.1 3.7 slice.35
  44.9 3.7 copy.63
  64.4 20.0 %all_to_all.20 = bf16[8,40,768]{2,1,0:T(8,128)(2,1)} all-to-all(bf16[8,40,768]{2,1,0:T(8,128)(2,1)S(1)} %select_multiply_fusion), channel_id=1, replica_groups=mesh['narrow'=4,'wide'=8] {'wide'}, dimensions={0} | all-to-all | bytes 983040 | tf_op jit(solution)/shard_map/all_to_all | solution.py:123
  84.7 33.3 %all-gather.5.cloned.1.call-done = bf16[32,40,768]{2,1,0:T(8,128)(2,1)} async-done(((bf16[8,40,768]{2,1,0:T(8,128)(2,1)}), bf16[32,40,768]{2,1,0:T(8,128)(2,1)}) %all-gather.5.cloned.1.call-update) | async-done | bytes 1966096 | tf_op jit(solution)/shard_map/all_gather | solution.py:126
  118.0 3.6 fusion.44
  123.5 3.9 convert_bitcast_fusion.1
  127.5 34.2 %reduce-scatter.3.cloned.1.call-done = bf16[8,1,40,768]{3,2,0,1:T(8,128)(2,1)} async-done(((bf16[32,1,40,768]{3,2,0,1:T(8,128)(2,1)}), bf16[8,1,40,768]{3,2,0,1:T(8,128)(2,1)}) %reduce-scatter.3.cloned.1.call-update) | async-done | bytes 491536 | tf_op jit(solution)/shard_map/reduce_scatter | solution.py:129
  161.7 5.3 all-to-all-start.1
  167.4 13.4 %all-to-all-done.1 = bf16[8,40,768]{2,1,0:T(8,128)(2,1)S(1)} async-done(((bf16[8,40,768]{2,1,0:T(8,128)(2,1)}), bf16[8,40,768]{2,1,0:T(8,128)(2,1)S(1)}, u32[]{:S(2)}, u32[]{:S(2)}) %all-to-all-start.1) | async-done | bytes 491552 | tf_op jit(solution)/shard_map/all_to_all | solution.py:139
  188.6 17.6 %all_to_all.21 = bf16[8,40,768]{2,1,0:T(8,128)(2,1)} all-to-all(bf16[8,40,768]{2,1,0:T(8,128)(2,1)S(1)} %multiply_convert_fusion.1), channel_id=1, replica_groups=mesh['narrow'=4,'wide'=8] {'wide'}, dimensions={0} | all-to-all | bytes 983040 | tf_op jit(solution)/shard_map/all_to_all | solution.py:152
  206.5 32.3 %all-gather.7.cloned.1.call-done = bf16[32,40,768]{2,1,0:T(8,128)(2,1)} async-done(((bf16[8,40,768]{2,1,0:T(8,128)(2,1)}), bf16[32,40,768]{2,1,0:T(8,128)(2,1)}) %all-gather.7.cloned.1.call-update) | async-done | bytes 1966096 | tf_op jit(solution)/shard_map/all_gather | solution.py:155
  238.8 6.9 %fusion.6 = bf16[32,1,40,768]{3,2,0,1:T(8,128)(2,1)S(1)} fusion(f32[32,40,768]{2,1,0:T(8,128)} %copy-done.74, bf16[32,40,768]{2,1,0:T(8,128)(2,1)} %all-gather.7.cloned.1.call-done, bf16[1,768,768]{2,1,0:T(8,128)(2,1)S(1)} %copy-done), kind=kOutput, calls=%fused_computation.16 | convolution fusion | flops 1529610240 | bytes 9043968 | tf_op jit(solution)/shard_map/recd,efd->recf/dot_general | solution.py:161
  251.0 6.2 %fusion.25 = f32[1,768,768]{2,1,0:T(8,128)} fusion(bf16[32,40,768]{2,1,0:T(8,128)(2,1)} %all-gather.7.cloned.1.call-done, f32[32,40,768]{2,1,0:T(8,128)} %copy-done.74), kind=kOutput, calls=%fused_computation.48 | convolution fusion | flops 1518796800 | bytes 8257536 | tf_op jit(solution)/shard_map/recf,recd->efd/dot_general | solution.py:165
  257.2 27.1 %reduce-scatter.5.cloned.1.call-done = bf16[8,1,40,768]{3,2,0,1:T(8,128)(2,1)} async-done(((bf16[32,1,40,768]{3,2,0,1:T(8,128)(2,1)}), bf16[8,1,40,768]{3,2,0,1:T(8,128)(2,1)}) %reduce-scatter.5.cloned.1.call-update) | async-done | bytes 491536 | tf_op jit(solution)/shard_map/reduce_scatter | solution.py:171
  284.4 5.3 all-to-all-start.3
  290.1 5.3 fusion.28
  295.4 8.0 %all-to-all-done.3 = bf16[8,40,768]{2,1,0:T(8,128)(2,1)S(1)} async-done(((bf16[8,40,768]{2,1,0:T(8,128)(2,1)}), bf16[8,40,768]{2,1,0:T(8,128)(2,1)S(1)}, u32[]{:S(2)}, u32[]{:S(2)}) %all-to-all-start.3) | async-done | bytes 491552 | tf_op jit(solution)/shard_map/all_to_all | solution.py:181
  325.5 6.7 %reshape.283 = bf16[12,130816]{1,0:T(8,128)(2,1)} reshape(bf16[12,256,511]{2,1,0:T(8,128)(2,1)S(1)} %pad.14.clone) | data formatting | bytes 6279168 | tf_op jit(solution)/shard_map/transpose(jvp())/reshape | solution.py:29
  342.1 5.1 copy.66
  350.3 40.1 %all-reduce.4 = (f32[768]{0:T(1024)}, f32[768]{0:T(1024)}, f32[768,8]{0,1:T(8,128)}, f32[32,12]{0,1:T(8,128)}) all-reduce(f32[768]{0:T(1024)S(1)} %get-tuple-element.15, f32[768]{0:T(1024)S(1)} %copy-done.66, f32[768,8]{0,1:T(8,128)S(1)} %copy-done.39, f32[32,12]{0,1:T(8,128)S(1)} %fusion.61), channel_id=1, replica_groups=mesh['narrow'=4,'wide'=8] {'narrow','wide'}, use_global_device_ids=true, to_apply=%region_23.25 | all-reduce | flops 8064 | bytes 64512 | tf_op jit(solution)/shard_map/psum | solution.py:258
  391.5 139.1 %all-reduce.8.cloned.1.call-done = (f32[768,768]{1,0:T(8,128)}, f32[768,768]{1,0:T(8,128)}, f32[768,768]{1,0:T(8,128)}, f32[768,768]{1,0:T(8,128)}) async-done(((f32[768,768]{1,0:T(8,128)}, f32[768,768]{1,0:T(8,128)}, f32[768,768]{1,0:T(8,128)}, f32[768,768]{1,0:T(8,128)}), (f32[768,768]{1,0:T(8,128)}, f32[768,768]{1,0:T(8,128)}, f32[768,768]{1,0:T(8,128)}, ...) | async-done | bytes 9437200 | tf_op jit(solution)/shard_map/psum | solution.py:258
  (247 shorter events, 93.6 us)
Async XLA Ops:
  7.2 116.3 %copy-start = (bf16[1,768,768]{2,1,0:T(8,128)(2,1)S(1)}, bf16[1,768,768]{2,1,0:T(8,128)(2,1)}, u32[]{:S(2)}) copy-start(bf16[1,768,768]{2,1,0:T(8,128)(2,1)} %param.28) | copy-start | bytes 3538948
  7.2 110.8 %all-gather.5.cloned.1.call-start = ((), (), s32[]{:S(2)}) async-start(), calls=%async_computation.8 | async-start | bytes 2457600 | tf_op jit(solution)/shard_map/all_gather | solution.py:126
  13.3 154.0 %copy-start.60 = (pred[256]{0:T(512)(128)(4,1)}, pred[256]{0:T(512)(128)(4,1)S(1)}, u32[]{:S(2)}) copy-start(pred[256]{0:T(512)(128)(4,1)S(1)} %get-tuple-element.38) | copy-start | bytes 772
  17.7 30.8 %copy-start.42 = (f32[256]{0:T(256)}, f32[256]{0:T(256)S(1)}, u32[]{:S(2)}) copy-start(f32[256]{0:T(256)S(1)} %get-tuple-element.34) | copy-start | bytes 3076
  19.8 31.1 %copy-start.13 = (bf16[256,768]{0,1:T(8,128)(2,1)}, bf16[256,768]{0,1:T(8,128)(2,1)S(1)}, u32[]{:S(2)}) copy-start(bf16[256,768]{0,1:T(8,128)(2,1)S(1)} %copy.50) | copy-start | bytes 1179652
  20.6 30.4 %copy-start.15 = (bf16[256,768]{0,1:T(8,128)(2,1)}, bf16[256,768]{0,1:T(8,128)(2,1)S(1)}, u32[]{:S(2)}) copy-start(bf16[256,768]{0,1:T(8,128)(2,1)S(1)} %copy.51) | copy-start | bytes 1179652
  56.7 248.1 %copy-start.9 = (f32[256,768]{1,0:T(8,128)}, f32[256,768]{1,0:T(8,128)S(1)}, u32[]{:S(2)}) copy-start(f32[256,768]{1,0:T(8,128)S(1)} %get-tuple-element.42) | copy-start | bytes 2359300
  84.4 77.3 %reduce-scatter.3.cloned.1.call-start = ((), (), s32[]{:S(2)}) async-start(), calls=%async_computation.6 | async-start | bytes 2457600 | tf_op jit(solution)/shard_map/reduce_scatter | solution.py:129
  123.5 43.5 %copy-start.73 = (s32[8]{0:T(128)S(1)}, s32[8]{0:T(128)}, u32[]{:S(2)}) copy-start(s32[8]{0:T(128)} %param.30) | copy-start | bytes 100
  123.5 43.5 %copy-start.50 = (bf16[768,8]{0,1:T(8,128)(2,1)S(1)}, bf16[768,8]{0,1:T(8,128)(2,1)}, u32[]{:S(2)}) copy-start(bf16[768,8]{0,1:T(8,128)(2,1)} %param.25) | copy-start | bytes 36868
  127.4 39.9 %copy-start.44 = (s32[256,1]{0,1:T(1,128)S(1)}, s32[256,1]{0,1:T(1,128)}, u32[]{:S(2)}) copy-start(s32[256,1]{0,1:T(1,128)} %param.29) | copy-start | bytes 3076
  127.5 55.2 %copy-start.56 = (s32[1024]{0:T(1024)}, s32[1024]{0:T(1024)S(1)}, u32[]{:S(2)}) copy-start(s32[1024]{0:T(1024)S(1)} %pad_clamp_fusion) | copy-start | bytes 12292
  161.7 19.1 %all-to-all-start.1 = ((bf16[8,40,768]{2,1,0:T(8,128)(2,1)}), bf16[8,40,768]{2,1,0:T(8,128)(2,1)S(1)}, u32[]{:S(2)}, u32[]{:S(2)}) async-start(bf16[8,40,768]{2,1,0:T(8,128)(2,1)} %bitcast.189), calls=%async_computation.2 | async-start | bytes 983040 | tf_op jit(solution)/shard_map/all_to_all | solution.py:139
  167.0 71.9 %all-gather.7.cloned.1.call-start = ((), (), s32[]{:S(2)}) async-start(), calls=%async_computation.9 | async-start | bytes 2457600 | tf_op jit(solution)/shard_map/all_gather | solution.py:155
  167.3 15.4 %copy-start.35 = (f32[256,8]{0,1:T(8,128)}, f32[256,8]{0,1:T(8,128)S(1)}, u32[]{:S(2)}) copy-start(f32[256,8]{0,1:T(8,128)S(1)} %get-tuple-element.44) | copy-start | bytes 24580
  167.3 15.4 %copy-start.46 = (f32[256]{0:T(256)}, f32[256]{0:T(256)S(1)}, u32[]{:S(2)}) copy-start(f32[256]{0:T(256)S(1)} %get-tuple-element.43) | copy-start | bytes 3076
  167.3 15.4 %copy-start.52 = (f32[256]{0:T(256)}, f32[256]{0:T(256)S(1)}, u32[]{:S(2)}) copy-start(f32[256]{0:T(256)S(1)} %fusion.73) | copy-start | bytes 3076
  167.4 15.3 %copy-start.54 = (f32[256]{0:T(256)}, f32[256]{0:T(256)S(1)}, u32[]{:S(2)}) copy-start(f32[256]{0:T(256)S(1)} %select_reduce_fusion) | copy-start | bytes 3076
  167.4 19.8 %copy-start.59 = (f32[256]{0:T(256)}, f32[256]{0:T(256)S(1)}, u32[]{:S(2)}) copy-start(f32[256]{0:T(256)S(1)} %broadcast_select_fusion.1) | copy-start | bytes 3076
  206.2 78.1 %reduce-scatter.5.cloned.1.call-start = ((), (), s32[]{:S(2)}) async-start(), calls=%async_computation.7 | async-start | bytes 2457600 | tf_op jit(solution)/shard_map/reduce_scatter | solution.py:171
  284.4 19.1 %all-to-all-start.3 = ((bf16[8,40,768]{2,1,0:T(8,128)(2,1)}), bf16[8,40,768]{2,1,0:T(8,128)(2,1)S(1)}, u32[]{:S(2)}, u32[]{:S(2)}) async-start(bf16[8,40,768]{2,1,0:T(8,128)(2,1)} %bitcast.188), calls=%async_computation.5 | async-start | bytes 983040 | tf_op jit(solution)/shard_map/all_to_all | solution.py:181
  289.6 240.9 %all-reduce.8.cloned.1.call-start = ((), (), s32[]{:S(2)}) async-start(), calls=%async_computation.10 | async-start | bytes 18874368 | tf_op jit(solution)/shard_map/psum | solution.py:258
  349.0 41.4 %copy-start.8 = (f32[256,768]{1,0:T(8,128)S(1)}, f32[256,768]{1,0:T(8,128)}, u32[]{:S(2)}) copy-start(f32[256,768]{1,0:T(8,128)} %copy-done.6) | copy-start | bytes 2359300
  349.6 40.8 %copy-start.63 = (f32[256]{0:T(256)S(1)}, f32[256]{0:T(256)}, u32[]{:S(2)}) copy-start(f32[256]{0:T(256)} %get-tuple-element.33) | copy-start | bytes 3076
  (58 other events, 245.4 us)
Sparse Core Ops, SparseCore 0:
  84.5 33.4 all-gather.4
  127.5 34.0 reduce-scatter.2
  206.4 32.4 all-gather.6
  250.2 34.0 reduce-scatter.4
  339.5 191.0 all-reduce.7
where the time goes:
time: 556 us; the launch traced here: 547 us
  waiting for transfers between devices  288 us (52%)
  blocking collectives  77.7 us (14%)
  local copies, waits for them, and re-layouts  75.3 us (14%)
  matrix products  58 us (10%)
  other arithmetic  22 us (4%)
  between operations  15 us (3%)
  starting transfers between devices  11.6 us (2%)
    psum x1, waiting for transfers between devices, local(): lax.psum((grad_w_query, grad_w_key, grad_w_value, grad_w_output, grad_gai...  139 us
    psum x1, blocking collectives, local(): lax.psum((grad_w_query, grad_w_key, grad_w_value, grad_w_output, grad_gai...  40.1 us
    reduce_scatter x1, waiting for transfers between devices, local(): lax.psum_scatter(jnp.einsum('recf,efd->recd', hidden, expert_out, preferr...  34.2 us
    all_gather x1, waiting for transfers between devices, local(): gathered = lax.all_gather(arrived, 'narrow', axis=0, tiled=True)  33.3 us
    unnamed x159, local copies, waits for them, and re-layouts  33 us
    all_gather x1, waiting for transfers between devices, local(): grad_rows = lax.all_gather(grad_arrived, 'narrow', axis=0, tiled=True)  32.3 us
    reduce_scatter x1, waiting for transfers between devices, local(): lax.psum_scatter(jnp.einsum('recf,edf->recd', grad_pre, full_in, preferre...  27.1 us
    all_to_all x1, blocking collectives, local(): lax.all_to_all(outgoing, 'wide', split_axis=0, concat_axis=0, tiled=True)  20 us
  transfers between devices with their start and end apart: 7, of which 7 were waited for; matrix products, arithmetic and copies ran while one was open for 4% of the time, Pallas kernels for 0%

commit v1 on v0

v1 whole, which is shorter than its diff:
```python
import functools

import jax
import jax.numpy as jnp
from jax import lax
from jax.experimental import pallas as pl
from jax.experimental.pallas import tpu as pltpu
from jax.sharding import PartitionSpec as P

epsilon = 1e-06
BF = jnp.bfloat16
F32 = jnp.float32
VMEM_LIMIT = 56 * 2**20


def mm(a, b):
    return lax.dot_general(a, b, (((1,), (0,)), ((), ())), preferred_element_type=F32)


def mm_nt(a, b):
    return lax.dot_general(a, b, (((1,), (1,)), ((), ())), preferred_element_type=F32)


def mm_tn(a, b):
    return lax.dot_general(a, b, (((0,), (0,)), ((), ())), preferred_element_type=F32)


def rms_scale(rows):
    return lax.rsqrt(jnp.mean(rows * rows, axis=-1, keepdims=True) + epsilon)


def half_masks(rows, width):
    lane = lax.broadcasted_iota(jnp.int32, (rows, width), 1)
    low = (lane < width // 2).astype(F32)
    return low.astype(BF), (1.0 - low).astype(BF)


def call(kernel, outs, *args, flops=0, transcendentals=0, scratch=(), smem=0):
    out_bytes = sum(o.size * o.dtype.itemsize for o in outs)
    in_bytes = sum(a.size * a.dtype.itemsize for a in args)
    specs = [pl.BlockSpec(memory_space=pltpu.SMEM)] * smem
    specs += [pl.BlockSpec(memory_space=pltpu.VMEM)] * (len(args) - smem)
    return pl.pallas_call(
        kernel,
        out_shape=tuple(outs),
        in_specs=specs,
        out_specs=tuple(pl.BlockSpec(memory_space=pltpu.VMEM) for _ in outs),
        scratch_shapes=list(scratch),
        compiler_params=pltpu.CompilerParams(vmem_limit_bytes=VMEM_LIMIT),
        cost_estimate=pl.CostEstimate(
            flops=flops, transcendentals=transcendentals, bytes_accessed=in_bytes + out_bytes
        ),
    )(*args)


def shaped(shape, dtype=BF):
    return jax.ShapeDtypeStruct(shape, dtype)


def front_kernel(
    heads,
    cap,
    tokens,
    cotangent,
    w_query,
    w_key,
    w_value,
    w_output,
    gain_attn,
    gain_ffn,
    w_router,
    table,
    spread,
    choices,
    levels,
    normed_one_out,
    query_out,
    key_out,
    value_out,
    probs_out,
    mixed_out,
    residual_out,
    normed_two_out,
    router_out,
    target_out,
    slots_out,
    grads_out,
):
    length, width = tokens.shape
    scale = (width // heads) ** (-0.5)
    experts = w_router.shape[1]
    flat_slots = slots_out.shape[0]
    inputs = tokens[...].astype(F32)
    normed = (inputs * rms_scale(inputs) * gain_attn[...]).astype(BF)
    normed_one_out[...] = normed
    query_out[...] = mm(normed, w_query[...]).astype(BF)
    key_out[...] = mm(normed, w_key[...]).astype(BF)
    value_out[...] = mm(normed, w_value[...]).astype(BF)
    buckets_n = table.shape[0]
    onehot = (
        lax.broadcasted_iota(jnp.int32, (buckets_n, 2 * length), 0) == spread[...]
    ).astype(F32)
    by_offset = lax.dot_general(
        table[...],
        onehot,
        (((0,), (0,)), ((), ())),
        precision=lax.Precision.HIGHEST,
        preferred_element_type=F32,
    )
    pair = 2 * width // heads
    masks = half_masks(length, pair)
    for p in range(heads // 2):
        at = slice(p * pair, (p + 1) * pair)
        q2, k2, v2 = query_out[:, at], key_out[:, at], value_out[:, at]
        probs = []
        for half in (0, 1):
            h = 2 * p + half
            base = jnp.broadcast_to(by_offset[h : h + 1, :], (length, 2 * length))
            bias = pltpu.roll(base, 0, 1, stride=1, stride_axis=0)[:, :length]
            scores = mm_nt(q2, k2 * masks[half]) * scale + bias
            e = jnp.exp(scores - jnp.max(scores, axis=-1, keepdims=True))
            e = (e / jnp.sum(e, axis=-1, keepdims=True)).astype(BF)
            probs_out[h] = e
            probs.append(e)
        mixed_out[:, at] = mm(
            jnp.concatenate(probs, axis=1),
            jnp.concatenate([v2 * masks[0], v2 * masks[1]], axis=0),
        ).astype(BF)
    residual = inputs + mm(mixed_out[...], w_output[...])
    residual_out[...] = residual
    normed_two = (residual * rms_scale(residual) * gain_ffn[...]).astype(BF)
    normed_two_out[...] = normed_two
    logits = mm(normed_two, w_router[...]) + 0.25 * levels[...].astype(F32)
    logit_exp = jnp.exp(logits - jnp.max(logits, axis=1, keepdims=True))
    router = logit_exp / jnp.sum(logit_exp, axis=1, keepdims=True)
    router_out[...] = router
    chosen = choices[...]
    mask = chosen == lax.broadcasted_iota(jnp.int32, (length, experts), 1)
    mask_f = mask.astype(F32)
    earlier = (
        lax.broadcasted_iota(jnp.int32, (length, length), 1)
        < lax.broadcasted_iota(jnp.int32, (length, length), 0)
    ).astype(F32)
    counts = mm(earlier.astype(BF), mask_f.astype(BF))
    position = jnp.sum(mask_f * counts, axis=1, keepdims=True).astype(jnp.int32)
    target = jnp.where(position < cap, chosen * cap + position, -1)
    target_out[...] = target
    gate = jnp.sum(mask_f * router, axis=1, keepdims=True)
    place = (target == lax.broadcasted_iota(jnp.int32, (length, flat_slots), 1)).astype(F32)
    place = place.astype(BF)
    slots_out[...] = mm_tn(place, normed_two).astype(BF)
    sent = (gate * cotangent[...].astype(F32)).astype(BF)
    grads_out[...] = mm_tn(place, sent).astype(BF)


def expert_forward_kernel(r0, r1a, r1b, r2a, r2b, r3a, r3b, w_in, w_out, hidden, slope, *outs):
    keep_a, send_a, keep_b, send_b = outs
    half = r1a.shape[0]
    c = 0.7978845608028654
    pieces = (
        (r0[:half], keep_a, 0),
        (r0[half:], keep_b, 0),
        (r1a[...], send_a, 0),
        (r1b[...], keep_b, 1),
        (r2a[...], keep_a, 1),
        (r2b[...], send_b, 0),
        (r3a[...], send_a, 1),
        (r3b[...], send_b, 1),
    )
    for i, (rows, out, slot) in enumerate(pieces):
        pre = mm(rows, w_in[...])
        square = pre * pre
        t = jnp.tanh(c * pre * (1.0 + 0.044715 * square))
        act = (0.5 * pre * (1.0 + t)).astype(BF)
        hidden[i] = act
        slope[i] = (
            0.5 * (1.0 + t) + 0.5 * c * pre * (1.0 - t * t) * (1.0 + 3 * 0.044715 * square)
        ).astype(BF)
        out[slot] = mm(act, w_out[...]).astype(BF)


def expert_backward_kernel(r0, r1a, r1b, r2a, r2b, r3a, r3b, w_in, w_out, slope, grad_pre, *outs):
    keep_a, send_a, keep_b, send_b = outs
    half = r1a.shape[0]
    pieces = (
        (r0[:half], keep_a, 0),
        (r0[half:], keep_b, 0),
        (r1a[...], send_a, 0),
        (r1b[...], keep_b, 1),
        (r2a[...], keep_a, 1),
        (r2b[...], send_b, 0),
        (r3a[...], send_a, 1),
        (r3b[...], send_b, 1),
    )
    for i, (rows, out, slot) in enumerate(pieces):
        g = (mm_nt(rows, w_out[...]) * slope[i].astype(F32)).astype(BF)
        grad_pre[i] = g
        out[slot] = mm_nt(g, w_in[...]).astype(BF)


def expert_weights_kernel(x0, x1, x2, x3, x4, x5, x6, g0, g1, g2, g3, g4, g5, g6, hidden, grad_pre, grad_in, grad_out):
    half = x1.shape[0]
    xs = jnp.concatenate([x0[...], x1[...], x2[...], x3[...], x4[...], x5[...], x6[...]], axis=0)
    gs = jnp.concatenate([g0[...], g1[...], g2[...], g3[...], g4[...], g5[...], g6[...]], axis=0)
    width = grad_in.shape[1]
    act = hidden[...].reshape(8 * half, -1)
    pre = grad_pre[...].reshape(8 * half, -1)
    step = 256
    for i in range(width // step):
        grad_in[0, i * step : (i + 1) * step, :] = mm_tn(xs[:, i * step : (i + 1) * step], pre)
    for i in range(act.shape[1] // step):
        grad_out[0, i * step : (i + 1) * step, :] = mm_tn(act[:, i * step : (i + 1) * step], gs)


def store_halves(core, h, value, keep, send):
    @pl.when(core == h)
    def _():
        keep[...] = value

    @pl.when(core != h)
    def _():
        send[...] = value


def middle_kernel(
    core_ref,
    target,
    choices,
    router,
    normed_two,
    residual_ref,
    cotangent,
    returned,
    returned_grad,
    gain_ffn,
    w_router,
    mixed,
    w_output,
    layer_output,
    grad_residual_out,
    grad_mixed_out,
    keep,
    send,
    grad_gain_out,
    grad_router_out,
):
    core = core_ref[0]
    length, width = residual_ref.shape
    experts = router.shape[1]
    residual = residual_ref[...]
    upstream = cotangent[...].astype(F32)
    goal = target[...]
    place = (
        goal == lax.broadcasted_iota(jnp.int32, (length, returned.shape[0]), 1)
    ).astype(F32)
    place = place.astype(BF)
    picked = mm(place, returned[...])
    kept = (goal >= 0).astype(F32)
    mask = (choices[...] == lax.broadcasted_iota(jnp.int32, (length, experts), 1)).astype(F32)
    probs = router[...]
    gate = jnp.sum(mask * probs, axis=1, keepdims=True)
    layer_output[...] = (residual + gate * kept * picked).astype(BF)
    grad_gate = jnp.sum(upstream * picked, axis=1, keepdims=True) * kept
    grad_logits = ((grad_gate * gate) * (mask - probs)).astype(BF)
    grad_router_out[...] = mm_tn(grad_logits, normed_two[...])
    grad_two = mm(place, returned_grad[...]) + mm_nt(grad_logits, w_router[...])
    scale_two = rms_scale(residual)
    grad_gain_out[...] = jnp.sum(grad_two * residual * scale_two, axis=0, keepdims=True)
    weighted = grad_two * gain_ffn[...]
    grad_residual = (
        upstream
        + scale_two * weighted
        - residual * (scale_two**3 * jnp.mean(weighted * residual, axis=1, keepdims=True))
    )
    grad_residual_out[...] = grad_residual
    grad_attn = grad_residual.astype(BF)
    half = width // 2
    for h in (0, 1):
        value = mm_tn(mixed[:, h * half : (h + 1) * half], grad_attn).astype(BF)
        store_halves(core, h, value, keep, send)
    grad_mixed_out[...] = mm_nt(grad_attn, w_output[...]).astype(BF)


def attention_backward_kernel(
    heads,
    core_ref,
    normed_one,
    query,
    key,
    value,
    probs,
    grad_mixed,
    spread,
    grad_all,
    keep,
    send,
    grad_table,
    stack,
):
    core = core_ref[0]
    length, width = query.shape
    scale = (width // heads) ** (-0.5)
    pair = 2 * width // heads
    masks = half_masks(length, pair)
    for p in range(heads // 2):
        at = slice(p * pair, (p + 1) * pair)
        q2, k2, v2, g2 = query[:, at], key[:, at], value[:, at], grad_mixed[:, at]
        attn, grads = [], []
        for half in (0, 1):
            h = 2 * p + half
            e = probs[h]
            attn.append(e)
            e = e.astype(F32)
            grad_probs = mm_nt(g2, v2 * masks[half])
            gs = e * (grad_probs - jnp.sum(e * grad_probs, axis=-1, keepdims=True))
            stack[h] = gs
            grads.append(gs.astype(BF))
        grad_q = mm(
            jnp.concatenate(grads, axis=1),
            jnp.concatenate([k2 * masks[0], k2 * masks[1]], axis=0),
        )
        grad_k = mm_tn(
            jnp.concatenate(grads, axis=0),
            jnp.concatenate([q2 * masks[0], q2 * masks[1]], axis=0),
        )
        grad_v = mm_tn(
            jnp.concatenate(attn, axis=0),
            jnp.concatenate([g2 * masks[0], g2 * masks[1]], axis=0),
        )
        grad_all[:, p * pair : (p + 1) * pair] = (grad_q * scale).astype(BF)
        grad_all[:, width + p * pair : width + (p + 1) * pair] = (grad_k * scale).astype(BF)
        grad_all[:, 2 * width + p * pair : 2 * width + (p + 1) * pair] = grad_v.astype(BF)
    half = width // 2
    for h in (0, 1):
        value_h = mm_tn(normed_one[:, h * half : (h + 1) * half], grad_all[...]).astype(BF)
        store_halves(core, h, value_h, keep, send)

    blocks = length // 8
    zeros = jnp.zeros((heads * 8, length), F32)

    def block(a):
        rows = stack[:, pl.ds(pl.multiple_of(a * 8, 8), 8), :].reshape(heads * 8, length)
        return jnp.concatenate([rows, zeros], axis=1)

    def step(i, total):
        return block(blocks - 2 - i) + pltpu.roll(total, 2 * length - 8, 1)

    total = lax.fori_loop(0, blocks - 1, step, block(blocks - 1))
    row = lax.broadcasted_iota(jnp.int32, total.shape, 0) % 8
    for bit in (1, 2, 4):
        total = jnp.where((row & bit) != 0, pltpu.roll(total, 2 * length - bit, 1), total)
    by_offset = jnp.sum(total.reshape(heads, 8, 2 * length), axis=1)
    onehot = (
        lax.broadcasted_iota(jnp.int32, (grad_table.shape[1], 2 * length), 0) == spread[...]
    ).astype(F32)
    grad_table[...] = lax.dot_general(
        by_offset,
        onehot,
        (((1,), (1,)), ((), ())),
        precision=lax.Precision.HIGHEST,
        preferred_element_type=F32,
    )


def input_kernel(
    grad_all,
    w_query,
    w_key,
    w_value,
    tokens,
    gain_attn,
    grad_residual,
    grad_gain_ffn,
    grad_router,
    grad_table,
    input_grad,
    small,
):
    width = tokens.shape[1]
    grad = mm_nt(grad_all[:, :width], w_query[...])
    grad = grad + mm_nt(grad_all[:, width : 2 * width], w_key[...])
    grad = grad + mm_nt(grad_all[:, 2 * width :], w_value[...])
    inputs = tokens[...].astype(F32)
    scale_one = rms_scale(inputs)
    gain_row = jnp.sum(grad * inputs * scale_one, axis=0, keepdims=True)
    weighted = grad * gain_attn[...]
    input_grad[...] = (
        grad_residual[...]
        + scale_one * weighted
        - inputs * (scale_one**3 * jnp.mean(weighted * inputs, axis=1, keepdims=True))
    ).astype(BF)
    experts = grad_router.shape[0]
    heads, buckets_n = grad_table.shape
    small[...] = jnp.zeros_like(small)
    small[0:1, :] = gain_row
    small[8:9, :] = grad_gain_ffn[...]
    small[16 : 16 + experts, :] = grad_router[...]
    small[16 + experts : 16 + experts + heads, :buckets_n] = grad_table[...]


def finish_kernel(place_ref, own_a, own_b, far_a, far_b, *outs):
    core, bit_x, bit_y = place_ref[0], place_ref[1], place_ref[2]
    block = own_a.shape[0] // 4
    columns = own_a.shape[1]
    width = outs[0].shape[1]
    for far, (a, b) in enumerate(((own_a, own_b), (far_a, far_b))):
        for first in (0, 1):
            for second in (0, 1):
                rows = slice((2 * first + second) * block, (2 * first + second + 1) * block)
                top = (core ^ far) * 4
                at_a = (top + (bit_x ^ first) * 2 + (bit_y ^ second)) * block
                at_b = (top + (bit_y ^ first) * 2 + (bit_x ^ second)) * block
                for m, out in enumerate(outs):
                    for source, at, left in ((a, at_a, 0), (b, at_b, columns)):
                        low = max(m * width, left)
                        high = min((m + 1) * width, left + columns)
                        if low < high:
                            out[
                                pl.ds(pl.multiple_of(at, block), block),
                                low - m * width : high - m * width,
                            ] = source[rows, low - left : high - left].astype(F32)


def pairs(size, k):
    return [(i, i ^ k) for i in range(size)]


def local(
    n_narrow,
    n_wide,
    tokens,
    cotangent,
    w_query,
    w_key,
    w_value,
    w_output,
    gain_attn,
    gain_ffn,
    w_router,
    bias_table,
    expert_in,
    expert_out,
    choices,
    router_levels,
    buckets,
):
    length, width = tokens.shape
    heads = bias_table.shape[1]
    buckets_n = bias_table.shape[0]
    experts = w_router.shape[1]
    cap = (5 * length + 4 * experts - 1) // (4 * experts)
    flat_slots = experts * cap
    half = flat_slots // 2
    core = lax.axis_index("wide") % 2
    bit_x = lax.axis_index("narrow") % 2
    bit_y = lax.axis_index("narrow") // 2
    core_ref = core.astype(jnp.int32).reshape(1)
    gain_attn = gain_attn.reshape(1, width)
    gain_ffn = gain_ffn.reshape(1, width)
    spread = jnp.concatenate(
        [buckets[length - 1 :], jnp.zeros((1,), jnp.int32), buckets[: length - 1]]
    ).reshape(1, 2 * length)
    rows_bf = shaped((length, width))
    attn_flops = 4 * length * length * width

    def across(x, k):
        return lax.ppermute(x, "narrow", pairs(n_narrow, k))

    def along(x, k):
        return lax.ppermute(x, "wide", pairs(n_wide, k))

    (
        normed_one,
        query,
        key,
        value,
        probs,
        mixed,
        residual,
        normed_two,
        router,
        target,
        slots,
        slot_grads,
    ) = call(
        functools.partial(front_kernel, heads, cap),
        [
            rows_bf,
            rows_bf,
            rows_bf,
            rows_bf,
            shaped((heads, length, length)),
            rows_bf,
            shaped((length, width), F32),
            rows_bf,
            shaped((length, experts), F32),
            shaped((length, 1), jnp.int32),
            shaped((flat_slots, width)),
            shaped((flat_slots, width)),
        ],
        tokens,
        cotangent,
        w_query,
        w_key,
        w_value,
        w_output,
        gain_attn,
        gain_ffn,
        w_router,
        bias_table,
        spread,
        choices,
        router_levels.reshape(1, experts),
        flops=8 * length * width * width + attn_flops,
        transcendentals=heads * length * length,
    )

    def exchange(x):
        return lax.all_to_all(x, "wide", split_axis=0, concat_axis=0, tiled=True)

    def gather(x):
        a, b = x[:half], x[half:]
        r1a, r2b = across(a, 1), across(b, 2)
        r2a, r1b = across(a, 2), across(b, 1)
        r3a, r3b = across(r1a, 2), across(r2b, 1)
        return (x, r1a, r1b, r2a, r2b, r3a, r3b)

    def reduce(keep_a, send_a, keep_b, send_b):
        got_a, got_b = across(send_a, 1), across(send_b, 2)
        next_a = (keep_a[1].astype(F32) + got_a[1].astype(F32)).astype(BF)
        next_b = (keep_b[1].astype(F32) + got_b[1].astype(F32)).astype(BF)
        last_a, last_b = across(next_a, 2), across(next_b, 1)
        sum_a = keep_a[0].astype(F32) + got_a[0].astype(F32) + last_a.astype(F32)
        sum_b = keep_b[0].astype(F32) + got_b[0].astype(F32) + last_b.astype(F32)
        return jnp.concatenate([sum_a.astype(BF), sum_b.astype(BF)], axis=0)

    w_in = expert_in.reshape(width, -1)
    w_out = expert_out.reshape(-1, width)
    units = w_in.shape[1]
    rows = gather(exchange(slots))
    row_grads = gather(exchange(slot_grads))
    piece = shaped((2, half, width))
    eight = shaped((8, half, units))
    expert_flops = 2 * 8 * half * width * units
    hidden, slope, *partial = call(
        expert_forward_kernel,
        [eight, eight, piece, piece, piece, piece],
        *rows,
        w_in,
        w_out,
        flops=2 * expert_flops,
        transcendentals=8 * half * units,
    )
    returned = exchange(reduce(*partial))
    grad_pre, *partial = call(
        expert_backward_kernel,
        [eight, piece, piece, piece, piece],
        *row_grads,
        w_in,
        w_out,
        slope,
        flops=2 * expert_flops,
    )
    returned_grad = exchange(reduce(*partial))
    grad_expert_in, grad_expert_out = call(
        expert_weights_kernel,
        [shaped(expert_in.shape, F32), shaped(expert_out.shape, F32)],
        *rows,
        *row_grads,
        hidden,
        grad_pre,
        flops=2 * expert_flops,
    )

    (
        layer_output,
        grad_residual,
        grad_mixed,
        output_keep,
        output_send,
        grad_gain_ffn,
        grad_router,
    ) = call(
        middle_kernel,
        [
            rows_bf,
            shaped((length, width), F32),
            rows_bf,
            shaped((width // 2, width)),
            shaped((width // 2, width)),
            shaped((1, width), F32),
            shaped((experts, width), F32),
        ],
        core_ref,
        target,
        choices,
        router,
        normed_two,
        residual,
        cotangent,
        returned,
        returned_grad,
        gain_ffn,
        w_router,
        mixed,
        w_output,
        smem=1,
        flops=4 * length * width * width,
    )
    grad_all, keep, send, grad_table = call(
        functools.partial(attention_backward_kernel, heads),
        [
            shaped((length, 3 * width)),
            shaped((width // 2, 3 * width)),
            shaped((width // 2, 3 * width)),
            shaped((heads, buckets_n), F32),
        ],
        core_ref,
        normed_one,
        query,
        key,
        value,
        probs,
        grad_mixed,
        spread,
        smem=1,
        scratch=[pltpu.VMEM((heads, length, length), F32)],
        flops=6 * length * width * width + 2 * attn_flops,
    )
    small_rows = -(-(16 + experts + heads) // 16) * 16
    input_grad, small = call(
        input_kernel,
        [rows_bf, shaped((small_rows, width), F32)],
        grad_all,
        w_query,
        w_key,
        w_value,
        tokens,
        gain_attn,
        grad_residual,
        grad_gain_ffn,
        grad_router,
        grad_table,
        flops=6 * length * width * width,
    )

    def split(x, bit):
        size = x.shape[0] // 2
        kept = lax.dynamic_slice_in_dim(x, bit * size, size, 0)
        other = lax.dynamic_slice_in_dim(x, (1 - bit) * size, size, 0)
        return kept, other

    def fold(x, bit, move, k):
        kept, other = split(x, bit)
        return (kept.astype(F32) + move(other, k).astype(F32)).astype(BF)

    depth_bits = [k for k in (2**i for i in range(1, 20)) if k < n_wide]
    place = jnp.stack([core, bit_x, bit_y]).astype(jnp.int32)

    def total(keep, send, count):
        x = (keep.astype(F32) + along(send, 1).astype(F32)).astype(BF)
        columns = x.shape[1] // 2
        a, b = x[:, :columns], x[:, columns:]
        a, b = fold(a, bit_x, across, 1), fold(b, bit_y, across, 2)
        a, b = fold(a, bit_y, across, 2), fold(b, bit_x, across, 1)
        x = jnp.concatenate([a, b], axis=1)
        for k in depth_bits:
            x = fold(x, (lax.axis_index("wide") // k) % 2, along, k)
        for k in reversed(depth_bits):
            far = along(x, k)
            bit = (lax.axis_index("wide") // k) % 2
            x = jnp.concatenate(
                [jnp.where(bit == 0, x, far), jnp.where(bit == 0, far, x)], axis=0
            )
        a, b = x[:, :columns], x[:, columns:]
        a = jnp.concatenate([a, across(a, 2)], axis=0)
        b = jnp.concatenate([b, across(b, 1)], axis=0)
        a = jnp.concatenate([a, across(a, 1)], axis=0)
        b = jnp.concatenate([b, across(b, 2)], axis=0)
        far_a, far_b = along(a, 1), along(b, 1)
        return call(
            finish_kernel,
            [shaped((width, width), F32)] * count,
            place,
            a,
            b,
            far_a,
            far_b,
            smem=1,
        )

    (grad_w_output,) = total(output_keep, output_send, 1)
    grad_w_query, grad_w_key, grad_w_value = total(keep, send, 3)
    if n_wide <= 8:
        every = lax.all_gather(small.astype(BF), ("narrow", "wide"), axis=0, tiled=False)
        small = jnp.sum(every.astype(F32), axis=0)
    else:
        small = lax.psum(small, ("narrow", "wide"))
    return (
        layer_output,
        input_grad,
        grad_w_query,
        grad_w_key,
        grad_w_value,
        grad_w_output,
        small[0],
        small[8],
        small[16 : 16 + experts].T,
        small[16 + experts : 16 + experts + heads, :buckets_n].T,
        grad_expert_in,
        grad_expert_out,
    )


def solution(mesh):
    tokens_spec = P(("narrow", "wide"), None)
    experts_in_spec = P("wide", None, "narrow")
    experts_out_spec = P("wide", "narrow", None)
    in_specs = (
        (tokens_spec, tokens_spec)
        + (P(),) * 8
        + (experts_in_spec, experts_out_spec, tokens_spec, P(), P())
    )
    out_specs = (tokens_spec, tokens_spec) + (P(),) * 8 + (experts_in_spec, experts_out_spec)
    body = functools.partial(local, mesh.shape["narrow"], mesh.shape["wide"])
    return jax.shard_map(body, mesh=mesh, in_specs=in_specs, out_specs=out_specs, check_vma=False)
```

time: 556 us -> 321 us (0.58); the launches traced: 547 us -> 320 us
  waiting for transfers between devices: 288 us -> 101 us
  starting transfers between devices: 11.6 us -> 82.7 us
  Pallas kernels: 0 us -> 70.5 us
  matrix products: 58 us -> 0 us
  blocking collectives: 77.7 us -> 20 us
  local copies, waits for them, and re-layouts: 75.3 us -> 19.3 us
  other arithmetic: 22 us -> 11.8 us
    psum x1 -> x0, waiting for transfers between devices: 139 us -> none  [local(): lax.psum((grad_w_query, grad_w_key, grad_w_value, grad_w_output, grad_gai...]
    pallas_call x0 -> x9, Pallas kernels: none -> 70.5 us  [call(): pl.pallas_call(kernel, out_shape=tuple(outs), in_specs=specs, out_specs=t...]
    ppermute x0 -> x50, waiting for transfers between devices: none -> 69 us  [the longest x36 50 us: across(): return lax.ppermute(x, 'narrow', pairs(n_narrow, k))]
    all_gather x2 -> x1, waiting for transfers between devices: 65.6 us -> 0.01 us  [local(): lax.all_gather(small.astype(BF), ('narrow', 'wide'), axis=0, tiled=False)]
    ppermute x0 -> x50, starting transfers between devices: none -> 62.2 us  [the longest x36 34.8 us: across(): return lax.ppermute(x, 'narrow', pairs(n_narrow, k))]
    reduce_scatter x2 -> x0, waiting for transfers between devices: 61.3 us -> none  [the longest x1 34.2 us: local(): lax.psum_scatter(jnp.einsum('recf,efd->recd', hidden, expert_out, preferr...]
    dot_general x29 -> x0, matrix products: 58 us -> none  [the longest x1 6.87 us: local(): jnp.einsum('recd,efd->recf', grad_rows, full_out, preferred_element_type=...]
    psum x1 -> x0, blocking collectives: 40.1 us -> none  [local(): lax.psum((grad_w_query, grad_w_key, grad_w_value, grad_w_output, grad_gai...]
  transfers between devices with their start and end apart: 7 -> 54, of which waited for: 7 -> 24; matrix products, arithmetic and copies ran while one was open for 4% -> 5% of each run, Pallas kernels for 0% -> 15%
where the time goes in v1:
time: 321 us; the launch traced here: 320 us
  waiting for transfers between devices  101 us (31%)
  starting transfers between devices  82.7 us (26%)
  Pallas kernels  70.5 us (22%)
  blocking collectives  20 us (6%)
  local copies, waits for them, and re-layouts  19.3 us (6%)
  between operations  14.6 us (5%)
  other arithmetic  11.8 us (4%)
    pallas_call x9, Pallas kernels, call(): pl.pallas_call(kernel, out_shape=tuple(outs), in_specs=specs, out_specs=t...  70.5 us
    ppermute x36, waiting for transfers between devices, across(): return lax.ppermute(x, 'narrow', pairs(n_narrow, k))  50 us
    ppermute x36, starting transfers between devices, across(): return lax.ppermute(x, 'narrow', pairs(n_narrow, k))  34.8 us
    all_to_all x3, waiting for transfers between devices, exchange(): return lax.all_to_all(x, 'wide', split_axis=0, concat_axis=0, tiled=True)  31.5 us
    ppermute x14, starting transfers between devices, along(): return lax.ppermute(x, 'wide', pairs(n_wide, k))  27.4 us
    all_to_all x3, starting transfers between devices, exchange(): return lax.all_to_all(x, 'wide', split_axis=0, concat_axis=0, tiled=True)  20.5 us
    all_to_all x1, blocking collectives, exchange(): return lax.all_to_all(x, 'wide', split_axis=0, concat_axis=0, tiled=True)  20 us
    ppermute x14, waiting for transfers between devices, along(): return lax.ppermute(x, 'wide', pairs(n_wide, k))  19 us
  transfers between devices with their start and end apart: 54, of which 24 were waited for; matrix products, arithmetic and copies ran while one was open for 5% of the time, Pallas kernels for 15%

profile of v1, /device:TPU:1, one launch (start us, length us, event | category | flops | bytes accessed | tf_op | source)
XLA Modules:
  0.0 319.5 jit_solution(1487711718804504196)
XLA Ops:
  16.2 11.3 %shard_map.238 = (bf16[256,768]{1,0:T(8,128)(2,1)}, bf16[256,768]{1,0:T(8,128)(2,1)}, bf16[256,768]{1,0:T(8,128)(2,1)}, bf16[256,768]{1,0:T(8,128)(2,1)}, bf16[1...) custom-call(bf16[256,768]{1,0:T(8,128)(2,1)} %tokens.3, ...), custom_call_target="tpu_custom_call" | custom-call | flops 1409286144 | bytes 11238944 | tf_op jit(solution)/shard_map/pallas_call | solution.py:43
  27.4 20.0 %all_to_all.44 = bf16[8,40,768]{2,1,0:T(8,128)(2,1)S(1)} all-to-all(bf16[8,40,768]{2,1,0:T(8,128)(2,1)} %bitcast.57), channel_id=1, replica_groups=mesh['narrow'=4,'wide'=8] {'wide'}, dimensions={0} | all-to-all | bytes 983040 | tf_op jit(solution)/shard_map/all_to_all | solution.py:519
  47.5 4.4 %all-to-all-start = ((bf16[8,40,768]{2,1,0:T(8,128)(2,1)}), bf16[8,40,768]{2,1,0:T(8,128)(2,1)S(1)}, u32[]{:S(2)}, u32[]{:S(2)}) async-start(bf16[8,40,768]{2,1,0:T(8,128)(2,1)} %bitcast.56), calls=%async_computation | async-start | bytes 983040 | tf_op jit(solution)/shard_map/all_to_all | solution.py:519
  53.2 12.5 %all-to-all-done = bf16[8,40,768]{2,1,0:T(8,128)(2,1)S(1)} async-done(((bf16[8,40,768]{2,1,0:T(8,128)(2,1)}), bf16[8,40,768]{2,1,0:T(8,128)(2,1)S(1)}, u32[]{:S(2)}, u32[]{:S(2)}) %all-to-all-start) | async-done | bytes 491552 | tf_op jit(solution)/shard_map/all_to_all | solution.py:519
  79.8 4.0 %collective-permute-done.2.r2a.x3 = bf16[160,768]{1,0:T(8,128)(2,1)S(1)} collective-permute-done((bf16[160,768]{1,0:T(8,128)(2,1)S(1)}, bf16[160,768]{1,0:T(8,128)(2,1)S(1)}, u32[]{:S(2)}, u32[]{:S(2)}) %collective-permute-start.2) | collective-permute-done | bytes 245792 | tf_op jit(solution)/shard_map/ppermute | solution.py:467
  90.1 9.3 %shard_map.239 = (bf16[8,160,768]{2,1,0:T(8,128)(2,1)}, bf16[8,160,768]{2,1,0:T(8,128)(2,1)}, bf16[2,160,768]{2,1,0:T(8,128)(2,1)}, bf16[2,160,768]{2,1,0:T(8,12...) custom-call(bf16[320,768]{1,0:T(8,128)(2,1)} %bitcast.52, bf16[160,768]{1,0:T(8,128)(2,1)} %copy-done.20, ...), custom_call_target="tpu_custom_call" | custom-call | flops 3019898880 | bytes 10223616 | tf_op jit(solution)/shard_map/pallas_call | solution.py:43
  102.7 9.6 %shard_map.240 = (bf16[8,160,768]{2,1,0:T(8,128)(2,1)}, bf16[2,160,768]{2,1,0:T(8,128)(2,1)}, bf16[2,160,768]{2,1,0:T(8,128)(2,1)}, bf16[2,160,768]{2,1,0:T(8,128)(2,1)}, bf16[2,160,768]{2,1,0:T(8,128)(2,1)}) custom-call(bf16[320,768]{1,0:T(8,128)(2,1)} %bitcast.50, bf16[160,768]{1,0:T(8,128)(2,1)} %copy-done.19, bf16[160,768]{1,0:T(8,128)(2,1)} %copy-done.28, ...), custom_call_target="tpu_custom_call" | custom-call | flops 3019898880 | bytes 10223616 | tf_op jit(solution)/shard_map/pallas_call | solution.py:43
  115.5 5.1 %collective-permute-done.16 = bf16[2,160,768]{2,1,0:T(8,128)(2,1)S(1)} collective-permute-done((bf16[2,160,768]{2,1,0:T(8,128)(2,1)}, bf16[2,160,768]{2,1,0:T(8,128)(2,1)S(1)}, u32[]{:S(2)}, u32[]{:S(2)}) %collective-permute-start.16) | collective-permute-done | bytes 491552 | tf_op jit(solution)/shard_map/ppermute | solution.py:467
  126.9 11.8 %all-to-all-start.1 = ((bf16[8,40,768]{2,1,0:T(8,128)(2,1)}), bf16[8,40,768]{2,1,0:T(8,128)(2,1)S(1)}, u32[]{:S(2)}, u32[]{:S(2)}) async-start(bf16[8,40,768]{2,1,0:T(8,128)(2,1)} %bitcast.13), calls=%async_computation.1 | async-start | bytes 983040 | tf_op jit(solution)/shard_map/all_to_all | solution.py:519
  140.3 6.2 %collective-permute-done.19 = bf16[160,768]{1,0:T(8,128)(2,1)S(1)} collective-permute-done((bf16[160,768]{1,0:T(8,128)(2,1)S(1)}, bf16[160,768]{1,0:T(8,128)(2,1)S(1)}, u32[]{:S(2)}, u32[]{:S(2)}) %collective-permute-start.19) | collective-permute-done | bytes 245792 | tf_op jit(solution)/shard_map/ppermute | solution.py:467
  147.4 5.2 %all-to-all-done.1 = bf16[8,40,768]{2,1,0:T(8,128)(2,1)S(1)} async-done(((bf16[8,40,768]{2,1,0:T(8,128)(2,1)}), bf16[8,40,768]{2,1,0:T(8,128)(2,1)S(1)}, u32[]{:S(2)}, u32[]{:S(2)}) %all-to-all-start.1) | async-done | bytes 491552 | tf_op jit(solution)/shard_map/all_to_all | solution.py:519
  152.6 4.3 %all-to-all-start.3 = ((bf16[8,40,768]{2,1,0:T(8,128)(2,1)}), bf16[8,40,768]{2,1,0:T(8,128)(2,1)S(1)}, u32[]{:S(2)}, u32[]{:S(2)}) async-start(bf16[8,40,768]{2,1,0:T(8,128)(2,1)} %bitcast.23), calls=%async_computation.3 | async-start | bytes 983040 | tf_op jit(solution)/shard_map/all_to_all | solution.py:519
  156.8 13.8 %all-to-all-done.3 = bf16[8,40,768]{2,1,0:T(8,128)(2,1)S(1)} async-done(((bf16[8,40,768]{2,1,0:T(8,128)(2,1)}), bf16[8,40,768]{2,1,0:T(8,128)(2,1)S(1)}, u32[]{:S(2)}, u32[]{:S(2)}) %all-to-all-start.3) | async-done | bytes 491552 | tf_op jit(solution)/shard_map/all_to_all | solution.py:519
  171.4 6.2 %shard_map.241 = (bf16[256,768]{1,0:T(8,128)(2,1)}, f32[256,768]{1,0:T(8,128)}, bf16[256,768]{1,0:T(8,128)(2,1)}, bf16[384,768]{1,0:T(8,128)(2,1)}, bf16[384,768...) custom-call(s32[1]{0:T(128)} %bitcast.core_ref, s32[256,1]{1,0:T(8,128)} %get-tuple-element.53.target, ...), custom_call_target="tpu_custom_call" | custom-call | flops 603979776 | bytes 6934532 | tf_op jit(solution)/shard_map/pallas_call | solution.py:43
  179.2 13.2 %shard_map.242 = (bf16[256,2304]{1,0:T(8,128)(2,1)}, bf16[384,2304]{1,0:T(8,128)(2,1)}, bf16[384,2304]{1,0:T(8,128)(2,1)}, f32[12,32]{1,0:T(8,128)}) custom-call(s32[1]{0:T(128)} %bitcast.core_ref, bf16[256,768]{1,0:T(8,128)(2,1)} %get-tuple-element.70.normed_one, bf16[256,768]{1,0:T(8,128)(2,1)} %get-tuple-element.71.query, ...), custom_call_target="tpu_custom_call" | custom-call | flops 1308622848 | bytes 8261124 | tf_op jit(solution)/shard_map/pallas_call | solution.py:43
  196.1 4.7 %shard_map.243 = (bf16[256,768]{1,0:T(8,128)(2,1)}, f32[48,768]{1,0:T(8,128)}) custom-call(bf16[256,2304]{1,0:T(8,128)(2,1)} %get-tuple-element.76.grad_all, bf16[768,768]{1,0:T(8,128)(2,1)} %w_query.3, bf16[768,768]{1,0:T(8,128)(2,1)} %w_key.3, bf16[768,768]{1,0:T(8,128)(2,1)} %w_value.3, bf16[256,768]{1,0:T(8,128)(2,1)} %tokens.3, ...), custom_call_target="tpu_custom_call" | custom-call | flops 905969664 | bytes 6471168 | tf_op jit(solution)/shard_map/pallas_call | solution.py:43
  217.9 4.6 %collective-permute-done.21 = bf16[192,1152]{1,0:T(8,128)(2,1)S(1)} collective-permute-done((bf16[192,1152]{1,0:T(8,128)(2,1)S(1)}, bf16[192,1152]{1,0:T(8,128)(2,1)S(1)}, u32[]{:S(2)}, u32[]{:S(2)}) %collective-permute-start.21) | collective-permute-done | bytes 442400 | tf_op jit(solution)/shard_map/ppermute | solution.py:467
  225.7 5.6 %collective-permute-done.22 = bf16[96,1152]{1,0:T(8,128)(2,1)S(1)} collective-permute-done((bf16[96,1152]{1,0:T(8,128)(2,1)S(1)}, bf16[96,1152]{1,0:T(8,128)(2,1)S(1)}, u32[]{:S(2)}, u32[]{:S(2)}) %collective-permute-start.22) | collective-permute-done | bytes 221216 | tf_op jit(solution)/shard_map/ppermute | solution.py:467
  239.5 4.6 %collective-permute-done.26 = bf16[24,2304]{1,0:T(8,128)(2,1)S(1)} collective-permute-done((bf16[24,2304]{1,0:T(8,128)(2,1)S(1)}, bf16[24,2304]{1,0:T(8,128)(2,1)S(1)}, u32[]{:S(2)}, u32[]{:S(2)}) %collective-permute-start.26) | collective-permute-done | bytes 110624 | tf_op jit(solution)/shard_map/ppermute | solution.py:470
  246.8 6.6 %collective-permute-done.27 = bf16[24,2304]{1,0:T(8,128)(2,1)S(1)} collective-permute-done((bf16[24,2304]{1,0:T(8,128)(2,1)S(1)}, bf16[24,2304]{1,0:T(8,128)(2,1)S(1)}, u32[]{:S(2)}, u32[]{:S(2)}) %collective-permute-start.27) | collective-permute-done | bytes 110624 | tf_op jit(solution)/shard_map/ppermute | solution.py:470
  270.0 12.1 %collective-permute-start.48 = (bf16[384,384]{1,0:T(8,128)(2,1)S(1)}, bf16[384,384]{1,0:T(8,128)(2,1)S(1)}, u32[]{:S(2)}, u32[]{:S(2)}) collective-permute-start(bf16[384,384]{1,0:T(8,128)(2,1)S(1)} %pad_maximum_fusion.6.own_a), channel_id=1, source_target_pairs={{0,1},{1,0},{2,3},{3,2},{4,5},{5,4},{6,7},{7,6},{8,9},{9,8},{10,11... | collective-permute-start | bytes 884744 | tf_op jit(solution)/shard_map/ppermute | solution.py:470
  282.4 4.9 %collective-permute-start.33 = (bf16[384,1152]{1,0:T(8,128)(2,1)S(1)}, bf16[384,1152]{1,0:T(8,128)(2,1)S(1)}, u32[]{:S(2)}, u32[]{:S(2)}) collective-permute-start(bf16[384,1152]{1,0:T(8,128)(2,1)S(1)} %pad_maximum_fusion.own_a), channel_id=1, source_target_pairs={{0,1},{1,0},{2,3},{3,2},{4,5},{5,4},{6,7},{7,6},{8,9},{9,8},{10,11... | collective-permute-start | bytes 2654216 | tf_op jit(solution)/shard_map/ppermute | solution.py:470
  289.3 8.1 %shard_map.246 = (f32[1,768,768]{2,1,0:T(8,128)}, f32[1,768,768]{2,1,0:T(8,128)}) custom-call(bf16[320,768]{1,0:T(8,128)(2,1)} %bitcast.53, bf16[160,768]{1,0:T(8,128)(2,1)} %copy-done.20, bf16[160,768]{1,0:T(8,128)(2,1)} %copy-done.24, bf16[160,768]{1,0:T(8,128)(2,1)} %copy-done.23, bf16[160,768]{1,0:T(8,128)(2,1)} %copy-done.21, ...), custom_call_target="tpu_custom_call" | custom-call | flops 3019898880 | bytes 12582912 | tf_op jit(solution)/shard_map/pallas_call | solution.py:43
  307.3 5.4 %shard_map.244 = (f32[768,768]{1,0:T(8,128)}, f32[768,768]{1,0:T(8,128)}, f32[768,768]{1,0:T(8,128)}) custom-call(s32[3]{0:T(128)} %pad_add_fusion.1.place_ref, bf16[384,1152]{1,0:T(8,128)(2,1)} %copy-done, bf16[384,1152]{1,0:T(8,128)(2,1)} %copy-done.1, bf16[384,1152]{1,0:T(8,128)(2,1)} %copy-done.10, bf16[384,1152]{1,0:T(8,128)(2,1)} %copy-done.11), custom_call_target="tpu_custom_call" | custom-call | bytes 10616844 | tf_op jit(solution)/shard_map/pallas_call | solution.py:43
  (227 shorter events, 111.3 us)
Async XLA Ops:
  47.5 18.2 %all-to-all-start = ((bf16[8,40,768]{2,1,0:T(8,128)(2,1)}), bf16[8,40,768]{2,1,0:T(8,128)(2,1)S(1)}, u32[]{:S(2)}, u32[]{:S(2)}) async-start(bf16[8,40,768]{2,1,0:T(8,128)(2,1)} %bitcast.56), calls=%async_computation | async-start | bytes 983040 | tf_op jit(solution)/shard_map/all_to_all | solution.py:519
  51.9 17.8 %collective-permute-start.10 = (bf16[160,768]{1,0:T(8,128)(2,1)S(1)}, bf16[160,768]{1,0:T(8,128)(2,1)S(1)}, u32[]{:S(2)}, u32[]{:S(2)}) collective-permute-start(bf16[160,768]{1,0:T(8,128)(2,1)S(1)} %bitcast.60), channel_id=1, source_target_pairs={{0,8},{8,0},{16,24},{24,16},{1,9},{9,1},{17,25},{25,17},{2,10},{10... | collective-permute-start | bytes 737288 | tf_op jit(solution)/shard_map/ppermute | solution.py:467
  68.5 15.4 %collective-permute-start.2 = (bf16[160,768]{1,0:T(8,128)(2,1)S(1)}, bf16[160,768]{1,0:T(8,128)(2,1)S(1)}, u32[]{:S(2)}, u32[]{:S(2)}) collective-permute-start(bf16[160,768]{1,0:T(8,128)(2,1)S(1)} %bitcast.65), channel_id=1, source_target_pairs={{0,16},{8,24},{16,0},{24,8},{1,17},{9,25},{17,1},{25,9},{2,18},{10... | collective-permute-start | bytes 737288 | tf_op jit(solution)/shard_map/ppermute | solution.py:467
  69.7 14.4 %collective-permute-start.1 = (bf16[160,768]{1,0:T(8,128)(2,1)S(1)}, bf16[160,768]{1,0:T(8,128)(2,1)S(1)}, u32[]{:S(2)}, u32[]{:S(2)}) collective-permute-start(bf16[160,768]{1,0:T(8,128)(2,1)S(1)} %bitcast.63), channel_id=1, source_target_pairs={{0,8},{8,0},{16,24},{24,16},{1,9},{9,1},{17,25},{25,17},{2,10},{10... | collective-permute-start | bytes 737288 | tf_op jit(solution)/shard_map/ppermute | solution.py:467
  72.4 16.7 %collective-permute-start.4 = (bf16[160,768]{1,0:T(8,128)(2,1)S(1)}, bf16[160,768]{1,0:T(8,128)(2,1)S(1)}, u32[]{:S(2)}, u32[]{:S(2)}) collective-permute-start(bf16[160,768]{1,0:T(8,128)(2,1)S(1)} %collective-permute-done.r1a.x1), channel_id=1, source_target_pairs={{0,16},{8,24},{16,0},{24,8},{1,17},{9,25},{17,1},{25,9},{2,18},{10... | collective-permute-start | bytes 737288 | tf_op jit(solution)/shard_map/ppermute | solution.py:467
  73.6 15.7 %collective-permute-start.5 = (bf16[160,768]{1,0:T(8,128)(2,1)S(1)}, bf16[160,768]{1,0:T(8,128)(2,1)S(1)}, u32[]{:S(2)}, u32[]{:S(2)}) collective-permute-start(bf16[160,768]{1,0:T(8,128)(2,1)S(1)} %collective-permute-done.3.r2b.x4), channel_id=1, source_target_pairs={{0,8},{8,0},{16,24},{24,16},{1,9},{9,1},{17,25},{25,17},{2,10},{10... | collective-permute-start | bytes 737288 | tf_op jit(solution)/shard_map/ppermute | solution.py:467
  78.6 22.1 %collective-permute-start.12 = (bf16[160,768]{1,0:T(8,128)(2,1)S(1)}, bf16[160,768]{1,0:T(8,128)(2,1)S(1)}, u32[]{:S(2)}, u32[]{:S(2)}) collective-permute-start(bf16[160,768]{1,0:T(8,128)(2,1)S(1)} %bitcast.61), channel_id=1, source_target_pairs={{0,16},{8,24},{16,0},{24,8},{1,17},{9,25},{17,1},{25,9},{2,18},{10... | collective-permute-start | bytes 737288 | tf_op jit(solution)/shard_map/ppermute | solution.py:467
  83.8 18.0 %collective-permute-start.11 = (bf16[160,768]{1,0:T(8,128)(2,1)S(1)}, bf16[160,768]{1,0:T(8,128)(2,1)S(1)}, u32[]{:S(2)}, u32[]{:S(2)}) collective-permute-start(bf16[160,768]{1,0:T(8,128)(2,1)S(1)} %bitcast.59), channel_id=1, source_target_pairs={{0,8},{8,0},{16,24},{24,16},{1,9},{9,1},{17,25},{25,17},{2,10},{10... | collective-permute-start | bytes 737288 | tf_op jit(solution)/shard_map/ppermute | solution.py:467
  84.1 17.8 %collective-permute-start.14 = (bf16[160,768]{1,0:T(8,128)(2,1)S(1)}, bf16[160,768]{1,0:T(8,128)(2,1)S(1)}, u32[]{:S(2)}, u32[]{:S(2)}) collective-permute-start(bf16[160,768]{1,0:T(8,128)(2,1)S(1)} %collective-permute-done.10.r1a.g1), channel_id=1, source_target_pairs={{0,16},{8,24},{16,0},{24,8},{1,17},{9,25},{17,1},{25,9},{2,18},{10... | collective-permute-start | bytes 737288 | tf_op jit(solution)/shard_map/ppermute | solution.py:467
  112.6 26.2 %collective-permute-start.18 = (bf16[2,160,768]{2,1,0:T(8,128)(2,1)}, bf16[2,160,768]{2,1,0:T(8,128)(2,1)S(1)}, u32[]{:S(2)}, u32[]{:S(2)}) collective-permute-start(bf16[2,160,768]{2,1,0:T(8,128)(2,1)} %get-tuple-element.67), channel_id=1, source_target_pairs={{0,16},{8,24},{16,0},{24,8},{1,17},{9,25},{17,1},{25,9},{2,18},{10... | collective-permute-start | bytes 1474568 | tf_op jit(solution)/shard_map/ppermute | solution.py:467
  121.7 18.5 %collective-permute-start.17 = (bf16[160,768]{1,0:T(8,128)(2,1)S(1)}, bf16[160,768]{1,0:T(8,128)(2,1)S(1)}, u32[]{:S(2)}, u32[]{:S(2)}) collective-permute-start(bf16[160,768]{1,0:T(8,128)(2,1)S(1)} %fusion.6), channel_id=1, source_target_pairs={{0,16},{8,24},{16,0},{24,8},{1,17},{9,25},{17,1},{25,9},{2,18},{10... | collective-permute-start | bytes 737288 | tf_op jit(solution)/shard_map/ppermute | solution.py:467
  126.9 25.6 %all-to-all-start.1 = ((bf16[8,40,768]{2,1,0:T(8,128)(2,1)}), bf16[8,40,768]{2,1,0:T(8,128)(2,1)S(1)}, u32[]{:S(2)}, u32[]{:S(2)}) async-start(bf16[8,40,768]{2,1,0:T(8,128)(2,1)} %bitcast.13), calls=%async_computation.1 | async-start | bytes 983040 | tf_op jit(solution)/shard_map/all_to_all | solution.py:519
  152.6 18.1 %all-to-all-start.3 = ((bf16[8,40,768]{2,1,0:T(8,128)(2,1)}), bf16[8,40,768]{2,1,0:T(8,128)(2,1)S(1)}, u32[]{:S(2)}, u32[]{:S(2)}) async-start(bf16[8,40,768]{2,1,0:T(8,128)(2,1)} %bitcast.23), calls=%async_computation.3 | async-start | bytes 983040 | tf_op jit(solution)/shard_map/all_to_all | solution.py:519
  156.8 144.8 %all-gather.3.cloned.1.call-start = ((), (), s32[]{:S(2)}) async-start(), calls=%async_computation.4 | async-start | bytes 2433024 | tf_op jit(solution)/shard_map/all_gather | solution.py:695
  177.7 14.9 %collective-permute-start.35 = (bf16[384,768]{1,0:T(8,128)(2,1)}, bf16[384,768]{1,0:T(8,128)(2,1)S(1)}, u32[]{:S(2)}, u32[]{:S(2)}) collective-permute-start(bf16[384,768]{1,0:T(8,128)(2,1)} %get-tuple-element.88), channel_id=1, source_target_pairs={{0,1},{1,0},{2,3},{3,2},{4,5},{5,4},{6,7},{7,6},{8,9},{9,8},{10,11... | collective-permute-start | bytes 1769480 | tf_op jit(solution)/shard_map/ppermute | solution.py:470
  192.4 20.7 %collective-permute-start.20 = (bf16[384,2304]{1,0:T(8,128)(2,1)}, bf16[384,2304]{1,0:T(8,128)(2,1)S(1)}, u32[]{:S(2)}, u32[]{:S(2)}) collective-permute-start(bf16[384,2304]{1,0:T(8,128)(2,1)} %get-tuple-element.83), channel_id=1, source_target_pairs={{0,1},{1,0},{2,3},{3,2},{4,5},{5,4},{6,7},{7,6},{8,9},{9,8},{10,11... | collective-permute-start | bytes 5308424 | tf_op jit(solution)/shard_map/ppermute | solution.py:470
  217.0 16.1 %collective-permute-start.41 = (bf16[24,768]{1,0:T(8,128)(2,1)S(1)}, bf16[24,768]{1,0:T(8,128)(2,1)S(1)}, u32[]{:S(2)}, u32[]{:S(2)}) collective-permute-start(bf16[24,768]{1,0:T(8,128)(2,1)S(1)} %constant_dynamic-slice_fusion), channel_id=1, source_target_pairs={{0,4},{1,5},{2,6},{3,7},{4,0},{5,1},{6,2},{7,3},{8,12},{9,13},{10,... | collective-permute-start | bytes 110600 | tf_op jit(solution)/shard_map/ppermute | solution.py:470
  260.4 21.8 %collective-permute-start.47 = (bf16[192,384]{1,0:T(8,128)(2,1)S(1)}, bf16[192,384]{1,0:T(8,128)(2,1)S(1)}, u32[]{:S(2)}, u32[]{:S(2)}) collective-permute-start(bf16[192,384]{1,0:T(8,128)(2,1)S(1)} %pad_maximum_fusion.11), channel_id=1, source_target_pairs={{0,16},{8,24},{16,0},{24,8},{1,17},{9,25},{17,1},{25,9},{2,18},{10... | collective-permute-start | bytes 442376 | tf_op jit(solution)/shard_map/ppermute | solution.py:467
  264.5 17.8 %collective-permute-start.30 = (bf16[192,1152]{1,0:T(8,128)(2,1)S(1)}, bf16[192,1152]{1,0:T(8,128)(2,1)S(1)}, u32[]{:S(2)}, u32[]{:S(2)}) collective-permute-start(bf16[192,1152]{1,0:T(8,128)(2,1)S(1)} %pad_maximum_fusion.4), channel_id=1, source_target_pairs={{0,8},{8,0},{16,24},{24,16},{1,9},{9,1},{17,25},{25,17},{2,10},{10... | collective-permute-start | bytes 1327112 | tf_op jit(solution)/shard_map/ppermute | solution.py:467
  268.2 19.0 %collective-permute-start.32 = (bf16[192,1152]{1,0:T(8,128)(2,1)S(1)}, bf16[192,1152]{1,0:T(8,128)(2,1)S(1)}, u32[]{:S(2)}, u32[]{:S(2)}) collective-permute-start(bf16[192,1152]{1,0:T(8,128)(2,1)S(1)} %pad_maximum_fusion.5), channel_id=1, source_target_pairs={{0,16},{8,24},{16,0},{24,8},{1,17},{9,25},{17,1},{25,9},{2,18},{10... | collective-permute-start | bytes 1327112 | tf_op jit(solution)/shard_map/ppermute | solution.py:467
  270.0 27.4 %collective-permute-start.48 = (bf16[384,384]{1,0:T(8,128)(2,1)S(1)}, bf16[384,384]{1,0:T(8,128)(2,1)S(1)}, u32[]{:S(2)}, u32[]{:S(2)}) collective-permute-start(bf16[384,384]{1,0:T(8,128)(2,1)S(1)} %pad_maximum_fusion.6.own_a), channel_id=1, source_target_pairs={{0,1},{1,0},{2,3},{3,2},{4,5},{5,4},{6,7},{7,6},{8,9},{9,8},{10,11... | collective-permute-start | bytes 884744 | tf_op jit(solution)/shard_map/ppermute | solution.py:470
  282.2 15.2 %collective-permute-start.49 = (bf16[384,384]{1,0:T(8,128)(2,1)S(1)}, bf16[384,384]{1,0:T(8,128)(2,1)S(1)}, u32[]{:S(2)}, u32[]{:S(2)}) collective-permute-start(bf16[384,384]{1,0:T(8,128)(2,1)S(1)} %pad_maximum_fusion.7.own_b), channel_id=1, source_target_pairs={{0,1},{1,0},{2,3},{3,2},{4,5},{5,4},{6,7},{7,6},{8,9},{9,8},{10,11... | collective-permute-start | bytes 884744 | tf_op jit(solution)/shard_map/ppermute | solution.py:470
  282.4 23.0 %collective-permute-start.33 = (bf16[384,1152]{1,0:T(8,128)(2,1)S(1)}, bf16[384,1152]{1,0:T(8,128)(2,1)S(1)}, u32[]{:S(2)}, u32[]{:S(2)}) collective-permute-start(bf16[384,1152]{1,0:T(8,128)(2,1)S(1)} %pad_maximum_fusion.own_a), channel_id=1, source_target_pairs={{0,1},{1,0},{2,3},{3,2},{4,5},{5,4},{6,7},{7,6},{8,9},{9,8},{10,11... | collective-permute-start | bytes 2654216 | tf_op jit(solution)/shard_map/ppermute | solution.py:470
  287.4 18.1 %collective-permute-start.34 = (bf16[384,1152]{1,0:T(8,128)(2,1)S(1)}, bf16[384,1152]{1,0:T(8,128)(2,1)S(1)}, u32[]{:S(2)}, u32[]{:S(2)}) collective-permute-start(bf16[384,1152]{1,0:T(8,128)(2,1)S(1)} %pad_maximum_fusion.1.own_b), channel_id=1, source_target_pairs={{0,1},{1,0},{2,3},{3,2},{4,5},{5,4},{6,7},{7,6},{8,9},{9,8},{10,11... | collective-permute-start | bytes 2654216 | tf_op jit(solution)/shard_map/ppermute | solution.py:470
  (61 other events, 561.1 us)
Sparse Core Ops, SparseCore 0:
  202.6 55.8 all-gather.2

commit v2 on v1

v2 whole, which is shorter than its diff:
```python
import functools

import jax
import jax.numpy as jnp
from jax import lax
from jax.experimental import pallas as pl
from jax.experimental.pallas import tpu as pltpu
from jax.sharding import PartitionSpec as P

epsilon = 1e-06
BF = jnp.bfloat16
F32 = jnp.float32
HIGH = 60 * 2**20
LOW = 12 * 2**20


def mm(a, b):
    return lax.dot_general(a, b, (((1,), (0,)), ((), ())), preferred_element_type=F32)


def mm_nt(a, b):
    return lax.dot_general(a, b, (((1,), (1,)), ((), ())), preferred_element_type=F32)


def mm_tn(a, b):
    return lax.dot_general(a, b, (((0,), (0,)), ((), ())), preferred_element_type=F32)


def rms_scale(rows):
    return lax.rsqrt(jnp.mean(rows * rows, axis=-1, keepdims=True) + epsilon)


def half_masks(rows, width):
    lane = lax.broadcasted_iota(jnp.int32, (rows, width), 1)
    low = (lane < width // 2).astype(F32)
    return low.astype(BF), (1.0 - low).astype(BF)


def as_row(ref):
    return ref[...].reshape(1, -1)


def as_column(ref):
    return ref[...].reshape(-1, 1)


def bucket_mask(count, spread):
    shape = (count, spread.shape[1])
    return (lax.broadcasted_iota(jnp.int32, shape, 0) == spread[...]).astype(F32)


class Fetched:
    def __init__(self, source, buffer, semaphore):
        self.buffer, self.copy = buffer, pltpu.make_async_copy(source, buffer, semaphore)
        self.copy.start()
        self.waiting = True

    @property
    def shape(self):
        return self.buffer.shape

    def wait(self):
        if self.waiting:
            self.copy.wait()
            self.waiting = False

    def __getitem__(self, index):
        self.wait()
        return self.buffer[index]


class Stored:
    def __init__(self, target, buffer, semaphore):
        self.buffer, self.copy = buffer, pltpu.make_async_copy(buffer, target, semaphore)
        self.sent = False
        self.dtype = buffer.dtype

    @property
    def shape(self):
        return self.buffer.shape

    def __getitem__(self, index):
        return self.buffer[index]

    def __setitem__(self, index, value):
        self.buffer[index] = value

    def send(self):
        if not self.sent:
            self.copy.start()
            self.sent = True


def large(x):
    return (
        len(x.shape) >= 2
        and x.shape[-2] % 16 == 0
        and x.shape[-1] % 128 == 0
        and x.size * x.dtype.itemsize >= 2**16
    )


def call(kernel, outs, *args, flops=0, transcendentals=0, scratch=(), smem=0, stream=True):
    out_bytes = sum(o.size * o.dtype.itemsize for o in outs)
    in_bytes = sum(a.size * a.dtype.itemsize for a in args)
    large_in = [stream and i >= smem and large(x) for i, x in enumerate(args)]
    large_out = [stream and large(x) for x in outs]
    moved = [x for x, flag in zip(args + tuple(outs), large_in + large_out) if flag]

    def body(*refs):
        operands, results = refs[: len(args)], refs[len(args) : len(args) + len(outs)]
        rest = refs[len(args) + len(outs) :]
        buffers = iter(rest[: len(moved)])
        semaphores = rest[len(moved)] if moved else None
        count = iter(range(len(moved)))
        operands = [
            Fetched(ref, next(buffers), semaphores.at[next(count)]) if flag else ref
            for ref, flag in zip(operands, large_in)
        ]
        results = [
            Stored(ref, next(buffers), semaphores.at[next(count)]) if flag else ref
            for ref, flag in zip(results, large_out)
        ]
        kernel(*operands, *results, *rest[len(moved) + bool(moved) :])
        for x in operands:
            if isinstance(x, Fetched):
                x.wait()
        for x in results:
            if isinstance(x, Stored):
                x.send()
        for x in results:
            if isinstance(x, Stored):
                x.copy.wait()

    def spec(flag):
        return pl.BlockSpec(memory_space=pl.ANY if flag else pltpu.VMEM)

    scratches = [pltpu.VMEM(x.shape, x.dtype) for x in moved]
    if moved:
        scratches.append(pltpu.SemaphoreType.DMA((len(moved),)))
    return pl.pallas_call(
        body,
        out_shape=tuple(outs),
        in_specs=[
            pl.BlockSpec(memory_space=pltpu.SMEM) if i < smem else spec(flag)
            for i, flag in enumerate(large_in)
        ],
        out_specs=tuple(spec(flag) for flag in large_out),
        scratch_shapes=scratches + list(scratch),
        compiler_params=pltpu.CompilerParams(vmem_limit_bytes=HIGH if stream else LOW),
        cost_estimate=pl.CostEstimate(
            flops=flops, transcendentals=transcendentals, bytes_accessed=in_bytes + out_bytes
        ),
    )(*args)


def shaped(shape, dtype=BF):
    return jax.ShapeDtypeStruct(shape, dtype)


def front_kernel(
    heads,
    cap,
    shift_ref,
    tokens,
    cotangent,
    w_query,
    w_key,
    w_value,
    w_output,
    gain_attn,
    gain_ffn,
    w_router,
    table,
    spread,
    choices,
    levels,
    normed_one_out,
    query_out,
    key_out,
    value_out,
    probs_out,
    mixed_out,
    residual_out,
    normed_two_out,
    router_out,
    target_out,
    *slots_out,
):
    length, width = tokens.shape
    scale = (width // heads) ** (-0.5)
    experts = w_router.shape[0]
    slot_rows = slots_out[0].shape[0]
    flat_slots = slot_rows * len(slots_out)
    inputs = tokens[...].astype(F32)
    normed = (inputs * rms_scale(inputs) * as_row(gain_attn)).astype(BF)
    normed_one_out[...] = normed
    normed_one_out.send()
    query_out[...] = mm(normed, w_query[...]).astype(BF)
    key_out[...] = mm(normed, w_key[...]).astype(BF)
    value_out[...] = mm(normed, w_value[...]).astype(BF)
    for out in (query_out, key_out, value_out):
        out.send()
    by_offset = lax.dot_general(
        table[...],
        bucket_mask(table.shape[1], spread),
        (((1,), (0,)), ((), ())),
        precision=lax.Precision.HIGHEST,
        preferred_element_type=F32,
    )
    pair = 2 * width // heads
    masks = half_masks(length, pair)
    for p in range(heads // 2):
        at = slice(p * pair, (p + 1) * pair)
        q2, k2, v2 = query_out[:, at], key_out[:, at], value_out[:, at]
        probs = []
        for half in (0, 1):
            h = 2 * p + half
            base = jnp.broadcast_to(by_offset[h : h + 1, :], (length, 2 * length))
            bias = pltpu.roll(base, 0, 1, stride=1, stride_axis=0)[:, :length]
            scores = mm_nt(q2, k2 * masks[half]) * scale + bias
            e = jnp.exp(scores - jnp.max(scores, axis=-1, keepdims=True))
            e = (e / jnp.sum(e, axis=-1, keepdims=True)).astype(BF)
            probs_out[h] = e
            probs.append(e)
        mixed_out[:, at] = mm(
            jnp.concatenate(probs, axis=1),
            jnp.concatenate([v2 * masks[0], v2 * masks[1]], axis=0),
        ).astype(BF)
    probs_out.send()
    mixed_out.send()
    residual = inputs + mm(mixed_out[...], w_output[...])
    residual_out[...] = residual
    residual_out.send()
    normed_two = (residual * rms_scale(residual) * as_row(gain_ffn)).astype(BF)
    normed_two_out[...] = normed_two
    normed_two_out.send()
    logits = mm_nt(w_router[...], normed_two) + 0.25 * as_column(levels).astype(F32)
    logit_exp = jnp.exp(logits - jnp.max(logits, axis=0, keepdims=True))
    router = logit_exp / jnp.sum(logit_exp, axis=0, keepdims=True)
    router_out[...] = router.T
    chosen = choices[...]
    mask = (chosen == lax.broadcasted_iota(jnp.int32, (experts, length), 0)).astype(F32)
    earlier = (
        lax.broadcasted_iota(jnp.int32, (length, length), 0)
        < lax.broadcasted_iota(jnp.int32, (length, length), 1)
    ).astype(F32)
    counts = mm(mask.astype(BF), earlier.astype(BF))
    position = jnp.sum(mask * counts, axis=0, keepdims=True).astype(jnp.int32)
    target = jnp.where(position < cap, (chosen ^ shift_ref[0]) * cap + position, -1)
    gate = jnp.sum(mask * router, axis=0, keepdims=True)
    row = lax.broadcasted_iota(jnp.int32, (8, length), 0)
    packed = jnp.where(
        row == 0, gate, jnp.where(row == 1, target.astype(F32), chosen.astype(F32))
    ).T
    target_out[...] = packed
    place = (target == lax.broadcasted_iota(jnp.int32, (flat_slots, length), 0)).astype(F32)
    place = place.astype(BF)
    sent = (packed[:, :1] * cotangent[...].astype(F32)).astype(BF)
    normed_slots, grad_slots = mm(place, normed_two), mm(place, sent)
    for i, out in enumerate(slots_out):
        rows = slice(i * slot_rows, (i + 1) * slot_rows)
        out[:, :width] = normed_slots[rows].astype(BF)
        out[:, width:] = grad_slots[rows].astype(BF)


def expert_kernel(*refs):
    w_in, first, w_out, second = refs[0], refs[1:5], refs[5], refs[6:10]
    hidden, grad_pre = refs[10:12], refs[12:14]
    keep_a0, keep_b0, send_a, send_b, keep_b1, keep_a1 = refs[14:]
    rows, double = first[0].shape
    width = double // 2
    c = 0.7978845608028654
    places = (
        ((keep_a0, ()), (keep_b0, ()), (send_a, (0,)), (keep_b1, ())),
        ((keep_a1, ()), (send_b, (0,)), (send_a, (1,)), (send_b, (1,))),
    )
    for i, (pieces, outs) in enumerate(zip((first, second), places)):
        both = jnp.concatenate([p[...] for p in pieces], axis=0)
        pre = mm(both[:, :width], w_in[...])
        square = pre * pre
        t = jnp.tanh(c * pre * (1.0 + 0.044715 * square))
        act = (0.5 * pre * (1.0 + t)).astype(BF)
        slope = 0.5 * (1.0 + t) + 0.5 * c * pre * (1.0 - t * t) * (1.0 + 3 * 0.044715 * square)
        grad = (mm_nt(both[:, width:], w_out[...]) * slope).astype(BF)
        hidden[i][...] = act
        hidden[i].send()
        grad_pre[i][...] = grad
        grad_pre[i].send()
        result = mm(act, w_out[...]).astype(BF)
        back = mm_nt(grad, w_in[...]).astype(BF)
        for j, (out, slot) in enumerate(outs):
            out[(*slot, slice(None), slice(0, width))] = result[j * rows : (j + 1) * rows]
            out[(*slot, slice(None), slice(width, double))] = back[j * rows : (j + 1) * rows]
            if slot != (0,):
                out.send()


def expert_weights_kernel(*refs):
    pieces, units, (grad_in, grad_out) = refs[:16], refs[16:24], refs[24:]
    width = grad_in.shape[1]
    both = jnp.concatenate([p[...] for p in pieces], axis=0)
    act = jnp.concatenate([units[i][...] for i in (0, 1, 4, 5)], axis=0)
    pre = jnp.concatenate([units[i][...] for i in (2, 3, 6, 7)], axis=0)
    step = 256
    for i in range(width // step):
        grad_in[0, i * step : (i + 1) * step, :] = mm_tn(both[:, i * step : (i + 1) * step], pre)
    grad_in.send()
    for i in range(act.shape[1] // step):
        grad_out[0, i * step : (i + 1) * step, :] = mm_tn(
            act[:, i * step : (i + 1) * step], both[:, width:]
        )


def store_halves(core, h, left, right, keep, send):
    columns = left.shape[1]

    @pl.when(core == h)
    def _():
        keep[:, :columns] = left
        keep[:, columns:] = right

    @pl.when(core != h)
    def _():
        send[:, :columns] = left
        send[:, columns:] = right


def diagonal_sums(scores):
    length = scores.shape[0]
    half = length // 2
    low, high = scores[:half], scores[half:]
    total = jnp.concatenate(
        [low[:, :half] + high[:, half:], low[:, half:], jnp.zeros_like(low[:, :half]), high[:, :half]],
        axis=1,
    )
    while total.shape[0] > 8:
        half = total.shape[0] // 2
        total = total[:half] + pltpu.roll(total[half:], 2 * length - half, 1)
    return total


def backward_kernel(
    heads,
    buckets_n,
    core_ref,
    packed,
    router,
    gain_ffn,
    w_router,
    spread,
    cotangent,
    residual_ref,
    w_output,
    value,
    probs_ref,
    normed_two,
    key,
    query,
    mixed,
    normed_one,
    w_value,
    w_query,
    w_key,
    tokens,
    gain_attn,
    *refs,
):
    returned, outs = refs[:-12], refs[-12:]
    layer_output, input_grad, keep_1, send_1, keep_2, send_2, small_out = outs[:7]
    small, grad_mixed_out, grad_value, grad_query, grad_key = outs[7:]
    core = core_ref[0]
    length, width = residual_ref.shape
    scale = (width // heads) ** (-0.5)
    experts = router.shape[1]
    slot_rows = returned[0].shape[0]
    gate, goal, chosen = packed[:, 0:1], packed[:, 1:2], packed[:, 2:3]
    if len(returned) > 1:
        back = jnp.concatenate([r[...].astype(F32) for r in returned], axis=0).astype(BF)
    else:
        back = returned[0][...]
    place = (
        goal.astype(jnp.int32)
        == lax.broadcasted_iota(jnp.int32, (length, slot_rows * len(returned)), 1)
    ).astype(F32)
    back = mm(place.astype(BF), back)
    picked = back[:, :width]
    kept = (goal >= 0).astype(F32)
    mask = (
        chosen.astype(jnp.int32) == lax.broadcasted_iota(jnp.int32, (length, experts), 1)
    ).astype(F32)
    probs = router[...]
    upstream = cotangent[...].astype(F32)
    residual = residual_ref[...]
    grad_gate = jnp.sum(upstream * picked, axis=1, keepdims=True) * kept
    grad_logits = ((grad_gate * gate) * (mask - probs)).astype(BF)
    grad_two = back[:, width:] + mm(grad_logits, w_router[...])
    scale_two = rms_scale(residual)
    weighted = grad_two * as_row(gain_ffn)
    grad_residual = (
        upstream
        + scale_two * weighted
        - residual * (scale_two**3 * jnp.mean(weighted * residual, axis=1, keepdims=True))
    )
    layer_output[...] = (residual + gate * kept * picked).astype(BF)
    layer_output.send()
    small[...] = jnp.zeros_like(small)
    small[1:2, :] = jnp.sum(grad_two * residual * scale_two, axis=0, keepdims=True)
    grad_attn = grad_residual.astype(BF)
    grad_mixed_out[...] = mm_nt(grad_attn, w_output[...]).astype(BF)
    small[2 : 2 + experts, :] = mm_tn(grad_logits, normed_two[...])
    pair = 2 * width // heads
    masks = half_masks(length, pair)
    sums = []
    for p in range(heads // 2):
        at = slice(p * pair, (p + 1) * pair)
        q2, k2, v2, g2 = query[:, at], key[:, at], value[:, at], grad_mixed_out[:, at]
        attn = probs_ref[2 * p], probs_ref[2 * p + 1]
        grads = []
        for half in (0, 1):
            e = attn[half].astype(F32)
            grad_probs = mm_nt(g2, v2 * masks[half])
            gs = e * (grad_probs - jnp.sum(e * grad_probs, axis=-1, keepdims=True))
            sums.append(diagonal_sums(gs))
            grads.append(gs.astype(BF))
        grad_v = mm_tn(
            jnp.concatenate(attn, axis=0),
            jnp.concatenate([g2 * masks[0], g2 * masks[1]], axis=0),
        )
        grad_q = mm(
            jnp.concatenate(grads, axis=1),
            jnp.concatenate([k2 * masks[0], k2 * masks[1]], axis=0),
        )
        grad_k = mm_tn(
            jnp.concatenate(grads, axis=0),
            jnp.concatenate([q2 * masks[0], q2 * masks[1]], axis=0),
        )
        grad_value[:, at] = grad_v.astype(BF)
        grad_query[:, at] = (grad_q * scale).astype(BF)
        grad_key[:, at] = (grad_k * scale).astype(BF)
    half = width // 2
    for h in (0, 1):
        at = slice(h * half, (h + 1) * half)
        left = mm_tn(mixed[:, at], grad_attn).astype(BF)
        right = mm_tn(normed_one[:, at], grad_value[...]).astype(BF)
        store_halves(core, h, left, right, keep_1, send_1)
    send_1.send()
    keep_1.send()
    for h in (0, 1):
        at = slice(h * half, (h + 1) * half)
        left = mm_tn(normed_one[:, at], grad_query[...]).astype(BF)
        right = mm_tn(normed_one[:, at], grad_key[...]).astype(BF)
        store_halves(core, h, left, right, keep_2, send_2)
    send_2.send()
    keep_2.send()
    grad_one = mm_nt(grad_value[...], w_value[...])
    grad_one = grad_one + mm_nt(grad_query[...], w_query[...])
    grad_one = grad_one + mm_nt(grad_key[...], w_key[...])
    inputs = tokens[...].astype(F32)
    scale_one = rms_scale(inputs)
    small[0:1, :] = jnp.sum(grad_one * inputs * scale_one, axis=0, keepdims=True)
    weighted = grad_one * as_row(gain_attn)
    input_grad[...] = (
        grad_residual
        + scale_one * weighted
        - inputs * (scale_one**3 * jnp.mean(weighted * inputs, axis=1, keepdims=True))
    ).astype(BF)
    input_grad.send()
    total = jnp.concatenate(sums, axis=0)
    row = lax.broadcasted_iota(jnp.int32, total.shape, 0) % 8
    for bit in (1, 2, 4):
        total = jnp.where((row & bit) != 0, pltpu.roll(total, 2 * length - bit, 1), total)
    by_offset = jnp.sum(total.reshape(heads, 8, 2 * length), axis=1)
    small[2 + experts : 2 + experts + heads, :buckets_n] = lax.dot_general(
        by_offset,
        bucket_mask(buckets_n, spread),
        (((1,), (1,)), ((), ())),
        precision=lax.Precision.HIGHEST,
        preferred_element_type=F32,
    )
    small_out[...] = small[...].astype(small_out.dtype)


def small_kernel(every, gain_attn, gain_ffn, router, table, small):
    small[...] = jnp.sum(every[...].astype(F32), axis=0)
    experts = router.shape[0]
    heads, buckets_n = table.shape
    gain_attn[...] = small[0:1, :].reshape(gain_attn.shape)
    gain_ffn[...] = small[1:2, :].reshape(gain_ffn.shape)
    router[...] = small[2 : 2 + experts, :]
    table[...] = small[2 + experts : 2 + experts + heads, :buckets_n]


def both(left, right, rows, columns):
    return left[rows, columns].astype(F32) + right[rows, columns].astype(F32)


def fold_kernel(bits, place_ref, *refs):
    count = len(refs) // 4 if len(refs) > 6 else 1
    for i, bit in enumerate(bits):
        own, got = refs[2 * i : 2 * i + 2] if count == 2 else refs[:2]
        keep, send = refs[-4 + 2 * i : len(refs) - 2 + 2 * i]
        half, columns = keep.shape
        left = 0 if count == 2 else i * columns
        for out, side in ((keep, place_ref[bit]), (send, 1 - place_ref[bit])):
            rows = pl.ds(pl.multiple_of(side * half, half), half)
            out[...] = both(own, got, rows, slice(left, left + columns)).astype(BF)


def join_kernel(bit, place_ref, own_a, got_a, own_b, got_b, keep, send):
    half = keep.shape[0]
    columns = own_a.shape[1]
    for out, side in ((keep, place_ref[bit]), (send, 1 - place_ref[bit])):
        rows = pl.ds(pl.multiple_of(side * half, half), half)
        out[:, :columns] = both(own_a, got_a, rows, slice(None)).astype(BF)
        out[:, columns:] = both(own_b, got_b, rows, slice(None)).astype(BF)


def columns_kernel(bit, place_ref, own, got, keep, send):
    columns = keep.shape[1]
    for out, side in ((keep, place_ref[bit]), (send, 1 - place_ref[bit])):
        at = pl.ds(pl.multiple_of(side * columns, columns), columns)
        out[...] = both(own, got, slice(None), at).astype(BF)


def beside_kernel(bit, place_ref, own, far, out):
    columns = own.shape[1]
    for source, side in ((own, place_ref[bit]), (far, 1 - place_ref[bit])):
        out[:, pl.ds(pl.multiple_of(side * columns, columns), columns)] = source[...]


def stack_kernel(bit, place_ref, own, far, out_a, out_b):
    rows, columns = own.shape[0], out_a.shape[1]
    for source, side in ((own, place_ref[bit]), (far, 1 - place_ref[bit])):
        at = pl.ds(pl.multiple_of(side * rows, rows), rows)
        out_a[at, :] = source[:, :columns]
        out_b[at, :] = source[:, columns:]


def double_kernel(own_a, far_a, own_b, far_b, out_a, out_b):
    rows = own_a.shape[0]
    for source, at, out in ((own_a, 0, out_a), (far_a, 1, out_a), (own_b, 0, out_b), (far_b, 1, out_b)):
        out[at * rows : (at + 1) * rows, :] = source[...]


def half_kernel(place_ref, own_a, far_a, own_b, far_b, out):
    block, columns = own_a.shape[0] // 2, own_a.shape[1]
    sources = ((own_a, 0, 0, 1, 2), (far_a, 0, 1, 1, 2), (own_b, 1, 0, 2, 1), (far_b, 1, 1, 2, 1))
    for source, side, far, bit_1, bit_2 in sources:
        for i in (0, 1):
            at = ((place_ref[bit_1] ^ far) * 2 + (place_ref[bit_2] ^ i)) * block
            out[
                pl.ds(pl.multiple_of(at, block), block), side * columns : (side + 1) * columns
            ] = source[i * block : (i + 1) * block, :]


def finish_kernel(other, count, place_ref, *refs):
    sources, outs, (buffer, semaphores) = refs[:count], refs[-2 - 2 * count : -2], refs[-2:]
    rows, width = sources[0].shape[0], outs[0].shape[1]
    side = (1 - place_ref[0]) if other else place_ref[0]
    at = pl.ds(pl.multiple_of(side * rows, rows), rows)
    copies = []
    for m, out in enumerate(outs):
        left = m % 2 * width
        buffer[m] = sources[m // 2][:, left : left + width].astype(F32)
        copies.append(pltpu.make_async_copy(buffer.at[m], out.at[at, :], semaphores.at[m]))
        copies[-1].start()
    for copy in copies:
        copy.wait()


def pairs(size, k):
    return [(i, i ^ k) for i in range(size)]


def local(
    n_narrow,
    n_wide,
    tokens,
    cotangent,
    w_query,
    w_key,
    w_value,
    w_output,
    gain_attn,
    gain_ffn,
    w_router,
    bias_table,
    expert_in,
    expert_out,
    choices,
    router_levels,
    buckets,
):
    length, width = tokens.shape
    buckets_n, heads = bias_table.shape
    experts = w_router.shape[1]
    cap = (5 * length + 4 * experts - 1) // (4 * experts)
    flat_slots = experts * cap
    direct = n_wide <= 8
    narrow_at, wide_at = lax.axis_index("narrow"), lax.axis_index("wide")
    core_ref = (wide_at % 2).reshape(1)
    shift_ref = (wide_at if direct else jnp.zeros((), jnp.int32)).reshape(1)
    w_router = w_router.T
    spread = jnp.roll(jnp.pad(buckets, (0, 1)), length + 1).reshape(1, 2 * length)
    rows_bf = shaped((length, width))
    attn_flops = 4 * length * length * width

    def across(x, k):
        return lax.ppermute(x, "narrow", pairs(n_narrow, k))

    def along(x, k):
        return lax.ppermute(x, "wide", pairs(n_wide, k))

    (
        normed_one,
        query,
        key,
        value,
        probs,
        mixed,
        residual,
        normed_two,
        router,
        packed,
        *slots,
    ) = call(
        functools.partial(front_kernel, heads, cap),
        [
            rows_bf,
            rows_bf,
            rows_bf,
            rows_bf,
            shaped((heads, length, length)),
            rows_bf,
            shaped((length, width), F32),
            rows_bf,
            shaped((length, experts), F32),
            shaped((length, 8), F32),
        ]
        + [shaped((cap if direct else flat_slots, 2 * width))] * (n_wide if direct else 1),
        shift_ref,
        tokens,
        cotangent,
        w_query,
        w_key,
        w_value,
        w_output,
        gain_attn,
        gain_ffn,
        w_router,
        bias_table.T,
        spread,
        choices.reshape(1, length),
        router_levels,
        smem=1,
        flops=8 * length * width * width + attn_flops,
        transcendentals=heads * length * length,
    )

    quarter = flat_slots // 4
    order = (0, 2, 1, 3)
    if direct:
        per = n_wide // 4
        moved = [slots[0]] + [along(slots[k], k) for k in range(1, n_wide)]
        parts = [moved[i * per : (i + 1) * per] for i in order]
    else:
        moved = lax.all_to_all(slots[0], "wide", split_axis=0, concat_axis=0, tiled=True)
        parts = [[moved[i * quarter : (i + 1) * quarter]] for i in range(4)]

    def gather(a, b):
        a1, b2 = across(a, 1), across(b, 2)
        a2, b1 = across(a, 2), across(b, 1)
        a3, b3 = across(a1, 2), across(b2, 1)
        return [a, b, a1, b1, a2, b2, a3, b3]

    quarters = [jnp.concatenate(part, axis=0) for part in parts]

    def reduce(keep_a, send_a, keep_b, send_b):
        got_a, got_b = across(send_a, 1), across(send_b, 2)
        next_a = (keep_a[1].astype(F32) + got_a[1].astype(F32)).astype(BF)
        next_b = (keep_b[1].astype(F32) + got_b[1].astype(F32)).astype(BF)
        last_a, last_b = across(next_a, 2), across(next_b, 1)
        sum_a = keep_a[0].astype(F32) + got_a[0].astype(F32) + last_a.astype(F32)
        sum_b = keep_b[0].astype(F32) + got_b[0].astype(F32) + last_b.astype(F32)
        return sum_a.astype(BF), sum_b.astype(BF)

    w_in = expert_in.reshape(width, -1)
    w_out = expert_out.reshape(-1, width)
    units = w_in.shape[1]
    piece = shaped((2, quarter, 2 * width))
    unit_rows = shaped((4 * quarter, units))
    slot_piece = shaped((quarter, 2 * width))
    expert_flops = 2 * 8 * quarter * width * units
    def experts_of(rows):
        return call(
            expert_kernel,
            [unit_rows] * 4 + [slot_piece, slot_piece, piece, piece, slot_piece, slot_piece],
            w_in,
            *rows[:4],
            w_out,
            *rows[4:],
            flops=4 * expert_flops,
            transcendentals=8 * quarter * units,
        )

    def reduced(keep_a0, keep_b0, send_a, send_b, keep_b1, keep_a1):
        return reduce((keep_a0, keep_a1), send_a, (keep_b0, keep_b1), send_b)

    first = gather(*quarters[:2])
    quarters[2], quarters[3], first[3], first[4] = lax.optimization_barrier(
        (quarters[2], quarters[3], first[3], first[4])
    )
    second = gather(*quarters[2:])
    done_1, done_2 = experts_of(first), experts_of(second)
    groups = [first, second]
    kept = done_1[:4] + done_2[:4]
    sums = [*reduced(*done_1[4:]), *reduced(*done_2[4:])]
    if direct:
        sums = [sums[i] for i in order]
        returned = [sums[k // per][k % per * cap : (k % per + 1) * cap] for k in range(n_wide)]
        returned = [returned[0]] + [along(returned[k], k) for k in range(1, n_wide)]
    else:
        returned = jnp.concatenate(sums, axis=0)
        returned = [lax.all_to_all(returned, "wide", split_axis=0, concat_axis=0, tiled=True)]
    grad_expert_in, grad_expert_out = call(
        expert_weights_kernel,
        [shaped(expert_in.shape, F32), shaped(expert_out.shape, F32)],
        *groups[0],
        *groups[1],
        *kept,
        flops=4 * expert_flops,
    )
    returned, grad_expert_in, grad_expert_out = lax.optimization_barrier(
        (returned, grad_expert_in, grad_expert_out)
    )

    half = width // 2
    small_rows = -(-(2 + experts + heads) // 16) * 16
    layer_output, input_grad, keep_1, send_1, keep_2, send_2, small = call(
        functools.partial(backward_kernel, heads, buckets_n),
        [rows_bf, rows_bf]
        + [shaped((half, 2 * width))] * 4
        + [shaped((small_rows, width), BF if direct else F32)],
        core_ref,
        packed,
        router,
        gain_ffn,
        w_router,
        spread,
        cotangent,
        residual,
        w_output,
        value,
        probs,
        normed_two,
        key,
        query,
        mixed,
        normed_one,
        w_value,
        w_query,
        w_key,
        tokens,
        gain_attn,
        *returned,
        smem=1,
        scratch=[pltpu.VMEM((small_rows, width), F32)] + [pltpu.VMEM((length, width), BF)] * 4,
        flops=16 * length * width * width + 3 * attn_flops,
    )

    place = jnp.stack(
        [wide_at % 2, narrow_at % 2, narrow_at // 2, wide_at // 2 % 2, wide_at // 4 % 2]
    ).astype(jnp.int32)
    deeper = [2**i for i in range(3, 20) if 2**i < n_wide]

    def hop(kernel, shapes, *args):
        return call(kernel, [shaped(x) for x in shapes], place, *args, smem=1, stream=False)

    def fold_first(keep, send):
        kernel = functools.partial(fold_kernel, (1, 2))
        return hop(kernel, [(half // 2, width)] * 4, keep, along(send, 1))

    def scatter(own_a, got_a, own_b, got_b):
        step = functools.partial
        own, other = hop(
            step(join_kernel, 3), [(half // 8, 2 * width)] * 2, own_a, got_a, own_b, got_b
        )
        own, other = hop(
            step(columns_kernel, 4), [(half // 8, width)] * 2, own, along(other, 2)
        )
        x = (own.astype(F32) + along(other, 4).astype(F32)).astype(BF)
        for k in deeper:
            bit, size = wide_at // k % 2, x.shape[0] // 2
            other = lax.dynamic_slice_in_dim(x, (1 - bit) * size, size, 0)
            own = lax.dynamic_slice_in_dim(x, bit * size, size, 0)
            x = (own.astype(F32) + along(other, k).astype(F32)).astype(BF)
        return x

    def spread_out(x):
        step = functools.partial
        for k in reversed(deeper):
            bit, far = wide_at // k % 2, along(x, k)
            x = jnp.concatenate([jnp.where(bit == 0, x, far), jnp.where(bit == 0, far, x)], axis=0)
        (x,) = hop(step(beside_kernel, 4), [(half // 8, 2 * width)], x, along(x, 4))
        a, b = hop(step(stack_kernel, 3), [(half // 4, width)] * 2, x, along(x, 2))
        a, b = call(
            double_kernel,
            [shaped((half // 2, width))] * 2,
            a,
            across(a, 2),
            b,
            across(b, 1),
            stream=False,
        )
        (x,) = hop(half_kernel, [(half, 2 * width)], a, across(a, 1), b, across(b, 2))
        return x

    def fold_second(own_a, send_a, own_b, send_b):
        own_a, send_a, own_b, send_b = hop(
            functools.partial(fold_kernel, (2, 1)),
            [(half // 4, width)] * 4,
            own_a,
            across(send_a, 1),
            own_b,
            across(send_b, 2),
        )
        return own_a, across(send_a, 2), own_b, across(send_b, 1)

    def finish(sources, outs=()):
        count = 2 * len(sources)
        return pl.pallas_call(
            functools.partial(finish_kernel, bool(outs), len(sources)),
            out_shape=(shaped((width, width), F32),) * count,
            in_specs=[pl.BlockSpec(memory_space=pltpu.SMEM)]
            + [pl.BlockSpec(memory_space=pltpu.VMEM)] * len(sources)
            + [pl.BlockSpec(memory_space=pl.ANY)] * len(outs),
            out_specs=(pl.BlockSpec(memory_space=pl.ANY),) * count,
            scratch_shapes=[
                pltpu.VMEM((count, half, width), F32),
                pltpu.SemaphoreType.DMA((count,)),
            ],
            input_output_aliases={1 + len(sources) + i: i for i in range(len(outs))},
            compiler_params=pltpu.CompilerParams(vmem_limit_bytes=LOW),
        )(place, *sources, *outs)

    after = lax.optimization_barrier
    first_1, first_2 = fold_first(keep_1, send_1), fold_first(keep_2, send_2)
    if direct:
        small = lax.all_gather(small, ("narrow", "wide"), axis=0, tiled=False)
    else:
        small = lax.psum(small, ("narrow", "wide"))[None]
    small = call(
        small_kernel,
        [
            shaped((width,), F32),
            shaped((width,), F32),
            shaped((experts, width), F32),
            shaped((heads, buckets_n), F32),
        ],
        small,
        scratch=[pltpu.VMEM((small_rows, width), F32)],
    )
    part_1 = spread_out(scatter(*fold_second(*first_1)))
    part_2 = spread_out(scatter(*fold_second(*first_2)))
    far_1, far_2 = along(part_1, 1), along(part_2, 1)
    near = finish((part_1, part_2))
    far_1, far_2, near, small = after((far_1, far_2, near, small))
    grad_w_output, grad_w_value, grad_w_query, grad_w_key = finish((far_1, far_2), near)
    return (
        layer_output,
        input_grad,
        grad_w_query,
        grad_w_key,
        grad_w_value,
        grad_w_output,
        small[0],
        small[1],
        small[2].T,
        small[3].T,
        grad_expert_in,
        grad_expert_out,
    )


def solution(mesh):
    tokens_spec = P(("narrow", "wide"), None)
    experts_in_spec = P("wide", None, "narrow")
    experts_out_spec = P("wide", "narrow", None)
    in_specs = (
        (tokens_spec, tokens_spec)
        + (P(),) * 8
        + (experts_in_spec, experts_out_spec, tokens_spec, P(), P())
    )
    out_specs = (tokens_spec, tokens_spec) + (P(),) * 8 + (experts_in_spec, experts_out_spec)
    body = functools.partial(local, mesh.shape["narrow"], mesh.shape["wide"])
    return jax.shard_map(body, mesh=mesh, in_specs=in_specs, out_specs=out_specs, check_vma=False)
```

time: 321 us -> 241 us (0.75)
  blocking collectives: 20 us -> 0 us
  waiting for transfers between devices: 101 us -> 81.4 us
  local copies, waits for them, and re-layouts: 19.3 us -> 5.94 us
  starting transfers between devices: 82.7 us -> 70.7 us
  other arithmetic: 11.8 us -> 1.33 us
  Pallas kernels: 70.5 us -> 66.4 us
    all_to_all x3 -> x0, waiting for transfers between devices: 31.5 us -> none  [exchange(): return lax.all_to_all(x, 'wide', split_axis=0, concat_axis=0, tiled=True)]
    all_to_all x3 -> x0, starting transfers between devices: 20.5 us -> none  [exchange(): return lax.all_to_all(x, 'wide', split_axis=0, concat_axis=0, tiled=True)]
    all_to_all x1 -> x0, blocking collectives: 20 us -> none  [exchange(): return lax.all_to_all(x, 'wide', split_axis=0, concat_axis=0, tiled=True)]
    ppermute x14 -> x26, starting transfers between devices: 27.4 us -> 42.9 us  [along(): return lax.ppermute(x, 'wide', pairs(n_wide, k))]
    ppermute x14 -> x26, waiting for transfers between devices: 19 us -> 30.7 us  [along(): return lax.ppermute(x, 'wide', pairs(n_wide, k))]
    ppermute x36, starting transfers between devices: 34.8 us -> 27.7 us  [across(): return lax.ppermute(x, 'narrow', pairs(n_narrow, k))]
    unnamed x65 -> x60, local copies, waits for them, and re-layouts: 10.7 us -> 3.68 us
    convert_element_type x19 -> x6, other arithmetic: 5.11 us -> 0.41 us  [the longest x4 0.36 us: reduce(): return (sum_a.astype(BF), sum_b.astype(BF))]
  transfers between devices with their start and end apart: 54 -> 63, of which waited for: 24 -> 29; matrix products, arithmetic and copies ran while one was open for 5% -> 1% of each run, Pallas kernels for 15% -> 15%
where the time goes in v2:
time: 241 us; the launch traced here: 240 us
  waiting for transfers between devices  81.4 us (34%)
  starting transfers between devices  70.7 us (29%)
  Pallas kernels  66.4 us (28%)
  between operations  14.8 us (6%)
  local copies, waits for them, and re-layouts  5.94 us (2%)
    pallas_call x22, Pallas kernels, call(): pl.pallas_call(body, out_shape=tuple(outs), in_specs=[pl.BlockSpec(memory...  60 us
    ppermute x36, waiting for transfers between devices, across(): return lax.ppermute(x, 'narrow', pairs(n_narrow, k))  50.7 us
    ppermute x26, starting transfers between devices, along(): return lax.ppermute(x, 'wide', pairs(n_wide, k))  42.9 us
    ppermute x26, waiting for transfers between devices, along(): return lax.ppermute(x, 'wide', pairs(n_wide, k))  30.7 us
    ppermute x36, starting transfers between devices, across(): return lax.ppermute(x, 'narrow', pairs(n_narrow, k))  27.7 us
    pallas_call x2, Pallas kernels, finish(): pl.pallas_call(functools.partial(finish_kernel, bool(outs), len(sources))...  6.4 us
  transfers between devices with their start and end apart: 63, of which 29 were waited for; matrix products, arithmetic and copies ran while one was open for 1% of the time, Pallas kernels for 15%

profile of v2, /device:TPU:1, one launch (start us, length us, event | category | flops | bytes accessed | tf_op | source)
XLA Modules:
  0.0 240.5 jit_solution(4700002437716890951)
XLA Ops:
  9.3 10.8 %shard_map.238 = (bf16[256,768]{1,0:T(8,128)(2,1)}, bf16[256,768]{1,0:T(8,128)(2,1)}, bf16[256,768]{1,0:T(8,128)(2,1)}, bf16[256,768]{1,0:T(8,128)(2,1)}, bf16[1...) custom-call(s32[1]{0:T(128)} %bitcast.1.refs_0_, ...), custom_call_target="tpu_custom_call" | custom-call | flops 1409286144 | bytes 11246116 | tf_op jit(solution)/shard_map/pallas_call | solution.py:141
  20.2 3.8 %collective-permute-start.1 = (bf16[40,1536]{1,0:T(8,128)(2,1)}, bf16[40,1536]{1,0:T(8,128)(2,1)S(1)}, u32[]{:S(2)}, u32[]{:S(2)}) collective-permute-start(bf16[40,1536]{1,0:T(8,128)(2,1)} %get-tuple-element.139), channel_id=1, source_target_pairs={{0,4},{1,5},{2,6},{3,7},{4,0},{5,1},{6,2},{7,3},{8,12},{9,13},{10,... | collective-permute-start | bytes 368648 | tf_op jit(solution)/shard_map/ppermute | solution.py:613
  27.0 6.2 %collective-permute-done.1 = bf16[40,1536]{1,0:T(8,128)(2,1)S(1)} collective-permute-done((bf16[40,1536]{1,0:T(8,128)(2,1)}, bf16[40,1536]{1,0:T(8,128)(2,1)S(1)}, u32[]{:S(2)}, u32[]{:S(2)}) %collective-permute-start.1) | collective-permute-done | bytes 122912 | tf_op jit(solution)/shard_map/ppermute | solution.py:613
  33.1 3.5 %collective-permute-start.6 = (bf16[40,1536]{1,0:T(8,128)(2,1)}, bf16[40,1536]{1,0:T(8,128)(2,1)S(1)}, u32[]{:S(2)}, u32[]{:S(2)}) collective-permute-start(bf16[40,1536]{1,0:T(8,128)(2,1)} %get-tuple-element.143), channel_id=1, source_target_pairs={{0,6},{1,7},{2,4},{3,5},{4,2},{5,3},{6,0},{7,1},{8,14},{9,15},{10,... | collective-permute-start | bytes 368648 | tf_op jit(solution)/shard_map/ppermute | solution.py:613
  40.9 3.7 %collective-permute-done.7 = bf16[40,1536]{1,0:T(8,128)(2,1)S(1)} collective-permute-done((bf16[40,1536]{1,0:T(8,128)(2,1)}, bf16[40,1536]{1,0:T(8,128)(2,1)S(1)}, u32[]{:S(2)}, u32[]{:S(2)}) %collective-permute-start.7) | collective-permute-done | bytes 122912 | tf_op jit(solution)/shard_map/ppermute | solution.py:613
  45.5 6.8 %collective-permute-done.8.refs_4_.refs_3_ = bf16[80,1536]{1,0:T(8,128)(2,1)S(1)} collective-permute-done((bf16[80,1536]{1,0:T(8,128)(2,1)S(1)}, bf16[80,1536]{1,0:T(8,128)(2,1)S(1)}, u32[]{:S(2)}, u32[]{:S(2)}) %collective-permute-start.8) | collective-permute-done | bytes 245792 | tf_op jit(solution)/shard_map/ppermute | solution.py:610
  55.3 3.7 %collective-permute-done.11.refs_8_.refs_6_ = bf16[80,1536]{1,0:T(8,128)(2,1)S(1)} collective-permute-done((bf16[80,1536]{1,0:T(8,128)(2,1)S(1)}, bf16[80,1536]{1,0:T(8,128)(2,1)S(1)}, u32[]{:S(2)}, u32[]{:S(2)}) %collective-permute-start.11) | collective-permute-done | bytes 245792 | tf_op jit(solution)/shard_map/ppermute | solution.py:610
  60.5 3.8 %collective-permute-done.19.refs_7_.refs_13_ = bf16[80,1536]{1,0:T(8,128)(2,1)S(1)} collective-permute-done((bf16[80,1536]{1,0:T(8,128)(2,1)S(1)}, bf16[80,1536]{1,0:T(8,128)(2,1)S(1)}, u32[]{:S(2)}, u32[]{:S(2)}) %collective-permute-start.19) | collective-permute-done | bytes 245792 | tf_op jit(solution)/shard_map/ppermute | solution.py:610
  66.3 7.0 %shard_map.239 = (bf16[320,768]{1,0:T(8,128)(2,1)}, bf16[320,768]{1,0:T(8,128)(2,1)}, bf16[320,768]{1,0:T(8,128)(2,1)}, bf16[320,768]{1,0:T(8,128)(2,1)}, bf16[8...) custom-call(bf16[768,768]{1,0:T(8,128)(2,1)} %bitcast.62, ...), custom_call_target="tpu_custom_call" | custom-call | flops 3019898880 | bytes 8257536 | tf_op jit(solution)/shard_map/pallas_call | solution.py:141
  75.0 7.2 %shard_map.240 = (bf16[320,768]{1,0:T(8,128)(2,1)}, bf16[320,768]{1,0:T(8,128)(2,1)}, bf16[320,768]{1,0:T(8,128)(2,1)}, bf16[320,768]{1,0:T(8,128)(2,1)}, bf16[8...) custom-call(bf16[768,768]{1,0:T(8,128)(2,1)} %bitcast.63, ...), custom_call_target="tpu_custom_call" | custom-call | flops 3019898880 | bytes 8257536 | tf_op jit(solution)/shard_map/pallas_call | solution.py:141
  87.0 13.0 %collective-permute-done.14 = bf16[80,1536]{1,0:T(8,128)(2,1)S(1)} collective-permute-done((bf16[80,1536]{1,0:T(8,128)(2,1)S(1)}, bf16[80,1536]{1,0:T(8,128)(2,1)S(1)}, u32[]{:S(2)}, u32[]{:S(2)}) %collective-permute-start.14) | collective-permute-done | bytes 245792 | tf_op jit(solution)/shard_map/ppermute | solution.py:610
  100.8 3.2 %collective-permute-start.15 = (bf16[40,1536]{1,0:T(8,128)(2,1)S(1)}, bf16[40,1536]{1,0:T(8,128)(2,1)S(1)}, u32[]{:S(2)}, u32[]{:S(2)}) collective-permute-start(bf16[40,1536]{1,0:T(8,128)(2,1)S(1)} %get-tuple-element.248), channel_id=1, source_target_pairs={{0,1},{1,0},{2,3},{3,2},{4,5},{5,4},{6,7},{7,6},{8,9},{9,8},{10,11... | collective-permute-start | bytes 368648 | tf_op jit(solution)/shard_map/ppermute | solution.py:613
  108.2 5.1 %collective-permute-done.23 = bf16[80,1536]{1,0:T(8,128)(2,1)S(1)} collective-permute-done((bf16[80,1536]{1,0:T(8,128)(2,1)S(1)}, bf16[80,1536]{1,0:T(8,128)(2,1)S(1)}, u32[]{:S(2)}, u32[]{:S(2)}) %collective-permute-start.23) | collective-permute-done | bytes 245792 | tf_op jit(solution)/shard_map/ppermute | solution.py:610
  120.5 8.2 %shard_map.241 = (f32[1,768,768]{2,1,0:T(8,128)}, f32[1,768,768]{2,1,0:T(8,128)}) custom-call(bf16[80,1536]{1,0:T(8,128)(2,1)} %copy-done.20, bf16[80,1536]{1,0:T(8,128)(2,1)} %copy-done.19, bf16[80,1536]{1,0:T(8,128)(2,1)} %copy-done.22, bf16[80,1536]{1,0:T(8,128)(2,1)} %copy-done.24, bf16[80,1536]{1,0:T(8,128)(2,1)} %copy-done.21, ...), custom_call_target="tpu_custom_call" | custom-call | flops 3019898880 | bytes 12582912 | tf_op jit(solution)/shard_map/pallas_call | solution.py:141
  129.7 15.7 %shard_map.242 = (bf16[256,768]{1,0:T(8,128)(2,1)}, bf16[256,768]{1,0:T(8,128)(2,1)}, bf16[384,1536]{1,0:T(8,128)(2,1)}, bf16[384,1536]{1,0:T(8,128)(2,1)}, bf16...) custom-call(s32[1]{0:T(128)} %bitcast.refs_0_, f32[256,8]{1,0:T(8,128)} %get-tuple-element.127.refs_1_, ...), custom_call_target="tpu_custom_call" | custom-call | flops 3019898880 | bytes 16797700 | tf_op jit(solution)/shard_map/pallas_call | solution.py:141
  154.9 4.7 %collective-permute-done.35.refs_2_ = bf16[192,768]{1,0:T(8,128)(2,1)S(1)} collective-permute-done((bf16[192,768]{1,0:T(8,128)(2,1)S(1)}, bf16[192,768]{1,0:T(8,128)(2,1)S(1)}, u32[]{:S(2)}, u32[]{:S(2)}) %collective-permute-start.35) | collective-permute-done | bytes 294944 | tf_op jit(solution)/shard_map/ppermute | solution.py:610
  162.3 3.8 %collective-permute-done.49.refs_2_ = bf16[192,768]{1,0:T(8,128)(2,1)S(1)} collective-permute-done((bf16[192,768]{1,0:T(8,128)(2,1)S(1)}, bf16[192,768]{1,0:T(8,128)(2,1)S(1)}, u32[]{:S(2)}, u32[]{:S(2)}) %collective-permute-start.49) | collective-permute-done | bytes 294944 | tf_op jit(solution)/shard_map/ppermute | solution.py:610
  184.0 4.8 %collective-permute-done.54 = bf16[48,768]{1,0:T(8,128)(2,1)S(1)} collective-permute-done((bf16[48,768]{1,0:T(8,128)(2,1)S(1)}, bf16[48,768]{1,0:T(8,128)(2,1)S(1)}, u32[]{:S(2)}, u32[]{:S(2)}) %collective-permute-start.54) | collective-permute-done | bytes 73760 | tf_op jit(solution)/shard_map/ppermute | solution.py:613
  193.4 3.5 %collective-permute-done.55.refs_2_ = bf16[48,768]{1,0:T(8,128)(2,1)S(1)} collective-permute-done((bf16[48,768]{1,0:T(8,128)(2,1)S(1)}, bf16[48,768]{1,0:T(8,128)(2,1)S(1)}, u32[]{:S(2)}, u32[]{:S(2)}) %collective-permute-start.55) | collective-permute-done | bytes 73760 | tf_op jit(solution)/shard_map/ppermute | solution.py:613
  197.5 3.1 %collective-permute-done.42.refs_2_ = bf16[48,1536]{1,0:T(8,128)(2,1)S(1)} collective-permute-done((bf16[48,1536]{1,0:T(8,128)(2,1)S(1)}, bf16[48,1536]{1,0:T(8,128)(2,1)S(1)}, u32[]{:S(2)}, u32[]{:S(2)}) %collective-permute-start.42) | collective-permute-done | bytes 147488 | tf_op jit(solution)/shard_map/ppermute | solution.py:613
  210.5 3.6 %collective-permute-done.45.refs_2_ = bf16[192,768]{1,0:T(8,128)(2,1)S(1)} collective-permute-done((bf16[192,768]{1,0:T(8,128)(2,1)S(1)}, bf16[192,768]{1,0:T(8,128)(2,1)S(1)}, u32[]{:S(2)}, u32[]{:S(2)}) %collective-permute-start.45) | collective-permute-done | bytes 294944 | tf_op jit(solution)/shard_map/ppermute | solution.py:610
  214.7 7.1 %collective-permute-start.47 = (bf16[384,1536]{1,0:T(8,128)(2,1)S(1)}, bf16[384,1536]{1,0:T(8,128)(2,1)S(1)}, u32[]{:S(2)}, u32[]{:S(2)}) collective-permute-start(bf16[384,1536]{1,0:T(8,128)(2,1)S(1)} %shard_map.250.refs_0_), channel_id=1, source_target_pairs={{0,1},{1,0},{2,3},{3,2},{4,5},{5,4},{6,7},{7,6},{8,9},{9,8},{10,11... | collective-permute-start | bytes 3538952 | tf_op jit(solution)/shard_map/ppermute | solution.py:613
  225.0 2.8 %shard_map.259 = (f32[768,768]{1,0:T(8,128)}, f32[768,768]{1,0:T(8,128)}, f32[768,768]{1,0:T(8,128)}, f32[768,768]{1,0:T(8,128)}) custom-call(s32[5]{0:T(128)S(1)} %stack.20.refs_0_.place_ref, bf16[384,1536]{1,0:T(8,128)(2,1)S(1)} %shard_map.250.refs_0_, bf16[384,1536]{1,0:T(8,128)(2,1)S(1)} %shard_map.258.refs_1_), custom_call_target="tpu_custom_call" | custom-call | tf_op jit(solution)/shard_map/pallas_call | solution.py:832
  230.1 3.6 %shard_map.261 = (f32[768,768]{1,0:T(8,128)}, f32[768,768]{1,0:T(8,128)}, f32[768,768]{1,0:T(8,128)}, f32[768,768]{1,0:T(8,128)}) custom-call(s32[5]{0:T(128)S(1)} %stack.20.refs_0_.place_ref, bf16[384,1536]{1,0:T(8,128)(2,1)S(1)} %collective-permute-done.47.refs_0_, ...), custom_call_target="tpu_custom_call", output_to_operand_aliasing={{0}: (3, {}), {1}: (4, {}), {2}: (5, {}), {3}: (6, {})} | custom-call | tf_op jit(solution)/shard_map/pallas_call | solution.py:832
  (209 shorter events, 87.1 us)
Async XLA Ops:
  7.2 220.7 %all-gather.3.cloned.1.call-start = ((), (), s32[]{:S(2)}) async-start(), calls=%async_computation | async-start | bytes 1622016 | tf_op jit(solution)/shard_map/all_gather | solution.py:850
  20.1 16.5 %collective-permute-start = (bf16[40,1536]{1,0:T(8,128)(2,1)}, bf16[40,1536]{1,0:T(8,128)(2,1)S(1)}, u32[]{:S(2)}, u32[]{:S(2)}) collective-permute-start(bf16[40,1536]{1,0:T(8,128)(2,1)} %get-tuple-element.138), channel_id=1, source_target_pairs={{0,1},{1,0},{2,3},{3,2},{4,5},{5,4},{6,7},{7,6},{8,9},{9,8},{10,11... | collective-permute-start | bytes 368648 | tf_op jit(solution)/shard_map/ppermute | solution.py:613
  20.2 12.9 %collective-permute-start.1 = (bf16[40,1536]{1,0:T(8,128)(2,1)}, bf16[40,1536]{1,0:T(8,128)(2,1)S(1)}, u32[]{:S(2)}, u32[]{:S(2)}) collective-permute-start(bf16[40,1536]{1,0:T(8,128)(2,1)} %get-tuple-element.139), channel_id=1, source_target_pairs={{0,4},{1,5},{2,6},{3,7},{4,0},{5,1},{6,2},{7,3},{8,12},{9,13},{10,... | collective-permute-start | bytes 368648 | tf_op jit(solution)/shard_map/ppermute | solution.py:613
  24.0 13.6 %collective-permute-start.2 = (bf16[40,1536]{1,0:T(8,128)(2,1)}, bf16[40,1536]{1,0:T(8,128)(2,1)S(1)}, u32[]{:S(2)}, u32[]{:S(2)}) collective-permute-start(bf16[40,1536]{1,0:T(8,128)(2,1)} %get-tuple-element.140), channel_id=1, source_target_pairs={{0,5},{1,4},{2,7},{3,6},{4,1},{5,0},{6,3},{7,2},{8,13},{9,12},{10,... | collective-permute-start | bytes 368648 | tf_op jit(solution)/shard_map/ppermute | solution.py:613
  24.0 15.2 %collective-permute-start.4 = (bf16[40,1536]{1,0:T(8,128)(2,1)}, bf16[40,1536]{1,0:T(8,128)(2,1)S(1)}, u32[]{:S(2)}, u32[]{:S(2)}) collective-permute-start(bf16[40,1536]{1,0:T(8,128)(2,1)} %get-tuple-element.141), channel_id=1, source_target_pairs={{0,2},{1,3},{2,0},{3,1},{4,6},{5,7},{6,4},{7,5},{8,10},{9,11},{10,... | collective-permute-start | bytes 368648 | tf_op jit(solution)/shard_map/ppermute | solution.py:613
  25.6 14.9 %collective-permute-start.5 = (bf16[40,1536]{1,0:T(8,128)(2,1)}, bf16[40,1536]{1,0:T(8,128)(2,1)S(1)}, u32[]{:S(2)}, u32[]{:S(2)}) collective-permute-start(bf16[40,1536]{1,0:T(8,128)(2,1)} %get-tuple-element.142), channel_id=1, source_target_pairs={{0,3},{1,2},{2,1},{3,0},{4,7},{5,6},{6,5},{7,4},{8,11},{9,10},{10,... | collective-permute-start | bytes 368648 | tf_op jit(solution)/shard_map/ppermute | solution.py:613
  39.2 13.0 %collective-permute-start.3 = (bf16[80,1536]{1,0:T(8,128)(2,1)S(1)}, bf16[80,1536]{1,0:T(8,128)(2,1)S(1)}, u32[]{:S(2)}, u32[]{:S(2)}) collective-permute-start(bf16[80,1536]{1,0:T(8,128)(2,1)S(1)} %constant_dynamic-update-slice_fusion.refs_1_.refs_0_), channel_id=1, source_target_pairs={{0,8},{8,0},{16,24},{24,16},{1,9},{9,1},{17,25},{25,17},{2,10},{10... | collective-permute-start | bytes 737288 | tf_op jit(solution)/shard_map/ppermute | solution.py:610
  40.5 14.5 %collective-permute-start.10 = (bf16[80,1536]{1,0:T(8,128)(2,1)S(1)}, bf16[80,1536]{1,0:T(8,128)(2,1)S(1)}, u32[]{:S(2)}, u32[]{:S(2)}) collective-permute-start(bf16[80,1536]{1,0:T(8,128)(2,1)S(1)} %constant_dynamic-update-slice_fusion.2.refs_2_.refs_1_), channel_id=1, source_target_pairs={{0,16},{8,24},{16,0},{24,8},{1,17},{9,25},{17,1},{25,9},{2,18},{10... | collective-permute-start | bytes 737288 | tf_op jit(solution)/shard_map/ppermute | solution.py:610
  55.2 18.4 %collective-permute-start.18 = (bf16[80,1536]{1,0:T(8,128)(2,1)S(1)}, bf16[80,1536]{1,0:T(8,128)(2,1)}, u32[]{:S(2)}, u32[]{:S(2)}) collective-permute-start(bf16[80,1536]{1,0:T(8,128)(2,1)S(1)} %pad_maximum_fusion.refs_1_.refs_8_), channel_id=1, source_target_pairs={{0,16},{8,24},{16,0},{24,8},{1,17},{9,25},{17,1},{25,9},{2,18},{10... | collective-permute-start | bytes 737288 | tf_op jit(solution)/shard_map/ppermute | solution.py:610
  59.1 15.5 %collective-permute-start.17 = (bf16[80,1536]{1,0:T(8,128)(2,1)S(1)}, bf16[80,1536]{1,0:T(8,128)(2,1)}, u32[]{:S(2)}, u32[]{:S(2)}) collective-permute-start(bf16[80,1536]{1,0:T(8,128)(2,1)S(1)} %pad_maximum_fusion.1.refs_2_.refs_9_), channel_id=1, source_target_pairs={{0,8},{8,0},{16,24},{24,16},{1,9},{9,1},{17,25},{25,17},{2,10},{10... | collective-permute-start | bytes 737288 | tf_op jit(solution)/shard_map/ppermute | solution.py:610
  60.3 14.7 %collective-permute-start.20 = (bf16[80,1536]{1,0:T(8,128)(2,1)S(1)}, bf16[80,1536]{1,0:T(8,128)(2,1)}, u32[]{:S(2)}, u32[]{:S(2)}) collective-permute-start(bf16[80,1536]{1,0:T(8,128)(2,1)S(1)} %collective-permute-done.16.refs_3_.refs_10_), channel_id=1, source_target_pairs={{0,16},{8,24},{16,0},{24,8},{1,17},{9,25},{17,1},{25,9},{2,18},{10... | collective-permute-start | bytes 737288 | tf_op jit(solution)/shard_map/ppermute | solution.py:610
  82.1 24.4 %collective-permute-start.22 = (bf16[2,80,1536]{2,1,0:T(8,128)(2,1)}, bf16[2,80,1536]{2,1,0:T(8,128)(2,1)S(1)}, u32[]{:S(2)}, u32[]{:S(2)}) collective-permute-start(bf16[2,80,1536]{2,1,0:T(8,128)(2,1)} %get-tuple-element.153), channel_id=1, source_target_pairs={{0,8},{8,0},{16,24},{24,16},{1,9},{9,1},{17,25},{25,17},{2,10},{10... | collective-permute-start | bytes 1474568 | tf_op jit(solution)/shard_map/ppermute | solution.py:610
  83.4 24.1 %collective-permute-start.30 = (bf16[2,80,1536]{2,1,0:T(8,128)(2,1)}, bf16[2,80,1536]{2,1,0:T(8,128)(2,1)S(1)}, u32[]{:S(2)}, u32[]{:S(2)}) collective-permute-start(bf16[2,80,1536]{2,1,0:T(8,128)(2,1)} %get-tuple-element.159), channel_id=1, source_target_pairs={{0,16},{8,24},{16,0},{24,8},{1,17},{9,25},{17,1},{25,9},{2,18},{10... | collective-permute-start | bytes 1474568 | tf_op jit(solution)/shard_map/ppermute | solution.py:610
  84.7 15.3 %collective-permute-start.14 = (bf16[80,1536]{1,0:T(8,128)(2,1)S(1)}, bf16[80,1536]{1,0:T(8,128)(2,1)S(1)}, u32[]{:S(2)}, u32[]{:S(2)}) collective-permute-start(bf16[80,1536]{1,0:T(8,128)(2,1)S(1)} %fusion.9), channel_id=1, source_target_pairs={{0,16},{8,24},{16,0},{24,8},{1,17},{9,25},{17,1},{25,9},{2,18},{10... | collective-permute-start | bytes 737288 | tf_op jit(solution)/shard_map/ppermute | solution.py:610
  85.6 18.4 %collective-permute-start.27 = (bf16[80,1536]{1,0:T(8,128)(2,1)S(1)}, bf16[80,1536]{1,0:T(8,128)(2,1)S(1)}, u32[]{:S(2)}, u32[]{:S(2)}) collective-permute-start(bf16[80,1536]{1,0:T(8,128)(2,1)S(1)} %fusion.3), channel_id=1, source_target_pairs={{0,8},{8,0},{16,24},{24,16},{1,9},{9,1},{17,25},{25,17},{2,10},{10... | collective-permute-start | bytes 737288 | tf_op jit(solution)/shard_map/ppermute | solution.py:610
  100.8 15.9 %collective-permute-start.15 = (bf16[40,1536]{1,0:T(8,128)(2,1)S(1)}, bf16[40,1536]{1,0:T(8,128)(2,1)S(1)}, u32[]{:S(2)}, u32[]{:S(2)}) collective-permute-start(bf16[40,1536]{1,0:T(8,128)(2,1)S(1)} %get-tuple-element.248), channel_id=1, source_target_pairs={{0,1},{1,0},{2,3},{3,2},{4,5},{5,4},{6,7},{7,6},{8,9},{9,8},{10,11... | collective-permute-start | bytes 368648 | tf_op jit(solution)/shard_map/ppermute | solution.py:613
  104.2 14.7 %collective-permute-start.29 = (bf16[40,1536]{1,0:T(8,128)(2,1)S(1)}, bf16[40,1536]{1,0:T(8,128)(2,1)S(1)}, u32[]{:S(2)}, u32[]{:S(2)}) collective-permute-start(bf16[40,1536]{1,0:T(8,128)(2,1)S(1)} %get-tuple-element.244), channel_id=1, source_target_pairs={{0,5},{1,4},{2,7},{3,6},{4,1},{5,0},{6,3},{7,2},{8,13},{9,12},{10,... | collective-permute-start | bytes 368648 | tf_op jit(solution)/shard_map/ppermute | solution.py:613
  105.4 23.4 %collective-permute-start.28 = (bf16[40,1536]{1,0:T(8,128)(2,1)S(1)}, bf16[40,1536]{1,0:T(8,128)(2,1)S(1)}, u32[]{:S(2)}, u32[]{:S(2)}) collective-permute-start(bf16[40,1536]{1,0:T(8,128)(2,1)S(1)} %get-tuple-element.245), channel_id=1, source_target_pairs={{0,4},{1,5},{2,6},{3,7},{4,0},{5,1},{6,2},{7,3},{8,12},{9,13},{10,... | collective-permute-start | bytes 368648 | tf_op jit(solution)/shard_map/ppermute | solution.py:613
  113.5 15.4 %collective-permute-start.25 = (bf16[40,1536]{1,0:T(8,128)(2,1)S(1)}, bf16[40,1536]{1,0:T(8,128)(2,1)S(1)}, u32[]{:S(2)}, u32[]{:S(2)}) collective-permute-start(bf16[40,1536]{1,0:T(8,128)(2,1)S(1)} %get-tuple-element.246), channel_id=1, source_target_pairs={{0,3},{1,2},{2,1},{3,0},{4,7},{5,6},{6,5},{7,4},{8,11},{9,10},{10,... | collective-permute-start | bytes 368648 | tf_op jit(solution)/shard_map/ppermute | solution.py:613
  116.0 12.9 %collective-permute-start.24 = (bf16[40,1536]{1,0:T(8,128)(2,1)S(1)}, bf16[40,1536]{1,0:T(8,128)(2,1)S(1)}, u32[]{:S(2)}, u32[]{:S(2)}) collective-permute-start(bf16[40,1536]{1,0:T(8,128)(2,1)S(1)} %get-tuple-element.247), channel_id=1, source_target_pairs={{0,2},{1,3},{2,0},{3,1},{4,6},{5,7},{6,4},{7,5},{8,10},{9,11},{10,... | collective-permute-start | bytes 368648 | tf_op jit(solution)/shard_map/ppermute | solution.py:613
  153.7 12.4 %collective-permute-start.49 = (bf16[192,768]{1,0:T(8,128)(2,1)S(1)}, bf16[192,768]{1,0:T(8,128)(2,1)S(1)}, u32[]{:S(2)}, u32[]{:S(2)}) collective-permute-start(bf16[192,768]{1,0:T(8,128)(2,1)S(1)} %get-tuple-element.202), channel_id=1, source_target_pairs={{0,8},{8,0},{16,24},{24,16},{1,9},{9,1},{17,25},{25,17},{2,10},{10... | collective-permute-start | bytes 884744 | tf_op jit(solution)/shard_map/ppermute | solution.py:610
  154.0 12.6 %collective-permute-start.50 = (bf16[192,768]{1,0:T(8,128)(2,1)S(1)}, bf16[192,768]{1,0:T(8,128)(2,1)S(1)}, u32[]{:S(2)}, u32[]{:S(2)}) collective-permute-start(bf16[192,768]{1,0:T(8,128)(2,1)S(1)} %get-tuple-element.204), channel_id=1, source_target_pairs={{0,16},{8,24},{16,0},{24,8},{1,17},{9,25},{17,1},{25,9},{2,18},{10... | collective-permute-start | bytes 884744 | tf_op jit(solution)/shard_map/ppermute | solution.py:610
  207.8 14.0 %collective-permute-start.59 = (bf16[192,768]{1,0:T(8,128)(2,1)S(1)}, bf16[192,768]{1,0:T(8,128)(2,1)S(1)}, u32[]{:S(2)}, u32[]{:S(2)}) collective-permute-start(bf16[192,768]{1,0:T(8,128)(2,1)S(1)} %get-tuple-element.215.refs_1_), channel_id=1, source_target_pairs={{0,8},{8,0},{16,24},{24,16},{1,9},{9,1},{17,25},{25,17},{2,10},{10... | collective-permute-start | bytes 884744 | tf_op jit(solution)/shard_map/ppermute | solution.py:610
  214.7 15.3 %collective-permute-start.47 = (bf16[384,1536]{1,0:T(8,128)(2,1)S(1)}, bf16[384,1536]{1,0:T(8,128)(2,1)S(1)}, u32[]{:S(2)}, u32[]{:S(2)}) collective-permute-start(bf16[384,1536]{1,0:T(8,128)(2,1)S(1)} %shard_map.250.refs_0_), channel_id=1, source_target_pairs={{0,1},{1,0},{2,3},{3,2},{4,5},{5,4},{6,7},{7,6},{8,9},{9,8},{10,11... | collective-permute-start | bytes 3538952 | tf_op jit(solution)/shard_map/ppermute | solution.py:613
  (68 other events, 629.7 us)
Sparse Core Ops, SparseCore 0:
  146.4 55.8 all-gather.2

commit v3 on v2

--- a/solution.py
+++ b/solution.py
@@ -44,16 +44,18 @@
     return ref[...].reshape(-1, 1)
 
 
-def bucket_mask(count, spread):
-    shape = (count, spread.shape[1])
-    return (lax.broadcasted_iota(jnp.int32, shape, 0) == spread[...]).astype(F32)
+def bucket_mask(count, buckets):
+    span = buckets.shape[0] + 1
+    row = jnp.concatenate([buckets[...].reshape(1, -1), jnp.zeros((1, 1), jnp.int32)], axis=1)
+    rows = pltpu.roll(jnp.broadcast_to(row, (8, span)), span // 2 + 1, 1)
+    index = lax.broadcasted_iota(jnp.int32, (count, span), 0)
+    return (index == rows[:1]).astype(F32)
 
 
 class Fetched:
-    def __init__(self, source, buffer, semaphore):
+    def __init__(self, source, buffer, semaphore, later):
         self.buffer, self.copy = buffer, pltpu.make_async_copy(source, buffer, semaphore)
-        self.copy.start()
-        self.waiting = True
+        self.later, self.waiting = later, True
 
     @property
     def shape(self):
@@ -63,6 +65,8 @@
         if self.waiting:
             self.copy.wait()
             self.waiting = False
+            while self.later:
+                self.later.pop(0).copy.start()
 
     def __getitem__(self, index):
         self.wait()
@@ -100,7 +104,7 @@
     )
 
 
-def call(kernel, outs, *args, flops=0, transcendentals=0, scratch=(), smem=0, stream=True):
+def call(kernel, outs, *args, flops=0, transcendentals=0, scratch=(), smem=0, stream=True, early=99):
     out_bytes = sum(o.size * o.dtype.itemsize for o in outs)
     in_bytes = sum(a.size * a.dtype.itemsize for a in args)
     large_in = [stream and i >= smem and large(x) for i, x in enumerate(args)]
@@ -113,10 +117,15 @@
         buffers = iter(rest[: len(moved)])
         semaphores = rest[len(moved)] if moved else None
         count = iter(range(len(moved)))
+        later = []
         operands = [
-            Fetched(ref, next(buffers), semaphores.at[next(count)]) if flag else ref
+            Fetched(ref, next(buffers), semaphores.at[next(count)], later) if flag else ref
             for ref, flag in zip(operands, large_in)
         ]
+        fetched = [x for x in operands if isinstance(x, Fetched)]
+        later += fetched[early:]
+        for x in fetched[:early]:
+            x.copy.start()
         results = [
             Stored(ref, next(buffers), semaphores.at[next(count)]) if flag else ref
             for ref, flag in zip(results, large_out)
@@ -163,16 +172,16 @@
     cap,
     shift_ref,
     tokens,
-    cotangent,
     w_query,
     w_key,
     w_value,
     w_output,
+    cotangent,
     gain_attn,
     gain_ffn,
     w_router,
     table,
-    spread,
+    buckets,
     choices,
     levels,
     normed_one_out,
@@ -183,8 +192,7 @@
     mixed_out,
     residual_out,
     normed_two_out,
-    router_out,
-    target_out,
+    packed_out,
     *slots_out,
 ):
     length, width = tokens.shape
@@ -203,7 +211,7 @@
         out.send()
     by_offset = lax.dot_general(
         table[...],
-        bucket_mask(table.shape[1], spread),
+        bucket_mask(table.shape[1], buckets),
         (((1,), (0,)), ((), ())),
         precision=lax.Precision.HIGHEST,
         preferred_element_type=F32,
@@ -238,7 +246,6 @@
     logits = mm_nt(w_router[...], normed_two) + 0.25 * as_column(levels).astype(F32)
     logit_exp = jnp.exp(logits - jnp.max(logits, axis=0, keepdims=True))
     router = logit_exp / jnp.sum(logit_exp, axis=0, keepdims=True)
-    router_out[...] = router.T
     chosen = choices[...]
     mask = (chosen == lax.broadcasted_iota(jnp.int32, (experts, length), 0)).astype(F32)
     earlier = (
@@ -252,11 +259,12 @@
     row = lax.broadcasted_iota(jnp.int32, (8, length), 0)
     packed = jnp.where(
         row == 0, gate, jnp.where(row == 1, target.astype(F32), chosen.astype(F32))
-    ).T
-    target_out[...] = packed
+    )
+    packed_out[:8, :] = packed
+    packed_out[8:, :] = router
     place = (target == lax.broadcasted_iota(jnp.int32, (flat_slots, length), 0)).astype(F32)
     place = place.astype(BF)
-    sent = (packed[:, :1] * cotangent[...].astype(F32)).astype(BF)
+    sent = (packed.T[:, :1] * cotangent[...].astype(F32)).astype(BF)
     normed_slots, grad_slots = mm(place, normed_two), mm(place, sent)
     for i, out in enumerate(slots_out):
         rows = slice(i * slot_rows, (i + 1) * slot_rows)
@@ -315,15 +323,17 @@
 def store_halves(core, h, left, right, keep, send):
     columns = left.shape[1]
 
+    rows = slice(0, left.shape[0])
+
     @pl.when(core == h)
     def _():
-        keep[:, :columns] = left
-        keep[:, columns:] = right
+        keep[rows, :columns] = left
+        keep[rows, columns:] = right
 
     @pl.when(core != h)
     def _():
-        send[:, :columns] = left
-        send[:, columns:] = right
+        send[rows, :columns] = left
+        send[rows, columns:] = right
 
 
 def diagonal_sums(scores):
@@ -344,11 +354,10 @@
     heads,
     buckets_n,
     core_ref,
-    packed,
-    router,
+    packed_ref,
     gain_ffn,
     w_router,
-    spread,
+    buckets,
     cotangent,
     residual_ref,
     w_output,
@@ -368,12 +377,14 @@
 ):
     returned, outs = refs[:-12], refs[-12:]
     layer_output, input_grad, keep_1, send_1, keep_2, send_2, small_out = outs[:7]
+    ride = keep_1.shape[0] > keep_2.shape[0]
     small, grad_mixed_out, grad_value, grad_query, grad_key = outs[7:]
     core = core_ref[0]
     length, width = residual_ref.shape
     scale = (width // heads) ** (-0.5)
-    experts = router.shape[1]
+    experts = packed_ref.shape[0] - 8
     slot_rows = returned[0].shape[0]
+    packed = packed_ref[...].T
     gate, goal, chosen = packed[:, 0:1], packed[:, 1:2], packed[:, 2:3]
     if len(returned) > 1:
         back = jnp.concatenate([r[...].astype(F32) for r in returned], axis=0).astype(BF)
@@ -389,7 +400,7 @@
     mask = (
         chosen.astype(jnp.int32) == lax.broadcasted_iota(jnp.int32, (length, experts), 1)
     ).astype(F32)
-    probs = router[...]
+    probs = packed[:, 8:]
     upstream = cotangent[...].astype(F32)
     residual = residual_ref[...]
     grad_gate = jnp.sum(upstream * picked, axis=1, keepdims=True) * kept
@@ -444,8 +455,6 @@
         left = mm_tn(mixed[:, at], grad_attn).astype(BF)
         right = mm_tn(normed_one[:, at], grad_value[...]).astype(BF)
         store_halves(core, h, left, right, keep_1, send_1)
-    send_1.send()
-    keep_1.send()
     for h in (0, 1):
         at = slice(h * half, (h + 1) * half)
         left = mm_tn(normed_one[:, at], grad_query[...]).astype(BF)
@@ -473,16 +482,26 @@
     by_offset = jnp.sum(total.reshape(heads, 8, 2 * length), axis=1)
     small[2 + experts : 2 + experts + heads, :buckets_n] = lax.dot_general(
         by_offset,
-        bucket_mask(buckets_n, spread),
+        bucket_mask(buckets_n, buckets),
         (((1,), (1,)), ((), ())),
         precision=lax.Precision.HIGHEST,
         preferred_element_type=F32,
     )
-    small_out[...] = small[...].astype(small_out.dtype)
-
-
-def small_kernel(every, gain_attn, gain_ffn, router, table, small):
-    small[...] = jnp.sum(every[...].astype(F32), axis=0)
+    if ride:
+        top, count = keep_2.shape[0], small.shape[0] // 2
+        for out in (keep_1, send_1):
+            out[top:, :width] = small[:count].astype(BF)
+            out[top:, width:] = small[count:].astype(BF)
+    else:
+        small_out[...] = small[...]
+
+
+def both(left, right, rows, columns):
+    return left[rows, columns].astype(F32) + right[rows, columns].astype(F32)
+
+
+def small_kernel(rows, own, got, gain_attn, gain_ffn, router, table, small):
+    small[...] = both(own, got, slice(rows, None), slice(None))
     experts = router.shape[0]
     heads, buckets_n = table.shape
     gain_attn[...] = small[0:1, :].reshape(gain_attn.shape)
@@ -491,36 +510,66 @@
     table[...] = small[2 + experts : 2 + experts + heads, :buckets_n]
 
 
-def both(left, right, rows, columns):
-    return left[rows, columns].astype(F32) + right[rows, columns].astype(F32)
-
-
-def fold_kernel(bits, place_ref, *refs):
-    count = len(refs) // 4 if len(refs) > 6 else 1
-    for i, bit in enumerate(bits):
-        own, got = refs[2 * i : 2 * i + 2] if count == 2 else refs[:2]
-        keep, send = refs[-4 + 2 * i : len(refs) - 2 + 2 * i]
-        half, columns = keep.shape
-        left = 0 if count == 2 else i * columns
+def side_by_side(rows):
+    half = rows.shape[0] // 2
+    return jnp.concatenate([rows[:half], rows[half:]], axis=1)
+
+
+def one_over_other(rows):
+    half = rows.shape[1] // 2
+    return jnp.concatenate([rows[:, :half], rows[:, half:]], axis=0)
+
+
+def first_kernel(place_ref, own, got, keep_a, send_a, keep_b, send_b):
+    half, columns = keep_b.shape
+    for i, (bit, keep, send) in enumerate(((1, keep_a, send_a), (2, keep_b, send_b))):
+        at = slice(i * columns, (i + 1) * columns)
         for out, side in ((keep, place_ref[bit]), (send, 1 - place_ref[bit])):
             rows = pl.ds(pl.multiple_of(side * half, half), half)
-            out[...] = both(own, got, rows, slice(left, left + columns)).astype(BF)
-
-
-def join_kernel(bit, place_ref, own_a, got_a, own_b, got_b, keep, send):
-    half = keep.shape[0]
-    columns = own_a.shape[1]
-    for out, side in ((keep, place_ref[bit]), (send, 1 - place_ref[bit])):
-        rows = pl.ds(pl.multiple_of(side * half, half), half)
-        out[:, :columns] = both(own_a, got_a, rows, slice(None)).astype(BF)
-        out[:, columns:] = both(own_b, got_b, rows, slice(None)).astype(BF)
-
-
-def columns_kernel(bit, place_ref, own, got, keep, send):
+            out[:half, :] = both(own, got, rows, at).astype(BF)
+    if own.shape[0] > 2 * half:
+        tail = both(own, got, slice(2 * half, None), slice(None))
+        for out in (keep_a, send_a):
+            out[half:, :] = one_over_other(tail).astype(BF)
+
+
+def second_kernel(place_ref, own_a, got_a, own_b, got_b, keep_a, send_a, keep_b, send_b):
+    half = keep_b.shape[0]
+    for bit, own, got, keep, send in (
+        (2, own_a, got_a, keep_a, send_a),
+        (1, own_b, got_b, keep_b, send_b),
+    ):
+        for out, side in ((keep, place_ref[bit]), (send, 1 - place_ref[bit])):
+            rows = pl.ds(pl.multiple_of(side * half, half), half)
+            out[:half, :] = both(own, got, rows, slice(None)).astype(BF)
+    if own_a.shape[0] > 2 * half:
+        tail = both(own_a, got_a, slice(2 * half, None), slice(None))
+        for out in (keep_a, send_a):
+            out[half:, :] = tail.astype(BF)
+
+
+def join_kernel(place_ref, own_a, got_a, own_b, got_b, keep, send):
+    rows, columns = own_b.shape
+    half = rows // 2
+    for out, side in ((keep, place_ref[3]), (send, 1 - place_ref[3])):
+        at = pl.ds(pl.multiple_of(side * half, half), half)
+        out[:half, :columns] = both(own_a, got_a, at, slice(None)).astype(BF)
+        out[:half, columns:] = both(own_b, got_b, at, slice(None)).astype(BF)
+    if own_a.shape[0] > rows:
+        tail = both(own_a, got_a, slice(rows, None), slice(None))
+        for out in (keep, send):
+            out[half:, :] = side_by_side(tail).astype(BF)
+
+
+def columns_kernel(rows, place_ref, own, got, keep, send):
     columns = keep.shape[1]
-    for out, side in ((keep, place_ref[bit]), (send, 1 - place_ref[bit])):
+    for out, side in ((keep, place_ref[4]), (send, 1 - place_ref[4])):
         at = pl.ds(pl.multiple_of(side * columns, columns), columns)
-        out[...] = both(own, got, slice(None), at).astype(BF)
+        out[:rows, :] = both(own, got, slice(0, rows), at).astype(BF)
+    if own.shape[0] > rows:
+        tail = both(own, got, slice(rows, None), slice(None))
+        for out in (keep, send):
+            out[rows:, :] = one_over_other(tail).astype(BF)
 
 
 def beside_kernel(bit, place_ref, own, far, out):
@@ -602,7 +651,6 @@
     core_ref = (wide_at % 2).reshape(1)
     shift_ref = (wide_at if direct else jnp.zeros((), jnp.int32)).reshape(1)
     w_router = w_router.T
-    spread = jnp.roll(jnp.pad(buckets, (0, 1)), length + 1).reshape(1, 2 * length)
     rows_bf = shaped((length, width))
     attn_flops = 4 * length * length * width
 
@@ -621,7 +669,6 @@
         mixed,
         residual,
         normed_two,
-        router,
         packed,
         *slots,
     ) = call(
@@ -635,35 +682,36 @@
             rows_bf,
             shaped((length, width), F32),
             rows_bf,
-            shaped((length, experts), F32),
-            shaped((length, 8), F32),
+            shaped((8 + experts, length), F32),
         ]
         + [shaped((cap if direct else flat_slots, 2 * width))] * (n_wide if direct else 1),
         shift_ref,
         tokens,
-        cotangent,
         w_query,
         w_key,
         w_value,
         w_output,
+        cotangent,
         gain_attn,
         gain_ffn,
         w_router,
         bias_table.T,
-        spread,
+        buckets,
         choices.reshape(1, length),
         router_levels,
         smem=1,
+        early=2,
         flops=8 * length * width * width + attn_flops,
         transcendentals=heads * length * length,
     )
 
     quarter = flat_slots // 4
-    order = (0, 2, 1, 3)
+    order = (0, 3, 1, 2)
     if direct:
         per = n_wide // 4
-        moved = [slots[0]] + [along(slots[k], k) for k in range(1, n_wide)]
-        parts = [moved[i * per : (i + 1) * per] for i in order]
+        near = jnp.split(along(jnp.concatenate(slots[1::2], axis=0), 1), n_wide // 2)
+        parts = [jnp.concatenate([slots[2 * i], near[i]], axis=0) for i in order]
+        parts = [[along(p, 2 * i) if i else p] for i, p in zip(order, parts)]
     else:
         moved = lax.all_to_all(slots[0], "wide", split_axis=0, concat_axis=0, tiled=True)
         parts = [[moved[i * quarter : (i + 1) * quarter]] for i in range(4)]
@@ -700,6 +748,7 @@
             *rows[:4],
             w_out,
             *rows[4:],
+            early=5,
             flops=4 * expert_flops,
             transcendentals=8 * quarter * units,
         )
@@ -711,13 +760,19 @@
     quarters[2], quarters[3], first[3], first[4] = lax.optimization_barrier(
         (quarters[2], quarters[3], first[3], first[4])
     )
-    second = gather(*quarters[2:])
-    done_1, done_2 = experts_of(first), experts_of(second)
+    done_1 = experts_of(first)
+    a, b = quarters[2:]
+    a1, b2 = across(a, 1), across(b, 2)
+    a2, b1 = across(a, 2), across(b, 1)
+    a1, b2, done_1 = lax.optimization_barrier((a1, b2, done_1))
+    a3, b3 = across(a1, 2), across(b2, 1)
+    second = [a, b, a1, b1, a2, b2, a3, b3]
+    done_2 = experts_of(second)
     groups = [first, second]
     kept = done_1[:4] + done_2[:4]
     sums = [*reduced(*done_1[4:]), *reduced(*done_2[4:])]
     if direct:
-        sums = [sums[i] for i in order]
+        sums = [sums[order.index(i)] for i in range(4)]
         returned = [sums[k // per][k % per * cap : (k % per + 1) * cap] for k in range(n_wide)]
         returned = [returned[0]] + [along(returned[k], k) for k in range(1, n_wide)]
     else:
@@ -736,18 +791,19 @@
     )
 
     half = width // 2
-    small_rows = -(-(2 + experts + heads) // 16) * 16
+    small_rows = -(-(2 + experts + heads) // 32) * 32
+    ride = small_rows if direct else 0
     layer_output, input_grad, keep_1, send_1, keep_2, send_2, small = call(
         functools.partial(backward_kernel, heads, buckets_n),
         [rows_bf, rows_bf]
-        + [shaped((half, 2 * width))] * 4
-        + [shaped((small_rows, width), BF if direct else F32)],
+        + [shaped((half + ride // 2, 2 * width))] * 2
+        + [shaped((half, 2 * width))] * 2
+        + [shaped((8, 128) if direct else (small_rows, width), F32)],
         core_ref,
         packed,
-        router,
         gain_ffn,
         w_router,
-        spread,
+        buckets,
         cotangent,
         residual,
         w_output,
@@ -765,6 +821,7 @@
         gain_attn,
         *returned,
         smem=1,
+        early=4,
         scratch=[pltpu.VMEM((small_rows, width), F32)] + [pltpu.VMEM((length, width), BF)] * 4,
         flops=16 * length * width * width + 3 * attn_flops,
     )
@@ -777,25 +834,44 @@
     def hop(kernel, shapes, *args):
         return call(kernel, [shaped(x) for x in shapes], place, *args, smem=1, stream=False)
 
-    def fold_first(keep, send):
-        kernel = functools.partial(fold_kernel, (1, 2))
-        return hop(kernel, [(half // 2, width)] * 4, keep, along(send, 1))
-
-    def scatter(own_a, got_a, own_b, got_b):
-        step = functools.partial
+    def scatter(keep, send, tail):
+        own_a, send_a, own_b, send_b = hop(
+            first_kernel,
+            [(half // 2 + tail, width)] * 2 + [(half // 2, width)] * 2,
+            keep,
+            along(send, 1),
+        )
+        own_a, send_a, own_b, send_b = hop(
+            second_kernel,
+            [(half // 4 + tail, width)] * 2 + [(half // 4, width)] * 2,
+            own_a,
+            across(send_a, 1),
+            own_b,
+            across(send_b, 2),
+        )
+        rows = half // 8
         own, other = hop(
-            step(join_kernel, 3), [(half // 8, 2 * width)] * 2, own_a, got_a, own_b, got_b
+            join_kernel,
+            [(rows + tail // 2, 2 * width)] * 2,
+            own_a,
+            across(send_a, 2),
+            own_b,
+            across(send_b, 1),
         )
         own, other = hop(
-            step(columns_kernel, 4), [(half // 8, width)] * 2, own, along(other, 2)
+            functools.partial(columns_kernel, rows),
+            [(rows + tail, width)] * 2,
+            own,
+            along(other, 2),
         )
-        x = (own.astype(F32) + along(other, 4).astype(F32)).astype(BF)
+        got = along(other, 4)
+        x = (own[:rows].astype(F32) + got[:rows].astype(F32)).astype(BF)
         for k in deeper:
             bit, size = wide_at // k % 2, x.shape[0] // 2
             other = lax.dynamic_slice_in_dim(x, (1 - bit) * size, size, 0)
-            own = lax.dynamic_slice_in_dim(x, bit * size, size, 0)
-            x = (own.astype(F32) + along(other, k).astype(F32)).astype(BF)
-        return x
+            mine = lax.dynamic_slice_in_dim(x, bit * size, size, 0)
+            x = (mine.astype(F32) + along(other, k).astype(F32)).astype(BF)
+        return x, own, got
 
     def spread_out(x):
         step = functools.partial
@@ -816,17 +892,6 @@
         (x,) = hop(half_kernel, [(half, 2 * width)], a, across(a, 1), b, across(b, 2))
         return x
 
-    def fold_second(own_a, send_a, own_b, send_b):
-        own_a, send_a, own_b, send_b = hop(
-            functools.partial(fold_kernel, (2, 1)),
-            [(half // 4, width)] * 4,
-            own_a,
-            across(send_a, 1),
-            own_b,
-            across(send_b, 2),
-        )
-        return own_a, across(send_a, 2), own_b, across(send_b, 1)
-
     def finish(sources, outs=()):
         count = 2 * len(sources)
         return pl.pallas_call(
@@ -844,28 +909,28 @@
             compiler_params=pltpu.CompilerParams(vmem_limit_bytes=LOW),
         )(place, *sources, *outs)
 
-    after = lax.optimization_barrier
-    first_1, first_2 = fold_first(keep_1, send_1), fold_first(keep_2, send_2)
-    if direct:
-        small = lax.all_gather(small, ("narrow", "wide"), axis=0, tiled=False)
-    else:
-        small = lax.psum(small, ("narrow", "wide"))[None]
+    part_1, own, got = scatter(keep_1, send_1, ride)
+    part_2, _, _ = scatter(keep_2, send_2, 0)
+    if not direct:
+        own = lax.psum(small, ("narrow", "wide"))
+        got = jnp.zeros_like(own)
     small = call(
-        small_kernel,
+        functools.partial(small_kernel, half // 8 if direct else 0),
         [
             shaped((width,), F32),
             shaped((width,), F32),
             shaped((experts, width), F32),
             shaped((heads, buckets_n), F32),
         ],
-        small,
+        own,
+        got,
         scratch=[pltpu.VMEM((small_rows, width), F32)],
-    )
-    part_1 = spread_out(scatter(*fold_second(*first_1)))
-    part_2 = spread_out(scatter(*fold_second(*first_2)))
+        stream=False,
+    )
+    part_1, part_2 = spread_out(part_1), spread_out(part_2)
     far_1, far_2 = along(part_1, 1), along(part_2, 1)
     near = finish((part_1, part_2))
-    far_1, far_2, near, small = after((far_1, far_2, near, small))
+    far_1, far_2, near, small = lax.optimization_barrier((far_1, far_2, near, small))
     grad_w_output, grad_w_value, grad_w_query, grad_w_key = finish((far_1, far_2), near)
     return (
         layer_output,

time: 241 us -> 223 us (0.925)
  between operations: 14.8 us -> 1.49 us
  waiting for transfers between devices: 81.4 us -> 74.1 us
  starting transfers between devices: 70.7 us -> 75 us
    ppermute x36, waiting for transfers between devices: 50.7 us -> 41 us  [across(): return lax.ppermute(x, 'narrow', pairs(n_narrow, k))]
    ppermute x26 -> x23, starting transfers between devices: 42.9 us -> 46.4 us  [along(): return lax.ppermute(x, 'wide', pairs(n_wide, k))]
    ppermute x26 -> x23, waiting for transfers between devices: 30.7 us -> 33.1 us  [along(): return lax.ppermute(x, 'wide', pairs(n_wide, k))]
  transfers between devices with their start and end apart: 63 -> 59, of which waited for: 29 -> 28; matrix products, arithmetic and copies ran while one was open for 1% -> 1% of each run, Pallas kernels for 15% -> 16%
where the time goes in v3:
time: 223 us; the launch traced here: 222 us
  starting transfers between devices  75 us (34%)
  waiting for transfers between devices  74.1 us (33%)
  Pallas kernels  65.4 us (29%)
  local copies, waits for them, and re-layouts  4.25 us (2%)
    pallas_call x22, Pallas kernels, call(): pl.pallas_call(body, out_shape=tuple(outs), in_specs=[pl.BlockSpec(memory...  59.8 us
    ppermute x23, starting transfers between devices, along(): return lax.ppermute(x, 'wide', pairs(n_wide, k))  46.4 us
    ppermute x36, waiting for transfers between devices, across(): return lax.ppermute(x, 'narrow', pairs(n_narrow, k))  41 us
    ppermute x23, waiting for transfers between devices, along(): return lax.ppermute(x, 'wide', pairs(n_wide, k))  33.1 us
    ppermute x36, starting transfers between devices, across(): return lax.ppermute(x, 'narrow', pairs(n_narrow, k))  28.6 us
    pallas_call x2, Pallas kernels, finish(): pl.pallas_call(functools.partial(finish_kernel, bool(outs), len(sources))...  5.66 us
  transfers between devices with their start and end apart: 59, of which 28 were waited for; matrix products, arithmetic and copies ran while one was open for 1% of the time, Pallas kernels for 16%

profile of v3, /device:TPU:1, one launch (start us, length us, event | category | flops | bytes accessed | tf_op | source)
XLA Modules:
  0.0 222.2 jit_solution(3992972963751264394)
XLA Ops:
  0.6 11.2 %shard_map.238 = (bf16[256,768]{1,0:T(8,128)(2,1)}, bf16[256,768]{1,0:T(8,128)(2,1)}, bf16[256,768]{1,0:T(8,128)(2,1)}, bf16[256,768]{1,0:T(8,128)(2,1)}, bf16[1...) custom-call(s32[1]{0:T(128)} %bitcast.1.refs_0_, ...), custom_call_target="tpu_custom_call" | custom-call | flops 1409286144 | bytes 11246112 | tf_op jit(solution)/shard_map/pallas_call | solution.py:150
  15.1 4.5 %collective-permute-start.3 = (bf16[80,1536]{1,0:T(8,128)(2,1)S(1)}, bf16[80,1536]{1,0:T(8,128)(2,1)S(1)}, u32[]{:S(2)}, u32[]{:S(2)}) collective-permute-start(bf16[80,1536]{1,0:T(8,128)(2,1)S(1)} %pad_maximum_fusion.3), channel_id=1, source_target_pairs={{0,6},{1,7},{2,4},{3,5},{4,2},{5,3},{6,0},{7,1},{8,14},{9,15},{10,... | collective-permute-start | bytes 737288 | tf_op jit(solution)/shard_map/ppermute | solution.py:661
  21.0 4.7 %collective-permute-done.3.refs_2_.refs_1_ = bf16[80,1536]{1,0:T(8,128)(2,1)S(1)} collective-permute-done((bf16[80,1536]{1,0:T(8,128)(2,1)S(1)}, bf16[80,1536]{1,0:T(8,128)(2,1)S(1)}, u32[]{:S(2)}, u32[]{:S(2)}) %collective-permute-start.3) | collective-permute-done | bytes 245792 | tf_op jit(solution)/shard_map/ppermute | solution.py:661
  27.2 5.4 %collective-permute-start.2 = (bf16[80,1536]{1,0:T(8,128)(2,1)S(1)}, bf16[80,1536]{1,0:T(8,128)(2,1)S(1)}, u32[]{:S(2)}, u32[]{:S(2)}) collective-permute-start(bf16[80,1536]{1,0:T(8,128)(2,1)S(1)} %pad_maximum_fusion.2), channel_id=1, source_target_pairs={{0,4},{1,5},{2,6},{3,7},{4,0},{5,1},{6,2},{7,3},{8,12},{9,13},{10,... | collective-permute-start | bytes 737288 | tf_op jit(solution)/shard_map/ppermute | solution.py:661
  35.3 7.8 %collective-permute-done.2.refs_2_.refs_9_ = bf16[80,1536]{1,0:T(8,128)(2,1)S(1)} collective-permute-done((bf16[80,1536]{1,0:T(8,128)(2,1)S(1)}, bf16[80,1536]{1,0:T(8,128)(2,1)S(1)}, u32[]{:S(2)}, u32[]{:S(2)}) %collective-permute-start.2) | collective-permute-done | bytes 245792 | tf_op jit(solution)/shard_map/ppermute | solution.py:661
  46.9 7.1 %shard_map.239 = (bf16[320,768]{1,0:T(8,128)(2,1)}, bf16[320,768]{1,0:T(8,128)(2,1)}, bf16[320,768]{1,0:T(8,128)(2,1)}, bf16[320,768]{1,0:T(8,128)(2,1)}, bf16[8...) custom-call(bf16[768,768]{1,0:T(8,128)(2,1)} %bitcast.57, ...), custom_call_target="tpu_custom_call" | custom-call | flops 3019898880 | bytes 8257536 | tf_op jit(solution)/shard_map/pallas_call | solution.py:150
  61.9 7.2 %shard_map.240 = (bf16[320,768]{1,0:T(8,128)(2,1)}, bf16[320,768]{1,0:T(8,128)(2,1)}, bf16[320,768]{1,0:T(8,128)(2,1)}, bf16[320,768]{1,0:T(8,128)(2,1)}, bf16[8...) custom-call(bf16[768,768]{1,0:T(8,128)(2,1)} %bitcast.58, ...), custom_call_target="tpu_custom_call" | custom-call | flops 3019898880 | bytes 8257536 | tf_op jit(solution)/shard_map/pallas_call | solution.py:150
  72.7 9.2 %collective-permute-done.13 = bf16[80,1536]{1,0:T(8,128)(2,1)S(1)} collective-permute-done((bf16[80,1536]{1,0:T(8,128)(2,1)S(1)}, bf16[80,1536]{1,0:T(8,128)(2,1)S(1)}, u32[]{:S(2)}, u32[]{:S(2)}) %collective-permute-start.13) | collective-permute-done | bytes 245792 | tf_op jit(solution)/shard_map/ppermute | solution.py:658
  82.7 7.6 %collective-permute-start.14 = (bf16[40,1536]{1,0:T(8,128)(2,1)S(1)}, bf16[40,1536]{1,0:T(8,128)(2,1)S(1)}, u32[]{:S(2)}, u32[]{:S(2)}) collective-permute-start(bf16[40,1536]{1,0:T(8,128)(2,1)S(1)} %get-tuple-element.272), channel_id=1, source_target_pairs={{0,1},{1,0},{2,3},{3,2},{4,5},{5,4},{6,7},{7,6},{8,9},{9,8},{10,11... | collective-permute-start | bytes 368648 | tf_op jit(solution)/shard_map/ppermute | solution.py:661
  96.2 4.9 %collective-permute-done.20 = bf16[80,1536]{1,0:T(8,128)(2,1)S(1)} collective-permute-done((bf16[80,1536]{1,0:T(8,128)(2,1)S(1)}, bf16[80,1536]{1,0:T(8,128)(2,1)S(1)}, u32[]{:S(2)}, u32[]{:S(2)}) %collective-permute-start.20) | collective-permute-done | bytes 245792 | tf_op jit(solution)/shard_map/ppermute | solution.py:658
  107.3 8.2 %shard_map.241 = (f32[1,768,768]{2,1,0:T(8,128)}, f32[1,768,768]{2,1,0:T(8,128)}) custom-call(bf16[80,1536]{1,0:T(8,128)(2,1)} %copy-done.2, bf16[80,1536]{1,0:T(8,128)(2,1)} %copy-done.22, bf16[80,1536]{1,0:T(8,128)(2,1)} %copy-done.24, bf16[80,1536]{1,0:T(8,128)(2,1)} %copy-done.28, bf16[80,1536]{1,0:T(8,128)(2,1)} %copy-done.26, ...), custom_call_target="tpu_custom_call" | custom-call | flops 3019898880 | bytes 12582912 | tf_op jit(solution)/shard_map/pallas_call | solution.py:150
  115.7 3.2 %collective-permute-done.25.refs_24_ = bf16[40,1536]{1,0:T(8,128)(2,1)S(1)} collective-permute-done((bf16[40,1536]{1,0:T(8,128)(2,1)S(1)}, bf16[40,1536]{1,0:T(8,128)(2,1)S(1)}, u32[]{:S(2)}, u32[]{:S(2)}) %collective-permute-start.25) | collective-permute-done | bytes 122912 | tf_op jit(solution)/shard_map/ppermute | solution.py:661
  119.5 16.3 %shard_map.242 = (bf16[256,768]{1,0:T(8,128)(2,1)}, bf16[256,768]{1,0:T(8,128)(2,1)}, bf16[400,1536]{1,0:T(8,128)(2,1)}, bf16[400,1536]{1,0:T(8,128)(2,1)}, bf16...) custom-call(s32[1]{0:T(128)} %bitcast.refs_0_, f32[16,256]{1,0:T(8,128)} %get-tuple-element.137.refs_1_, ...), custom_call_target="tpu_custom_call" | custom-call | flops 3019898880 | bytes 16850944 | tf_op jit(solution)/shard_map/pallas_call | solution.py:150
  136.5 2.6 %collective-permute-done.31.refs_2_ = bf16[400,1536]{1,0:T(8,128)(2,1)S(1)} collective-permute-done((bf16[400,1536]{1,0:T(8,128)(2,1)}, bf16[400,1536]{1,0:T(8,128)(2,1)S(1)}, u32[]{:S(2)}, u32[]{:S(2)}) %collective-permute-start.31) | collective-permute-done | bytes 1228832 | tf_op jit(solution)/shard_map/ppermute | solution.py:661
  145.1 5.3 %collective-permute-done.33.refs_4_ = bf16[192,768]{1,0:T(8,128)(2,1)S(1)} collective-permute-done((bf16[192,768]{1,0:T(8,128)(2,1)S(1)}, bf16[192,768]{1,0:T(8,128)(2,1)S(1)}, u32[]{:S(2)}, u32[]{:S(2)}) %collective-permute-start.33) | collective-permute-done | bytes 294944 | tf_op jit(solution)/shard_map/ppermute | solution.py:658
  152.2 4.7 %collective-permute-done.46.refs_2_ = bf16[192,768]{1,0:T(8,128)(2,1)S(1)} collective-permute-done((bf16[192,768]{1,0:T(8,128)(2,1)S(1)}, bf16[192,768]{1,0:T(8,128)(2,1)S(1)}, u32[]{:S(2)}, u32[]{:S(2)}) %collective-permute-start.46) | collective-permute-done | bytes 294944 | tf_op jit(solution)/shard_map/ppermute | solution.py:658
  159.9 4.0 %collective-permute-done.48.refs_2_ = bf16[96,768]{1,0:T(8,128)(2,1)S(1)} collective-permute-done((bf16[96,768]{1,0:T(8,128)(2,1)S(1)}, bf16[96,768]{1,0:T(8,128)(2,1)S(1)}, u32[]{:S(2)}, u32[]{:S(2)}) %collective-permute-start.48) | collective-permute-done | bytes 147488 | tf_op jit(solution)/shard_map/ppermute | solution.py:658
  177.3 3.0 %collective-permute-start.38 = (bf16[48,768]{1,0:T(8,128)(2,1)S(1)}, bf16[48,768]{1,0:T(8,128)(2,1)S(1)}, u32[]{:S(2)}, u32[]{:S(2)}) collective-permute-start(bf16[48,768]{1,0:T(8,128)(2,1)S(1)} %add_convert_fusion.1.refs_1_), channel_id=1, source_target_pairs={{0,4},{1,5},{2,6},{3,7},{4,0},{5,1},{6,2},{7,3},{8,12},{9,13},{10,... | collective-permute-start | bytes 221192 | tf_op jit(solution)/shard_map/ppermute | solution.py:661
  180.3 3.7 %collective-permute-done.52.refs_2_ = bf16[48,768]{1,0:T(8,128)(2,1)S(1)} collective-permute-done((bf16[48,768]{1,0:T(8,128)(2,1)S(1)}, bf16[48,768]{1,0:T(8,128)(2,1)S(1)}, u32[]{:S(2)}, u32[]{:S(2)}) %collective-permute-start.52) | collective-permute-done | bytes 73760 | tf_op jit(solution)/shard_map/ppermute | solution.py:661
  186.7 2.7 %collective-permute-done.53.refs_2_ = bf16[48,1536]{1,0:T(8,128)(2,1)S(1)} collective-permute-done((bf16[48,1536]{1,0:T(8,128)(2,1)S(1)}, bf16[48,1536]{1,0:T(8,128)(2,1)S(1)}, u32[]{:S(2)}, u32[]{:S(2)}) %collective-permute-start.53) | collective-permute-done | bytes 147488 | tf_op jit(solution)/shard_map/ppermute | solution.py:661
  201.0 3.7 %collective-permute-done.57.refs_4_ = bf16[192,768]{1,0:T(8,128)(2,1)S(1)} collective-permute-done((bf16[192,768]{1,0:T(8,128)(2,1)S(1)}, bf16[192,768]{1,0:T(8,128)(2,1)S(1)}, u32[]{:S(2)}, u32[]{:S(2)}) %collective-permute-start.57) | collective-permute-done | bytes 294944 | tf_op jit(solution)/shard_map/ppermute | solution.py:658
  205.4 7.1 %collective-permute-start.58 = (bf16[384,1536]{1,0:T(8,128)(2,1)S(1)}, bf16[384,1536]{1,0:T(8,128)(2,1)S(1)}, u32[]{:S(2)}, u32[]{:S(2)}) collective-permute-start(bf16[384,1536]{1,0:T(8,128)(2,1)S(1)} %shard_map.258.refs_1_), channel_id=1, source_target_pairs={{0,1},{1,0},{2,3},{3,2},{4,5},{5,4},{6,7},{7,6},{8,9},{9,8},{10,11... | collective-permute-start | bytes 3538952 | tf_op jit(solution)/shard_map/ppermute | solution.py:661
  216.3 2.8 %shard_map.259 = (f32[768,768]{1,0:T(8,128)}, f32[768,768]{1,0:T(8,128)}, f32[768,768]{1,0:T(8,128)}, f32[768,768]{1,0:T(8,128)}) custom-call(s32[5]{0:T(128)S(1)} %stack.20.refs_0_.place_ref, bf16[384,1536]{1,0:T(8,128)(2,1)S(1)} %shard_map.250.refs_0_, bf16[384,1536]{1,0:T(8,128)(2,1)S(1)} %shard_map.258.refs_1_), custom_call_target="tpu_custom_call" | custom-call | tf_op jit(solution)/shard_map/pallas_call | solution.py:897
  219.2 2.8 %shard_map.261 = (f32[768,768]{1,0:T(8,128)}, f32[768,768]{1,0:T(8,128)}, f32[768,768]{1,0:T(8,128)}, f32[768,768]{1,0:T(8,128)}) custom-call(s32[5]{0:T(128)S(1)} %stack.20.refs_0_.place_ref, bf16[384,1536]{1,0:T(8,128)(2,1)S(1)} %collective-permute-done.44.refs_0_, ...), custom_call_target="tpu_custom_call", output_to_operand_aliasing={{0}: (3, {}), {1}: (4, {}), {2}: (5, {}), {3}: (6, {})} | custom-call | tf_op jit(solution)/shard_map/pallas_call | solution.py:897
  (207 shorter events, 81.0 us)
Async XLA Ops:
  19.6 13.0 %collective-permute-start.1 = (bf16[80,1536]{1,0:T(8,128)(2,1)S(1)}, bf16[80,1536]{1,0:T(8,128)(2,1)S(1)}, u32[]{:S(2)}, u32[]{:S(2)}) collective-permute-start(bf16[80,1536]{1,0:T(8,128)(2,1)S(1)} %pad_maximum_fusion.1), channel_id=1, source_target_pairs={{0,2},{1,3},{2,0},{3,1},{4,6},{5,7},{6,4},{7,5},{8,10},{9,11},{10,... | collective-permute-start | bytes 737288 | tf_op jit(solution)/shard_map/ppermute | solution.py:661
  19.8 14.0 %collective-permute-start.8 = (bf16[80,1536]{1,0:T(8,128)(2,1)S(1)}, bf16[80,1536]{1,0:T(8,128)(2,1)S(1)}, u32[]{:S(2)}, u32[]{:S(2)}) collective-permute-start(bf16[80,1536]{1,0:T(8,128)(2,1)S(1)} %pad_maximum_fusion.4.refs_1_.refs_0_), channel_id=1, source_target_pairs={{0,8},{8,0},{16,24},{24,16},{1,9},{9,1},{17,25},{25,17},{2,10},{10... | collective-permute-start | bytes 737288 | tf_op jit(solution)/shard_map/ppermute | solution.py:658
  26.7 16.4 %collective-permute-start.5 = (bf16[80,1536]{1,0:T(8,128)(2,1)S(1)}, bf16[80,1536]{1,0:T(8,128)(2,1)S(1)}, u32[]{:S(2)}, u32[]{:S(2)}) collective-permute-start(bf16[80,1536]{1,0:T(8,128)(2,1)S(1)} %pad_maximum_fusion.4.refs_1_.refs_0_), channel_id=1, source_target_pairs={{0,16},{8,24},{16,0},{24,8},{1,17},{9,25},{17,1},{25,9},{2,18},{10... | collective-permute-start | bytes 737288 | tf_op jit(solution)/shard_map/ppermute | solution.py:658
  27.2 15.9 %collective-permute-start.2 = (bf16[80,1536]{1,0:T(8,128)(2,1)S(1)}, bf16[80,1536]{1,0:T(8,128)(2,1)S(1)}, u32[]{:S(2)}, u32[]{:S(2)}) collective-permute-start(bf16[80,1536]{1,0:T(8,128)(2,1)S(1)} %pad_maximum_fusion.2), channel_id=1, source_target_pairs={{0,4},{1,5},{2,6},{3,7},{4,0},{5,1},{6,2},{7,3},{8,12},{9,13},{10,... | collective-permute-start | bytes 737288 | tf_op jit(solution)/shard_map/ppermute | solution.py:661
  33.8 12.1 %collective-permute-start.10 = (bf16[80,1536]{1,0:T(8,128)(2,1)S(1)}, bf16[80,1536]{1,0:T(8,128)(2,1)S(1)}, u32[]{:S(2)}, u32[]{:S(2)}) collective-permute-start(bf16[80,1536]{1,0:T(8,128)(2,1)S(1)} %collective-permute-done.8.refs_3_.refs_2_), channel_id=1, source_target_pairs={{0,16},{8,24},{16,0},{24,8},{1,17},{9,25},{17,1},{25,9},{2,18},{10... | collective-permute-start | bytes 737288 | tf_op jit(solution)/shard_map/ppermute | solution.py:658
  43.2 14.0 %collective-permute-start.16 = (bf16[80,1536]{1,0:T(8,128)(2,1)S(1)}, bf16[80,1536]{1,0:T(8,128)(2,1)S(1)}, u32[]{:S(2)}, u32[]{:S(2)}) collective-permute-start(bf16[80,1536]{1,0:T(8,128)(2,1)S(1)} %collective-permute-done.1.refs_1_.refs_8_), channel_id=1, source_target_pairs={{0,16},{8,24},{16,0},{24,8},{1,17},{9,25},{17,1},{25,9},{2,18},{10... | collective-permute-start | bytes 737288 | tf_op jit(solution)/shard_map/ppermute | solution.py:658
  45.7 11.8 %collective-permute-start.15 = (bf16[80,1536]{1,0:T(8,128)(2,1)S(1)}, bf16[80,1536]{1,0:T(8,128)(2,1)}, u32[]{:S(2)}, u32[]{:S(2)}) collective-permute-start(bf16[80,1536]{1,0:T(8,128)(2,1)S(1)} %collective-permute-done.2.refs_2_.refs_9_), channel_id=1, source_target_pairs={{0,8},{8,0},{16,24},{24,16},{1,9},{9,1},{17,25},{25,17},{2,10},{10... | collective-permute-start | bytes 737288 | tf_op jit(solution)/shard_map/ppermute | solution.py:658
  56.9 14.2 %collective-permute-start.12 = (bf16[2,80,1536]{2,1,0:T(8,128)(2,1)}, bf16[2,80,1536]{2,1,0:T(8,128)(2,1)S(1)}, u32[]{:S(2)}, u32[]{:S(2)}) collective-permute-start(bf16[2,80,1536]{2,1,0:T(8,128)(2,1)} %get-tuple-element.169), channel_id=1, source_target_pairs={{0,8},{8,0},{16,24},{24,16},{1,9},{9,1},{17,25},{25,17},{2,10},{10... | collective-permute-start | bytes 1474568 | tf_op jit(solution)/shard_map/ppermute | solution.py:658
  57.1 14.9 %collective-permute-start.27 = (bf16[2,80,1536]{2,1,0:T(8,128)(2,1)}, bf16[2,80,1536]{2,1,0:T(8,128)(2,1)S(1)}, u32[]{:S(2)}, u32[]{:S(2)}) collective-permute-start(bf16[2,80,1536]{2,1,0:T(8,128)(2,1)} %get-tuple-element.180), channel_id=1, source_target_pairs={{0,16},{8,24},{16,0},{24,8},{1,17},{9,25},{17,1},{25,9},{2,18},{10... | collective-permute-start | bytes 1474568 | tf_op jit(solution)/shard_map/ppermute | solution.py:658
  69.1 24.8 %collective-permute-start.19 = (bf16[2,80,1536]{2,1,0:T(8,128)(2,1)}, bf16[2,80,1536]{2,1,0:T(8,128)(2,1)S(1)}, u32[]{:S(2)}, u32[]{:S(2)}) collective-permute-start(bf16[2,80,1536]{2,1,0:T(8,128)(2,1)} %get-tuple-element.174), channel_id=1, source_target_pairs={{0,8},{8,0},{16,24},{24,16},{1,9},{9,1},{17,25},{25,17},{2,10},{10... | collective-permute-start | bytes 1474568 | tf_op jit(solution)/shard_map/ppermute | solution.py:658
  70.4 24.5 %collective-permute-start.23 = (bf16[2,80,1536]{2,1,0:T(8,128)(2,1)}, bf16[2,80,1536]{2,1,0:T(8,128)(2,1)S(1)}, u32[]{:S(2)}, u32[]{:S(2)}) collective-permute-start(bf16[2,80,1536]{2,1,0:T(8,128)(2,1)} %get-tuple-element.177), channel_id=1, source_target_pairs={{0,16},{8,24},{16,0},{24,8},{1,17},{9,25},{17,1},{25,9},{2,18},{10... | collective-permute-start | bytes 1474568 | tf_op jit(solution)/shard_map/ppermute | solution.py:658
  72.1 18.2 %collective-permute-start.28 = (bf16[80,1536]{1,0:T(8,128)(2,1)S(1)}, bf16[80,1536]{1,0:T(8,128)(2,1)S(1)}, u32[]{:S(2)}, u32[]{:S(2)}) collective-permute-start(bf16[80,1536]{1,0:T(8,128)(2,1)S(1)} %fusion), channel_id=1, source_target_pairs={{0,8},{8,0},{16,24},{24,16},{1,9},{9,1},{17,25},{25,17},{2,10},{10... | collective-permute-start | bytes 737288 | tf_op jit(solution)/shard_map/ppermute | solution.py:658
  82.7 21.4 %collective-permute-start.14 = (bf16[40,1536]{1,0:T(8,128)(2,1)S(1)}, bf16[40,1536]{1,0:T(8,128)(2,1)S(1)}, u32[]{:S(2)}, u32[]{:S(2)}) collective-permute-start(bf16[40,1536]{1,0:T(8,128)(2,1)S(1)} %get-tuple-element.272), channel_id=1, source_target_pairs={{0,1},{1,0},{2,3},{3,2},{4,5},{5,4},{6,7},{7,6},{8,9},{9,8},{10,11... | collective-permute-start | bytes 368648 | tf_op jit(solution)/shard_map/ppermute | solution.py:661
  90.4 15.3 %collective-permute-start.30 = (bf16[40,1536]{1,0:T(8,128)(2,1)S(1)}, bf16[40,1536]{1,0:T(8,128)(2,1)S(1)}, u32[]{:S(2)}, u32[]{:S(2)}) collective-permute-start(bf16[40,1536]{1,0:T(8,128)(2,1)S(1)} %get-tuple-element.266), channel_id=1, source_target_pairs={{0,7},{1,6},{2,5},{3,4},{4,3},{5,2},{6,1},{7,0},{8,15},{9,14},{10,... | collective-permute-start | bytes 368648 | tf_op jit(solution)/shard_map/ppermute | solution.py:661
  92.0 23.6 %collective-permute-start.29 = (bf16[40,1536]{1,0:T(8,128)(2,1)S(1)}, bf16[40,1536]{1,0:T(8,128)(2,1)S(1)}, u32[]{:S(2)}, u32[]{:S(2)}) collective-permute-start(bf16[40,1536]{1,0:T(8,128)(2,1)S(1)} %get-tuple-element.267), channel_id=1, source_target_pairs={{0,6},{1,7},{2,4},{3,5},{4,2},{5,3},{6,0},{7,1},{8,14},{9,15},{10,... | collective-permute-start | bytes 368648 | tf_op jit(solution)/shard_map/ppermute | solution.py:661
  101.2 14.4 %collective-permute-start.22 = (bf16[40,1536]{1,0:T(8,128)(2,1)S(1)}, bf16[40,1536]{1,0:T(8,128)(2,1)S(1)}, u32[]{:S(2)}, u32[]{:S(2)}) collective-permute-start(bf16[40,1536]{1,0:T(8,128)(2,1)S(1)} %get-tuple-element.270), channel_id=1, source_target_pairs={{0,3},{1,2},{2,1},{3,0},{4,7},{5,6},{6,5},{7,4},{8,11},{9,10},{10,... | collective-permute-start | bytes 368648 | tf_op jit(solution)/shard_map/ppermute | solution.py:661
  103.7 11.9 %collective-permute-start.21 = (bf16[40,1536]{1,0:T(8,128)(2,1)S(1)}, bf16[40,1536]{1,0:T(8,128)(2,1)S(1)}, u32[]{:S(2)}, u32[]{:S(2)}) collective-permute-start(bf16[40,1536]{1,0:T(8,128)(2,1)S(1)} %get-tuple-element.271), channel_id=1, source_target_pairs={{0,2},{1,3},{2,0},{3,1},{4,6},{5,7},{6,4},{7,5},{8,10},{9,11},{10,... | collective-permute-start | bytes 368648 | tf_op jit(solution)/shard_map/ppermute | solution.py:661
  105.7 13.1 %collective-permute-start.25 = (bf16[40,1536]{1,0:T(8,128)(2,1)S(1)}, bf16[40,1536]{1,0:T(8,128)(2,1)S(1)}, u32[]{:S(2)}, u32[]{:S(2)}) collective-permute-start(bf16[40,1536]{1,0:T(8,128)(2,1)S(1)} %get-tuple-element.269), channel_id=1, source_target_pairs={{0,4},{1,5},{2,6},{3,7},{4,0},{5,1},{6,2},{7,3},{8,12},{9,13},{10,... | collective-permute-start | bytes 368648 | tf_op jit(solution)/shard_map/ppermute | solution.py:661
  144.2 12.7 %collective-permute-start.46 = (bf16[192,768]{1,0:T(8,128)(2,1)S(1)}, bf16[192,768]{1,0:T(8,128)(2,1)S(1)}, u32[]{:S(2)}, u32[]{:S(2)}) collective-permute-start(bf16[192,768]{1,0:T(8,128)(2,1)S(1)} %get-tuple-element.223), channel_id=1, source_target_pairs={{0,8},{8,0},{16,24},{24,16},{1,9},{9,1},{17,25},{25,17},{2,10},{10... | collective-permute-start | bytes 884744 | tf_op jit(solution)/shard_map/ppermute | solution.py:658
  144.5 12.4 %collective-permute-start.47 = (bf16[192,768]{1,0:T(8,128)(2,1)S(1)}, bf16[192,768]{1,0:T(8,128)(2,1)S(1)}, u32[]{:S(2)}, u32[]{:S(2)}) collective-permute-start(bf16[192,768]{1,0:T(8,128)(2,1)S(1)} %get-tuple-element.225), channel_id=1, source_target_pairs={{0,16},{8,24},{16,0},{24,8},{1,17},{9,25},{17,1},{25,9},{2,18},{10... | collective-permute-start | bytes 884744 | tf_op jit(solution)/shard_map/ppermute | solution.py:658
  151.3 13.4 %collective-permute-start.34 = (bf16[128,768]{1,0:T(8,128)(2,1)S(1)}, bf16[128,768]{1,0:T(8,128)(2,1)S(1)}, u32[]{:S(2)}, u32[]{:S(2)}) collective-permute-start(bf16[128,768]{1,0:T(8,128)(2,1)S(1)} %get-tuple-element.209), channel_id=1, source_target_pairs={{0,16},{8,24},{16,0},{24,8},{1,17},{9,25},{17,1},{25,9},{2,18},{10... | collective-permute-start | bytes 589832 | tf_op jit(solution)/shard_map/ppermute | solution.py:658
  197.8 14.7 %collective-permute-start.42 = (bf16[192,768]{1,0:T(8,128)(2,1)S(1)}, bf16[192,768]{1,0:T(8,128)(2,1)S(1)}, u32[]{:S(2)}, u32[]{:S(2)}) collective-permute-start(bf16[192,768]{1,0:T(8,128)(2,1)S(1)} %get-tuple-element.218.refs_1_), channel_id=1, source_target_pairs={{0,8},{8,0},{16,24},{24,16},{1,9},{9,1},{17,25},{25,17},{2,10},{10... | collective-permute-start | bytes 884744 | tf_op jit(solution)/shard_map/ppermute | solution.py:658
  197.9 14.6 %collective-permute-start.43 = (bf16[192,768]{1,0:T(8,128)(2,1)S(1)}, bf16[192,768]{1,0:T(8,128)(2,1)S(1)}, u32[]{:S(2)}, u32[]{:S(2)}) collective-permute-start(bf16[192,768]{1,0:T(8,128)(2,1)S(1)} %get-tuple-element.219.refs_3_), channel_id=1, source_target_pairs={{0,16},{8,24},{16,0},{24,8},{1,17},{9,25},{17,1},{25,9},{2,18},{10... | collective-permute-start | bytes 884744 | tf_op jit(solution)/shard_map/ppermute | solution.py:658
  205.4 13.7 %collective-permute-start.58 = (bf16[384,1536]{1,0:T(8,128)(2,1)S(1)}, bf16[384,1536]{1,0:T(8,128)(2,1)S(1)}, u32[]{:S(2)}, u32[]{:S(2)}) collective-permute-start(bf16[384,1536]{1,0:T(8,128)(2,1)S(1)} %shard_map.258.refs_1_), channel_id=1, source_target_pairs={{0,1},{1,0},{2,3},{3,2},{4,5},{5,4},{6,7},{7,6},{8,9},{9,8},{10,11... | collective-permute-start | bytes 3538952 | tf_op jit(solution)/shard_map/ppermute | solution.py:661
  (69 other events, 534.7 us)

commit v4 on v3

--- a/solution.py
+++ b/solution.py
@@ -165,6 +165,14 @@
 
 def shaped(shape, dtype=BF):
     return jax.ShapeDtypeStruct(shape, dtype)
+
+
+def spread_diagonals(rows, length):
+    while rows.shape[0] < length // 2:
+        rows = jnp.concatenate([rows, pltpu.roll(rows, rows.shape[0], 1)], axis=0)
+    half = length // 2
+    high = jnp.concatenate([rows[:, 3 * half :], rows[:, :half]], axis=1)
+    return jnp.concatenate([rows[:, :length], high], axis=0)
 
 
 def front_kernel(
@@ -198,8 +206,7 @@
     length, width = tokens.shape
     scale = (width // heads) ** (-0.5)
     experts = w_router.shape[0]
-    slot_rows = slots_out[0].shape[0]
-    flat_slots = slot_rows * len(slots_out)
+    flat_slots = sum(out.shape[0] for out in slots_out)
     inputs = tokens[...].astype(F32)
     normed = (inputs * rms_scale(inputs) * as_row(gain_attn)).astype(BF)
     normed_one_out[...] = normed
@@ -216,6 +223,11 @@
         precision=lax.Precision.HIGHEST,
         preferred_element_type=F32,
     )
+    rolled = jnp.broadcast_to(by_offset[:, None, :], (heads, 8, 2 * length))
+    rolled = rolled.reshape(8 * heads, 2 * length)
+    row = lax.broadcasted_iota(jnp.int32, rolled.shape, 0) % 8
+    for bit in (1, 2, 4):
+        rolled = jnp.where((row & bit) != 0, pltpu.roll(rolled, bit, 1), rolled)
     pair = 2 * width // heads
     masks = half_masks(length, pair)
     for p in range(heads // 2):
@@ -224,11 +236,10 @@
         probs = []
         for half in (0, 1):
             h = 2 * p + half
-            base = jnp.broadcast_to(by_offset[h : h + 1, :], (length, 2 * length))
-            bias = pltpu.roll(base, 0, 1, stride=1, stride_axis=0)[:, :length]
+            bias = spread_diagonals(rolled[8 * h : 8 * h + 8], length)
             scores = mm_nt(q2, k2 * masks[half]) * scale + bias
             e = jnp.exp(scores - jnp.max(scores, axis=-1, keepdims=True))
-            e = (e / jnp.sum(e, axis=-1, keepdims=True)).astype(BF)
+            e = (e * (1.0 / jnp.sum(e, axis=-1, keepdims=True))).astype(BF)
             probs_out[h] = e
             probs.append(e)
         mixed_out[:, at] = mm(
@@ -254,7 +265,10 @@
     ).astype(F32)
     counts = mm(mask.astype(BF), earlier.astype(BF))
     position = jnp.sum(mask * counts, axis=0, keepdims=True).astype(jnp.int32)
-    target = jnp.where(position < cap, (chosen ^ shift_ref[0]) * cap + position, -1)
+    slot = chosen ^ shift_ref[0]
+    if len(slots_out) > 1:
+        slot = (slot & 1) * (experts // 2) + (slot >> 1)
+    target = jnp.where(position < cap, slot * cap + position, -1)
     gate = jnp.sum(mask * router, axis=0, keepdims=True)
     row = lax.broadcasted_iota(jnp.int32, (8, length), 0)
     packed = jnp.where(
@@ -266,8 +280,10 @@
     place = place.astype(BF)
     sent = (packed.T[:, :1] * cotangent[...].astype(F32)).astype(BF)
     normed_slots, grad_slots = mm(place, normed_two), mm(place, sent)
-    for i, out in enumerate(slots_out):
-        rows = slice(i * slot_rows, (i + 1) * slot_rows)
+    first = 0
+    for out in slots_out:
+        rows = slice(first, first + out.shape[0])
+        first += out.shape[0]
         out[:, :width] = normed_slots[rows].astype(BF)
         out[:, width:] = grad_slots[rows].astype(BF)
 
@@ -548,6 +564,28 @@
             out[half:, :] = tail.astype(BF)
 
 
+def rows_kernel(place_ref, own, got, keep, send):
+    half = keep.shape[0]
+    for out, side in ((keep, place_ref[3]), (send, 1 - place_ref[3])):
+        rows = pl.ds(pl.multiple_of(side * half, half), half)
+        out[...] = both(own, got, rows, slice(None)).astype(BF)
+
+
+def pick_kernel(place_ref, own_a, got_a, own_b, got_b, keep, send):
+    left = both(own_a, got_a, slice(None), slice(None)).astype(BF)
+    right = both(own_b, got_b, slice(None), slice(None)).astype(BF)
+
+    @pl.when(place_ref[4] == 0)
+    def _():
+        keep[...] = left
+        send[...] = right
+
+    @pl.when(place_ref[4] != 0)
+    def _():
+        keep[...] = right
+        send[...] = left
+
+
 def join_kernel(place_ref, own_a, got_a, own_b, got_b, keep, send):
     rows, columns = own_b.shape
     half = rows // 2
@@ -592,15 +630,18 @@
         out[at * rows : (at + 1) * rows, :] = source[...]
 
 
-def half_kernel(place_ref, own_a, far_a, own_b, far_b, out):
+def half_kernel(parts, place_ref, own_a, far_a, own_b, far_b, out):
     block, columns = own_a.shape[0] // 2, own_a.shape[1]
+    rows = block // parts
     sources = ((own_a, 0, 0, 1, 2), (far_a, 0, 1, 1, 2), (own_b, 1, 0, 2, 1), (far_b, 1, 1, 2, 1))
     for source, side, far, bit_1, bit_2 in sources:
         for i in (0, 1):
-            at = ((place_ref[bit_1] ^ far) * 2 + (place_ref[bit_2] ^ i)) * block
-            out[
-                pl.ds(pl.multiple_of(at, block), block), side * columns : (side + 1) * columns
-            ] = source[i * block : (i + 1) * block, :]
+            at = ((place_ref[bit_1] ^ far) * 2 + (place_ref[bit_2] ^ i)) * rows
+            for part in range(parts):
+                out[
+                    pl.ds(pl.multiple_of(at + part * 4 * rows, rows), rows),
+                    side * columns : (side + 1) * columns,
+                ] = source[i * block + part * rows : i * block + (part + 1) * rows, :]
 
 
 def finish_kernel(other, count, place_ref, *refs):
@@ -647,6 +688,7 @@
     cap = (5 * length + 4 * experts - 1) // (4 * experts)
     flat_slots = experts * cap
     direct = n_wide <= 8
+    slot_counts = [cap] * (n_wide // 2) + [flat_slots // 2] if direct else [flat_slots]
     narrow_at, wide_at = lax.axis_index("narrow"), lax.axis_index("wide")
     core_ref = (wide_at % 2).reshape(1)
     shift_ref = (wide_at if direct else jnp.zeros((), jnp.int32)).reshape(1)
@@ -684,7 +726,7 @@
             rows_bf,
             shaped((8 + experts, length), F32),
         ]
-        + [shaped((cap if direct else flat_slots, 2 * width))] * (n_wide if direct else 1),
+        + [shaped((n, 2 * width)) for n in slot_counts],
         shift_ref,
         tokens,
         w_query,
@@ -706,11 +748,11 @@
     )
 
     quarter = flat_slots // 4
-    order = (0, 3, 1, 2)
+    order = (0, 2, 1, 3)
     if direct:
         per = n_wide // 4
-        near = jnp.split(along(jnp.concatenate(slots[1::2], axis=0), 1), n_wide // 2)
-        parts = [jnp.concatenate([slots[2 * i], near[i]], axis=0) for i in order]
+        near = jnp.split(along(slots[-1], 1), n_wide // 2)
+        parts = [jnp.concatenate([slots[i], near[i]], axis=0) for i in order]
         parts = [[along(p, 2 * i) if i else p] for i, p in zip(order, parts)]
     else:
         moved = lax.all_to_all(slots[0], "wide", split_axis=0, concat_axis=0, tiled=True)
@@ -723,6 +765,18 @@
         return [a, b, a1, b1, a2, b2, a3, b3]
 
     quarters = [jnp.concatenate(part, axis=0) for part in parts]
+
+    def hop_one(keep_a0, keep_b0, send_a, send_b, keep_b1, keep_a1):
+        got_a, got_b = across(send_a, 1), across(send_b, 2)
+        next_a = (keep_a1.astype(F32) + got_a[1].astype(F32)).astype(BF)
+        next_b = (keep_b1.astype(F32) + got_b[1].astype(F32)).astype(BF)
+        return [keep_a0, keep_b0, got_a, got_b, next_a, next_b]
+
+    def hop_two(keep_a0, keep_b0, got_a, got_b, next_a, next_b):
+        last_a, last_b = across(next_a, 2), across(next_b, 1)
+        sum_a = keep_a0.astype(F32) + got_a[0].astype(F32) + last_a.astype(F32)
+        sum_b = keep_b0.astype(F32) + got_b[0].astype(F32) + last_b.astype(F32)
+        return [sum_a.astype(BF), sum_b.astype(BF)]
 
     def reduce(keep_a, send_a, keep_b, send_b):
         got_a, got_b = across(send_a, 1), across(send_b, 2)
@@ -760,21 +814,19 @@
     quarters[2], quarters[3], first[3], first[4] = lax.optimization_barrier(
         (quarters[2], quarters[3], first[3], first[4])
     )
-    done_1 = experts_of(first)
-    a, b = quarters[2:]
-    a1, b2 = across(a, 1), across(b, 2)
-    a2, b1 = across(a, 2), across(b, 1)
-    a1, b2, done_1 = lax.optimization_barrier((a1, b2, done_1))
-    a3, b3 = across(a1, 2), across(b2, 1)
-    second = [a, b, a1, b1, a2, b2, a3, b3]
-    done_2 = experts_of(second)
+    second = gather(*quarters[2:])
+    done_1, done_2 = experts_of(first), experts_of(second)
     groups = [first, second]
     kept = done_1[:4] + done_2[:4]
-    sums = [*reduced(*done_1[4:]), *reduced(*done_2[4:])]
+    h1 = hop_one(*done_1[4:])
+    done_2, h1 = lax.optimization_barrier((done_2, h1))
+    h2 = hop_one(*done_2[4:])
+    sums = hop_two(*h1) + hop_two(*h2)
     if direct:
         sums = [sums[order.index(i)] for i in range(4)]
         returned = [sums[k // per][k % per * cap : (k % per + 1) * cap] for k in range(n_wide)]
         returned = [returned[0]] + [along(returned[k], k) for k in range(1, n_wide)]
+        returned = returned[::2] + returned[1::2]
     else:
         returned = jnp.concatenate(sums, axis=0)
         returned = [lax.all_to_all(returned, "wide", split_axis=0, concat_axis=0, tiled=True)]
@@ -864,16 +916,42 @@
             own,
             along(other, 2),
         )
-        got = along(other, 4)
+        return own, along(other, 4)
+
+    def scatter_deep(keep, send):
+        own, other = hop(rows_kernel, [(half // 2, 2 * width)] * 2, keep, along(send, 1))
+        own_a, send_a, own_b, send_b = hop(
+            first_kernel, [(half // 4, width)] * 4, own, along(other, 2)
+        )
+        own_a, send_a, own_b, send_b = hop(
+            second_kernel,
+            [(half // 8, width)] * 4,
+            own_a,
+            across(send_a, 1),
+            own_b,
+            across(send_b, 2),
+        )
+        own, other = hop(
+            pick_kernel,
+            [(half // 8, width)] * 2,
+            own_a,
+            across(send_a, 2),
+            own_b,
+            across(send_b, 1),
+        )
+        return own, along(other, 4)
+
+    def last_sum(own, got):
+        rows = half // 8
         x = (own[:rows].astype(F32) + got[:rows].astype(F32)).astype(BF)
         for k in deeper:
             bit, size = wide_at // k % 2, x.shape[0] // 2
             other = lax.dynamic_slice_in_dim(x, (1 - bit) * size, size, 0)
             mine = lax.dynamic_slice_in_dim(x, bit * size, size, 0)
             x = (mine.astype(F32) + along(other, k).astype(F32)).astype(BF)
-        return x, own, got
-
-    def spread_out(x):
+        return x
+
+    def spread_out(x, parts):
         step = functools.partial
         for k in reversed(deeper):
             bit, far = wide_at // k % 2, along(x, k)
@@ -889,7 +967,8 @@
             across(b, 1),
             stream=False,
         )
-        (x,) = hop(half_kernel, [(half, 2 * width)], a, across(a, 1), b, across(b, 2))
+        kernel = step(half_kernel, parts)
+        (x,) = hop(kernel, [(half, 2 * width)], a, across(a, 1), b, across(b, 2))
         return x
 
     def finish(sources, outs=()):
@@ -909,8 +988,8 @@
             compiler_params=pltpu.CompilerParams(vmem_limit_bytes=LOW),
         )(place, *sources, *outs)
 
-    part_1, own, got = scatter(keep_1, send_1, ride)
-    part_2, _, _ = scatter(keep_2, send_2, 0)
+    own, got = scatter(keep_1, send_1, ride)
+    part_1, part_2 = last_sum(own, got), last_sum(*scatter_deep(keep_2, send_2))
     if not direct:
         own = lax.psum(small, ("narrow", "wide"))
         got = jnp.zeros_like(own)
@@ -927,7 +1006,7 @@
         scratch=[pltpu.VMEM((small_rows, width), F32)],
         stream=False,
     )
-    part_1, part_2 = spread_out(part_1), spread_out(part_2)
+    part_1, part_2 = spread_out(part_1, 1), spread_out(part_2, 2)
     far_1, far_2 = along(part_1, 1), along(part_2, 1)
     near = finish((part_1, part_2))
     far_1, far_2, near, small = lax.optimization_barrier((far_1, far_2, near, small))

time: 223 us -> 218 us (0.978)
  waiting for transfers between devices: 74.1 us -> 65.8 us
  starting transfers between devices: 75 us -> 77.4 us
    ppermute x36, waiting for transfers between devices: 41 us -> 34.8 us  [across(): return lax.ppermute(x, 'narrow', pairs(n_narrow, k))]
    ppermute x36, starting transfers between devices: 28.6 us -> 31.1 us  [across(): return lax.ppermute(x, 'narrow', pairs(n_narrow, k))]
where the time goes in v4:
time: 218 us
  starting transfers between devices  77.4 us (36%)
  Pallas kernels  66.2 us (30%)
  waiting for transfers between devices  65.8 us (30%)
  local copies, waits for them, and re-layouts  5.12 us (2%)
    pallas_call x22, Pallas kernels, call(): pl.pallas_call(body, out_shape=tuple(outs), in_specs=[pl.BlockSpec(memory...  60.5 us
    ppermute x23, starting transfers between devices, along(): return lax.ppermute(x, 'wide', pairs(n_wide, k))  46.3 us
    ppermute x36, waiting for transfers between devices, across(): return lax.ppermute(x, 'narrow', pairs(n_narrow, k))  34.8 us
    ppermute x36, starting transfers between devices, across(): return lax.ppermute(x, 'narrow', pairs(n_narrow, k))  31.1 us
    ppermute x23, waiting for transfers between devices, along(): return lax.ppermute(x, 'wide', pairs(n_wide, k))  31 us
    pallas_call x2, Pallas kernels, finish(): pl.pallas_call(functools.partial(finish_kernel, bool(outs), len(sources))...  5.66 us
  transfers between devices with their start and end apart: 59, of which 28 were waited for; matrix products, arithmetic and copies ran while one was open for 1% of the time, Pallas kernels for 16%

profile of v4, /device:TPU:1, one launch (start us, length us, event | category | flops | bytes accessed | tf_op | source)
XLA Modules:
  0.0 217.7 jit_solution(9969547585823871512)
XLA Ops:
  0.6 11.2 %shard_map.238 = (bf16[256,768]{1,0:T(8,128)(2,1)}, bf16[256,768]{1,0:T(8,128)(2,1)}, bf16[256,768]{1,0:T(8,128)(2,1)}, bf16[256,768]{1,0:T(8,128)(2,1)}, bf16[1...) custom-call(s32[1]{0:T(128)} %bitcast.1.refs_0_, ...), custom_call_target="tpu_custom_call" | custom-call | flops 1409286144 | bytes 11246112 | tf_op jit(solution)/shard_map/pallas_call | solution.py:150
  15.0 2.5 %collective-permute-start.1 = (bf16[80,1536]{1,0:T(8,128)(2,1)S(1)}, bf16[80,1536]{1,0:T(8,128)(2,1)S(1)}, u32[]{:S(2)}, u32[]{:S(2)}) collective-permute-start(bf16[80,1536]{1,0:T(8,128)(2,1)S(1)} %pad_maximum_fusion), channel_id=1, source_target_pairs={{0,2},{1,3},{2,0},{3,1},{4,6},{5,7},{6,4},{7,5},{8,10},{9,11},{10,... | collective-permute-start | bytes 737288 | tf_op jit(solution)/shard_map/ppermute | solution.py:703
  22.5 5.2 %collective-permute-done.3.refs_2_.refs_1_ = bf16[80,1536]{1,0:T(8,128)(2,1)S(1)} collective-permute-done((bf16[80,1536]{1,0:T(8,128)(2,1)S(1)}, bf16[80,1536]{1,0:T(8,128)(2,1)S(1)}, u32[]{:S(2)}, u32[]{:S(2)}) %collective-permute-start.3) | collective-permute-done | bytes 245792 | tf_op jit(solution)/shard_map/ppermute | solution.py:703
  30.4 5.5 %collective-permute-done.2.refs_2_.refs_9_ = bf16[80,1536]{1,0:T(8,128)(2,1)S(1)} collective-permute-done((bf16[80,1536]{1,0:T(8,128)(2,1)S(1)}, bf16[80,1536]{1,0:T(8,128)(2,1)S(1)}, u32[]{:S(2)}, u32[]{:S(2)}) %collective-permute-start.2) | collective-permute-done | bytes 245792 | tf_op jit(solution)/shard_map/ppermute | solution.py:703
  43.5 2.7 %collective-permute-done.15.refs_9_.refs_7_ = bf16[80,1536]{1,0:T(8,128)(2,1)S(1)} collective-permute-done((bf16[80,1536]{1,0:T(8,128)(2,1)S(1)}, bf16[80,1536]{1,0:T(8,128)(2,1)S(1)}, u32[]{:S(2)}, u32[]{:S(2)}) %collective-permute-start.15) | collective-permute-done | bytes 245792 | tf_op jit(solution)/shard_map/ppermute | solution.py:700
  47.0 7.1 %shard_map.240 = (bf16[320,768]{1,0:T(8,128)(2,1)}, bf16[320,768]{1,0:T(8,128)(2,1)}, bf16[320,768]{1,0:T(8,128)(2,1)}, bf16[320,768]{1,0:T(8,128)(2,1)}, bf16[8...) custom-call(bf16[768,768]{1,0:T(8,128)(2,1)} %bitcast.53, ...), custom_call_target="tpu_custom_call" | custom-call | flops 3019898880 | bytes 8257536 | tf_op jit(solution)/shard_map/pallas_call | solution.py:150
  58.2 7.3 %shard_map.239 = (bf16[320,768]{1,0:T(8,128)(2,1)}, bf16[320,768]{1,0:T(8,128)(2,1)}, bf16[320,768]{1,0:T(8,128)(2,1)}, bf16[320,768]{1,0:T(8,128)(2,1)}, bf16[8...) custom-call(bf16[768,768]{1,0:T(8,128)(2,1)} %bitcast.54, ...), custom_call_target="tpu_custom_call" | custom-call | flops 3019898880 | bytes 8257536 | tf_op jit(solution)/shard_map/pallas_call | solution.py:150
  70.9 5.0 %collective-permute-done.18 = bf16[80,1536]{1,0:T(8,128)(2,1)S(1)} collective-permute-done((bf16[80,1536]{1,0:T(8,128)(2,1)S(1)}, bf16[80,1536]{1,0:T(8,128)(2,1)S(1)}, u32[]{:S(2)}, u32[]{:S(2)}) %collective-permute-start.18) | collective-permute-done | bytes 245792 | tf_op jit(solution)/shard_map/ppermute | solution.py:700
  76.7 11.6 %collective-permute-start.27 = (bf16[40,1536]{1,0:T(8,128)(2,1)S(1)}, bf16[40,1536]{1,0:T(8,128)(2,1)S(1)}, u32[]{:S(2)}, u32[]{:S(2)}) collective-permute-start(bf16[40,1536]{1,0:T(8,128)(2,1)S(1)} %get-tuple-element.266), channel_id=1, source_target_pairs={{0,1},{1,0},{2,3},{3,2},{4,5},{5,4},{6,7},{7,6},{8,9},{9,8},{10,11... | collective-permute-start | bytes 368648 | tf_op jit(solution)/shard_map/ppermute | solution.py:703
  88.4 3.0 %collective-permute-start.23 = (bf16[40,1536]{1,0:T(8,128)(2,1)S(1)}, bf16[40,1536]{1,0:T(8,128)(2,1)S(1)}, u32[]{:S(2)}, u32[]{:S(2)}) collective-permute-start(bf16[40,1536]{1,0:T(8,128)(2,1)S(1)} %get-tuple-element.263), channel_id=1, source_target_pairs={{0,4},{1,5},{2,6},{3,7},{4,0},{5,1},{6,2},{7,3},{8,12},{9,13},{10,... | collective-permute-start | bytes 368648 | tf_op jit(solution)/shard_map/ppermute | solution.py:703
  92.2 4.7 %collective-permute-done.20 = bf16[80,1536]{1,0:T(8,128)(2,1)S(1)} collective-permute-done((bf16[80,1536]{1,0:T(8,128)(2,1)S(1)}, bf16[80,1536]{1,0:T(8,128)(2,1)S(1)}, u32[]{:S(2)}, u32[]{:S(2)}) %collective-permute-start.20) | collective-permute-done | bytes 245792 | tf_op jit(solution)/shard_map/ppermute | solution.py:700
  97.0 4.1 %collective-permute-start.28 = (bf16[40,1536]{1,0:T(8,128)(2,1)S(1)}, bf16[40,1536]{1,0:T(8,128)(2,1)S(1)}, u32[]{:S(2)}, u32[]{:S(2)}) collective-permute-start(bf16[40,1536]{1,0:T(8,128)(2,1)S(1)} %get-tuple-element.264), channel_id=1, source_target_pairs={{0,3},{1,2},{2,1},{3,0},{4,7},{5,6},{6,5},{7,4},{8,11},{9,10},{10,... | collective-permute-start | bytes 368648 | tf_op jit(solution)/shard_map/ppermute | solution.py:703
  106.1 8.2 %shard_map.241 = (f32[1,768,768]{2,1,0:T(8,128)}, f32[1,768,768]{2,1,0:T(8,128)}) custom-call(bf16[80,1536]{1,0:T(8,128)(2,1)} %copy-done.2, bf16[80,1536]{1,0:T(8,128)(2,1)} %copy-done.24, bf16[80,1536]{1,0:T(8,128)(2,1)} %copy-done.25, bf16[80,1536]{1,0:T(8,128)(2,1)} %copy-done.28, bf16[80,1536]{1,0:T(8,128)(2,1)} %copy-done.26, ...), custom_call_target="tpu_custom_call" | custom-call | flops 3019898880 | bytes 12582912 | tf_op jit(solution)/shard_map/pallas_call | solution.py:150
  115.2 16.3 %shard_map.242 = (bf16[256,768]{1,0:T(8,128)(2,1)}, bf16[256,768]{1,0:T(8,128)(2,1)}, bf16[400,1536]{1,0:T(8,128)(2,1)}, bf16[400,1536]{1,0:T(8,128)(2,1)}, bf16...) custom-call(s32[1]{0:T(128)} %bitcast.refs_0_, f32[16,256]{1,0:T(8,128)} %get-tuple-element.134.refs_1_, ...), custom_call_target="tpu_custom_call" | custom-call | flops 3019898880 | bytes 16850944 | tf_op jit(solution)/shard_map/pallas_call | solution.py:150
  132.2 2.6 %collective-permute-done.45.refs_2_ = bf16[384,1536]{1,0:T(8,128)(2,1)} collective-permute-done((bf16[384,1536]{1,0:T(8,128)(2,1)}, bf16[384,1536]{1,0:T(8,128)(2,1)}, u32[]{:S(2)}, u32[]{:S(2)}) %collective-permute-start.45) | collective-permute-done | bytes 1179680 | tf_op jit(solution)/shard_map/ppermute | solution.py:703
  137.6 2.7 %collective-permute-start.46 = (bf16[192,1536]{1,0:T(8,128)(2,1)S(1)}, bf16[192,1536]{1,0:T(8,128)(2,1)S(1)}, u32[]{:S(2)}, u32[]{:S(2)}) collective-permute-start(bf16[192,1536]{1,0:T(8,128)(2,1)S(1)} %get-tuple-element.217), channel_id=1, source_target_pairs={{0,2},{1,3},{2,0},{3,1},{4,6},{5,7},{6,4},{7,5},{8,10},{9,11},{10,... | collective-permute-start | bytes 1769480 | tf_op jit(solution)/shard_map/ppermute | solution.py:703
  142.6 6.4 %collective-permute-done.33.refs_4_ = bf16[192,768]{1,0:T(8,128)(2,1)S(1)} collective-permute-done((bf16[192,768]{1,0:T(8,128)(2,1)S(1)}, bf16[192,768]{1,0:T(8,128)(2,1)S(1)}, u32[]{:S(2)}, u32[]{:S(2)}) %collective-permute-start.33) | collective-permute-done | bytes 294944 | tf_op jit(solution)/shard_map/ppermute | solution.py:700
  157.7 2.7 %collective-permute-done.47.refs_2_ = bf16[96,768]{1,0:T(8,128)(2,1)S(1)} collective-permute-done((bf16[96,768]{1,0:T(8,128)(2,1)S(1)}, bf16[96,768]{1,0:T(8,128)(2,1)S(1)}, u32[]{:S(2)}, u32[]{:S(2)}) %collective-permute-start.47) | collective-permute-done | bytes 147488 | tf_op jit(solution)/shard_map/ppermute | solution.py:700
  171.5 5.7 %collective-permute-done.37.refs_1_ = bf16[80,768]{1,0:T(8,128)(2,1)S(1)} collective-permute-done((bf16[80,768]{1,0:T(8,128)(2,1)S(1)}, bf16[80,768]{1,0:T(8,128)(2,1)S(1)}, u32[]{:S(2)}, u32[]{:S(2)}) %collective-permute-start.37) | collective-permute-done | bytes 122912 | tf_op jit(solution)/shard_map/ppermute | solution.py:703
  180.7 2.9 %collective-permute-done.38.refs_2_ = bf16[48,768]{1,0:T(8,128)(2,1)S(1)} collective-permute-done((bf16[48,768]{1,0:T(8,128)(2,1)S(1)}, bf16[48,768]{1,0:T(8,128)(2,1)S(1)}, u32[]{:S(2)}, u32[]{:S(2)}) %collective-permute-start.38) | collective-permute-done | bytes 73760 | tf_op jit(solution)/shard_map/ppermute | solution.py:703
  201.2 6.8 %collective-permute-start.58 = (bf16[384,1536]{1,0:T(8,128)(2,1)S(1)}, bf16[384,1536]{1,0:T(8,128)(2,1)S(1)}, u32[]{:S(2)}, u32[]{:S(2)}) collective-permute-start(bf16[384,1536]{1,0:T(8,128)(2,1)S(1)} %shard_map.258.refs_1_), channel_id=1, source_target_pairs={{0,1},{1,0},{2,3},{3,2},{4,5},{5,4},{6,7},{7,6},{8,9},{9,8},{10,11... | collective-permute-start | bytes 3538952 | tf_op jit(solution)/shard_map/ppermute | solution.py:703
  208.7 2.5 %collective-permute-start.44 = (bf16[384,1536]{1,0:T(8,128)(2,1)S(1)}, bf16[384,1536]{1,0:T(8,128)(2,1)S(1)}, u32[]{:S(2)}, u32[]{:S(2)}) collective-permute-start(bf16[384,1536]{1,0:T(8,128)(2,1)S(1)} %shard_map.250.refs_0_), channel_id=1, source_target_pairs={{0,1},{1,0},{2,3},{3,2},{4,5},{5,4},{6,7},{7,6},{8,9},{9,8},{10,11... | collective-permute-start | bytes 3538952 | tf_op jit(solution)/shard_map/ppermute | solution.py:703
  211.8 2.8 %shard_map.259 = (f32[768,768]{1,0:T(8,128)}, f32[768,768]{1,0:T(8,128)}, f32[768,768]{1,0:T(8,128)}, f32[768,768]{1,0:T(8,128)}) custom-call(s32[5]{0:T(128)S(1)} %stack.20.refs_0_.place_ref, bf16[384,1536]{1,0:T(8,128)(2,1)S(1)} %shard_map.250.refs_0_, bf16[384,1536]{1,0:T(8,128)(2,1)S(1)} %shard_map.258.refs_1_), custom_call_target="tpu_custom_call" | custom-call | tf_op jit(solution)/shard_map/pallas_call | solution.py:976
  214.7 2.8 %shard_map.261 = (f32[768,768]{1,0:T(8,128)}, f32[768,768]{1,0:T(8,128)}, f32[768,768]{1,0:T(8,128)}, f32[768,768]{1,0:T(8,128)}) custom-call(s32[5]{0:T(128)S(1)} %stack.20.refs_0_.place_ref, bf16[384,1536]{1,0:T(8,128)(2,1)S(1)} %collective-permute-done.44.refs_0_, ...), custom_call_target="tpu_custom_call", output_to_operand_aliasing={{0}: (3, {}), {1}: (4, {}), {2}: (5, {}), {3}: (6, {})} | custom-call | tf_op jit(solution)/shard_map/pallas_call | solution.py:976
  (214 shorter events, 83.7 us)
Async XLA Ops:
  15.0 14.0 %collective-permute-start.1 = (bf16[80,1536]{1,0:T(8,128)(2,1)S(1)}, bf16[80,1536]{1,0:T(8,128)(2,1)S(1)}, u32[]{:S(2)}, u32[]{:S(2)}) collective-permute-start(bf16[80,1536]{1,0:T(8,128)(2,1)S(1)} %pad_maximum_fusion), channel_id=1, source_target_pairs={{0,2},{1,3},{2,0},{3,1},{4,6},{5,7},{6,4},{7,5},{8,10},{9,11},{10,... | collective-permute-start | bytes 737288 | tf_op jit(solution)/shard_map/ppermute | solution.py:703
  17.5 10.3 %collective-permute-start.3 = (bf16[80,1536]{1,0:T(8,128)(2,1)S(1)}, bf16[80,1536]{1,0:T(8,128)(2,1)S(1)}, u32[]{:S(2)}, u32[]{:S(2)}) collective-permute-start(bf16[80,1536]{1,0:T(8,128)(2,1)S(1)} %pad_maximum_fusion.2), channel_id=1, source_target_pairs={{0,4},{1,5},{2,6},{3,7},{4,0},{5,1},{6,2},{7,3},{8,12},{9,13},{10,... | collective-permute-start | bytes 737288 | tf_op jit(solution)/shard_map/ppermute | solution.py:703
  19.9 10.3 %collective-permute-start.12 = (bf16[80,1536]{1,0:T(8,128)(2,1)S(1)}, bf16[80,1536]{1,0:T(8,128)(2,1)S(1)}, u32[]{:S(2)}, u32[]{:S(2)}) collective-permute-start(bf16[80,1536]{1,0:T(8,128)(2,1)S(1)} %pad_maximum_fusion.3.refs_1_.refs_0_), channel_id=1, source_target_pairs={{0,8},{8,0},{16,24},{24,16},{1,9},{9,1},{17,25},{25,17},{2,10},{10... | collective-permute-start | bytes 737288 | tf_op jit(solution)/shard_map/ppermute | solution.py:700
  21.2 14.8 %collective-permute-start.5 = (bf16[80,1536]{1,0:T(8,128)(2,1)S(1)}, bf16[80,1536]{1,0:T(8,128)(2,1)S(1)}, u32[]{:S(2)}, u32[]{:S(2)}) collective-permute-start(bf16[80,1536]{1,0:T(8,128)(2,1)S(1)} %pad_maximum_fusion.3.refs_1_.refs_0_), channel_id=1, source_target_pairs={{0,16},{8,24},{16,0},{24,8},{1,17},{9,25},{17,1},{25,9},{2,18},{10... | collective-permute-start | bytes 737288 | tf_op jit(solution)/shard_map/ppermute | solution.py:700
  22.4 13.5 %collective-permute-start.2 = (bf16[80,1536]{1,0:T(8,128)(2,1)S(1)}, bf16[80,1536]{1,0:T(8,128)(2,1)S(1)}, u32[]{:S(2)}, u32[]{:S(2)}) collective-permute-start(bf16[80,1536]{1,0:T(8,128)(2,1)S(1)} %pad_maximum_fusion.1), channel_id=1, source_target_pairs={{0,6},{1,7},{2,4},{3,5},{4,2},{5,3},{6,0},{7,1},{8,14},{9,15},{10,... | collective-permute-start | bytes 737288 | tf_op jit(solution)/shard_map/ppermute | solution.py:703
  38.7 16.7 %collective-permute-start.8 = (bf16[80,1536]{1,0:T(8,128)(2,1)S(1)}, bf16[80,1536]{1,0:T(8,128)(2,1)S(1)}, u32[]{:S(2)}, u32[]{:S(2)}) collective-permute-start(bf16[80,1536]{1,0:T(8,128)(2,1)S(1)} %collective-permute-done.1.refs_1_.refs_8_), channel_id=1, source_target_pairs={{0,16},{8,24},{16,0},{24,8},{1,17},{9,25},{17,1},{25,9},{2,18},{10... | collective-permute-start | bytes 737288 | tf_op jit(solution)/shard_map/ppermute | solution.py:700
  39.0 17.8 %collective-permute-start.7 = (bf16[80,1536]{1,0:T(8,128)(2,1)S(1)}, bf16[80,1536]{1,0:T(8,128)(2,1)S(1)}, u32[]{:S(2)}, u32[]{:S(2)}) collective-permute-start(bf16[80,1536]{1,0:T(8,128)(2,1)S(1)} %collective-permute-done.2.refs_2_.refs_9_), channel_id=1, source_target_pairs={{0,8},{8,0},{16,24},{24,16},{1,9},{9,1},{17,25},{25,17},{2,10},{10... | collective-permute-start | bytes 737288 | tf_op jit(solution)/shard_map/ppermute | solution.py:700
  41.1 15.7 %collective-permute-start.10 = (bf16[80,1536]{1,0:T(8,128)(2,1)S(1)}, bf16[80,1536]{1,0:T(8,128)(2,1)S(1)}, u32[]{:S(2)}, u32[]{:S(2)}) collective-permute-start(bf16[80,1536]{1,0:T(8,128)(2,1)S(1)} %collective-permute-done.6.refs_3_.refs_10_), channel_id=1, source_target_pairs={{0,16},{8,24},{16,0},{24,8},{1,17},{9,25},{17,1},{25,9},{2,18},{10... | collective-permute-start | bytes 737288 | tf_op jit(solution)/shard_map/ppermute | solution.py:700
  42.6 14.2 %collective-permute-start.11 = (bf16[80,1536]{1,0:T(8,128)(2,1)S(1)}, bf16[80,1536]{1,0:T(8,128)(2,1)S(1)}, u32[]{:S(2)}, u32[]{:S(2)}) collective-permute-start(bf16[80,1536]{1,0:T(8,128)(2,1)S(1)} %collective-permute-done.9.refs_7_.refs_13_), channel_id=1, source_target_pairs={{0,8},{8,0},{16,24},{24,16},{1,9},{9,1},{17,25},{25,17},{2,10},{10... | collective-permute-start | bytes 737288 | tf_op jit(solution)/shard_map/ppermute | solution.py:700
  54.1 13.6 %collective-permute-start.16 = (bf16[2,80,1536]{2,1,0:T(8,128)(2,1)}, bf16[2,80,1536]{2,1,0:T(8,128)(2,1)S(1)}, u32[]{:S(2)}, u32[]{:S(2)}) collective-permute-start(bf16[2,80,1536]{2,1,0:T(8,128)(2,1)} %get-tuple-element.164), channel_id=1, source_target_pairs={{0,8},{8,0},{16,24},{24,16},{1,9},{9,1},{17,25},{25,17},{2,10},{10... | collective-permute-start | bytes 1474568 | tf_op jit(solution)/shard_map/ppermute | solution.py:700
  55.4 12.4 %collective-permute-start.17 = (bf16[2,80,1536]{2,1,0:T(8,128)(2,1)}, bf16[2,80,1536]{2,1,0:T(8,128)(2,1)S(1)}, u32[]{:S(2)}, u32[]{:S(2)}) collective-permute-start(bf16[2,80,1536]{2,1,0:T(8,128)(2,1)} %get-tuple-element.165), channel_id=1, source_target_pairs={{0,16},{8,24},{16,0},{24,8},{1,17},{9,25},{17,1},{25,9},{2,18},{10... | collective-permute-start | bytes 1474568 | tf_op jit(solution)/shard_map/ppermute | solution.py:700
  69.2 19.1 %collective-permute-start.22 = (bf16[80,1536]{1,0:T(8,128)(2,1)S(1)}, bf16[80,1536]{1,0:T(8,128)(2,1)S(1)}, u32[]{:S(2)}, u32[]{:S(2)}) collective-permute-start(bf16[80,1536]{1,0:T(8,128)(2,1)S(1)} %fusion.10), channel_id=1, source_target_pairs={{0,8},{8,0},{16,24},{24,16},{1,9},{9,1},{17,25},{25,17},{2,10},{10... | collective-permute-start | bytes 737288 | tf_op jit(solution)/shard_map/ppermute | solution.py:700
  70.4 21.0 %collective-permute-start.19 = (bf16[2,80,1536]{2,1,0:T(8,128)(2,1)S(1)}, bf16[2,80,1536]{2,1,0:T(8,128)(2,1)S(1)}, u32[]{:S(2)}, u32[]{:S(2)}) collective-permute-start(bf16[2,80,1536]{2,1,0:T(8,128)(2,1)S(1)} %copy-done.22), channel_id=1, source_target_pairs={{0,8},{8,0},{16,24},{24,16},{1,9},{9,1},{17,25},{25,17},{2,10},{10... | collective-permute-start | bytes 1474568 | tf_op jit(solution)/shard_map/ppermute | solution.py:700
  70.6 21.4 %collective-permute-start.24 = (bf16[2,80,1536]{2,1,0:T(8,128)(2,1)S(1)}, bf16[2,80,1536]{2,1,0:T(8,128)(2,1)S(1)}, u32[]{:S(2)}, u32[]{:S(2)}) collective-permute-start(bf16[2,80,1536]{2,1,0:T(8,128)(2,1)S(1)} %copy-done.21), channel_id=1, source_target_pairs={{0,16},{8,24},{16,0},{24,8},{1,17},{9,25},{17,1},{25,9},{2,18},{10... | collective-permute-start | bytes 1474568 | tf_op jit(solution)/shard_map/ppermute | solution.py:700
  76.7 25.6 %collective-permute-start.27 = (bf16[40,1536]{1,0:T(8,128)(2,1)S(1)}, bf16[40,1536]{1,0:T(8,128)(2,1)S(1)}, u32[]{:S(2)}, u32[]{:S(2)}) collective-permute-start(bf16[40,1536]{1,0:T(8,128)(2,1)S(1)} %get-tuple-element.266), channel_id=1, source_target_pairs={{0,1},{1,0},{2,3},{3,2},{4,5},{5,4},{6,7},{7,6},{8,9},{9,8},{10,11... | collective-permute-start | bytes 368648 | tf_op jit(solution)/shard_map/ppermute | solution.py:703
  88.4 16.1 %collective-permute-start.29 = (bf16[40,1536]{1,0:T(8,128)(2,1)S(1)}, bf16[40,1536]{1,0:T(8,128)(2,1)S(1)}, u32[]{:S(2)}, u32[]{:S(2)}) collective-permute-start(bf16[40,1536]{1,0:T(8,128)(2,1)S(1)} %get-tuple-element.262), channel_id=1, source_target_pairs={{0,5},{1,4},{2,7},{3,6},{4,1},{5,0},{6,3},{7,2},{8,13},{9,12},{10,... | collective-permute-start | bytes 368648 | tf_op jit(solution)/shard_map/ppermute | solution.py:703
  88.4 25.9 %collective-permute-start.23 = (bf16[40,1536]{1,0:T(8,128)(2,1)S(1)}, bf16[40,1536]{1,0:T(8,128)(2,1)S(1)}, u32[]{:S(2)}, u32[]{:S(2)}) collective-permute-start(bf16[40,1536]{1,0:T(8,128)(2,1)S(1)} %get-tuple-element.263), channel_id=1, source_target_pairs={{0,4},{1,5},{2,6},{3,7},{4,0},{5,1},{6,2},{7,3},{8,12},{9,13},{10,... | collective-permute-start | bytes 368648 | tf_op jit(solution)/shard_map/ppermute | solution.py:703
  97.0 17.3 %collective-permute-start.28 = (bf16[40,1536]{1,0:T(8,128)(2,1)S(1)}, bf16[40,1536]{1,0:T(8,128)(2,1)S(1)}, u32[]{:S(2)}, u32[]{:S(2)}) collective-permute-start(bf16[40,1536]{1,0:T(8,128)(2,1)S(1)} %get-tuple-element.264), channel_id=1, source_target_pairs={{0,3},{1,2},{2,1},{3,0},{4,7},{5,6},{6,5},{7,4},{8,11},{9,10},{10,... | collective-permute-start | bytes 368648 | tf_op jit(solution)/shard_map/ppermute | solution.py:703
  101.1 13.3 %collective-permute-start.21 = (bf16[40,1536]{1,0:T(8,128)(2,1)S(1)}, bf16[40,1536]{1,0:T(8,128)(2,1)S(1)}, u32[]{:S(2)}, u32[]{:S(2)}) collective-permute-start(bf16[40,1536]{1,0:T(8,128)(2,1)S(1)} %get-tuple-element.265), channel_id=1, source_target_pairs={{0,2},{1,3},{2,0},{3,1},{4,6},{5,7},{6,4},{7,5},{8,10},{9,11},{10,... | collective-permute-start | bytes 368648 | tf_op jit(solution)/shard_map/ppermute | solution.py:703
  102.2 12.1 %collective-permute-start.30 = (bf16[40,1536]{1,0:T(8,128)(2,1)S(1)}, bf16[40,1536]{1,0:T(8,128)(2,1)S(1)}, u32[]{:S(2)}, u32[]{:S(2)}) collective-permute-start(bf16[40,1536]{1,0:T(8,128)(2,1)S(1)} %get-tuple-element.260), channel_id=1, source_target_pairs={{0,7},{1,6},{2,5},{3,4},{4,3},{5,2},{6,1},{7,0},{8,15},{9,14},{10,... | collective-permute-start | bytes 368648 | tf_op jit(solution)/shard_map/ppermute | solution.py:703
  137.6 16.1 %collective-permute-start.46 = (bf16[192,1536]{1,0:T(8,128)(2,1)S(1)}, bf16[192,1536]{1,0:T(8,128)(2,1)S(1)}, u32[]{:S(2)}, u32[]{:S(2)}) collective-permute-start(bf16[192,1536]{1,0:T(8,128)(2,1)S(1)} %get-tuple-element.217), channel_id=1, source_target_pairs={{0,2},{1,3},{2,0},{3,1},{4,6},{5,7},{6,4},{7,5},{8,10},{9,11},{10,... | collective-permute-start | bytes 1769480 | tf_op jit(solution)/shard_map/ppermute | solution.py:703
  193.3 14.7 %collective-permute-start.42 = (bf16[192,768]{1,0:T(8,128)(2,1)S(1)}, bf16[192,768]{1,0:T(8,128)(2,1)S(1)}, u32[]{:S(2)}, u32[]{:S(2)}) collective-permute-start(bf16[192,768]{1,0:T(8,128)(2,1)S(1)} %get-tuple-element.212.refs_1_), channel_id=1, source_target_pairs={{0,8},{8,0},{16,24},{24,16},{1,9},{9,1},{17,25},{25,17},{2,10},{10... | collective-permute-start | bytes 884744 | tf_op jit(solution)/shard_map/ppermute | solution.py:700
  194.5 13.6 %collective-permute-start.43 = (bf16[192,768]{1,0:T(8,128)(2,1)S(1)}, bf16[192,768]{1,0:T(8,128)(2,1)S(1)}, u32[]{:S(2)}, u32[]{:S(2)}) collective-permute-start(bf16[192,768]{1,0:T(8,128)(2,1)S(1)} %get-tuple-element.213.refs_3_), channel_id=1, source_target_pairs={{0,16},{8,24},{16,0},{24,8},{1,17},{9,25},{17,1},{25,9},{2,18},{10... | collective-permute-start | bytes 884744 | tf_op jit(solution)/shard_map/ppermute | solution.py:700
  201.2 13.4 %collective-permute-start.58 = (bf16[384,1536]{1,0:T(8,128)(2,1)S(1)}, bf16[384,1536]{1,0:T(8,128)(2,1)S(1)}, u32[]{:S(2)}, u32[]{:S(2)}) collective-permute-start(bf16[384,1536]{1,0:T(8,128)(2,1)S(1)} %shard_map.258.refs_1_), channel_id=1, source_target_pairs={{0,1},{1,0},{2,3},{3,2},{4,5},{5,4},{6,7},{7,6},{8,9},{9,8},{10,11... | collective-permute-start | bytes 3538952 | tf_op jit(solution)/shard_map/ppermute | solution.py:703
  (73 other events, 568.2 us)

commit v5 on v4

--- a/solution.py
+++ b/solution.py
@@ -74,10 +74,9 @@
 
 
 class Stored:
-    def __init__(self, target, buffer, semaphore):
-        self.buffer, self.copy = buffer, pltpu.make_async_copy(buffer, target, semaphore)
-        self.sent = False
-        self.dtype = buffer.dtype
+    def __init__(self, target, buffer, semaphores):
+        self.target, self.buffer, self.semaphores = target, buffer, semaphores
+        self.copies, self.sent, self.dtype = [], 0, buffer.dtype
 
     @property
     def shape(self):
@@ -89,10 +88,16 @@
     def __setitem__(self, index, value):
         self.buffer[index] = value
 
-    def send(self):
-        if not self.sent:
-            self.copy.start()
-            self.sent = True
+    def send(self, end=None):
+        end = self.shape[0] if end is None else end
+        if end > self.sent:
+            rows = pl.ds(self.sent, end - self.sent)
+            copy = pltpu.make_async_copy(
+                self.buffer.at[rows], self.target.at[rows], self.semaphores.at[len(self.copies)]
+            )
+            copy.start()
+            self.copies.append(copy)
+            self.sent = end
 
 
 def large(x):
@@ -119,7 +124,7 @@
         count = iter(range(len(moved)))
         later = []
         operands = [
-            Fetched(ref, next(buffers), semaphores.at[next(count)], later) if flag else ref
+            Fetched(ref, next(buffers), semaphores.at[next(count), 0], later) if flag else ref
             for ref, flag in zip(operands, large_in)
         ]
         fetched = [x for x in operands if isinstance(x, Fetched)]
@@ -139,14 +144,15 @@
                 x.send()
         for x in results:
             if isinstance(x, Stored):
-                x.copy.wait()
+                for copy in x.copies:
+                    copy.wait()
 
     def spec(flag):
         return pl.BlockSpec(memory_space=pl.ANY if flag else pltpu.VMEM)
 
     scratches = [pltpu.VMEM(x.shape, x.dtype) for x in moved]
     if moved:
-        scratches.append(pltpu.SemaphoreType.DMA((len(moved),)))
+        scratches.append(pltpu.SemaphoreType.DMA((len(moved), 2)))
     return pl.pallas_call(
         body,
         out_shape=tuple(outs),
@@ -391,10 +397,10 @@
     gain_attn,
     *refs,
 ):
-    returned, outs = refs[:-12], refs[-12:]
+    returned, outs = refs[:-10], refs[-10:]
     layer_output, input_grad, keep_1, send_1, keep_2, send_2, small_out = outs[:7]
     ride = keep_1.shape[0] > keep_2.shape[0]
-    small, grad_mixed_out, grad_value, grad_query, grad_key = outs[7:]
+    small, grad_mixed_out, grad_all = outs[7:]
     core = core_ref[0]
     length, width = residual_ref.shape
     scale = (width // heads) ** (-0.5)
@@ -462,25 +468,20 @@
             jnp.concatenate(grads, axis=0),
             jnp.concatenate([q2 * masks[0], q2 * masks[1]], axis=0),
         )
-        grad_value[:, at] = grad_v.astype(BF)
-        grad_query[:, at] = (grad_q * scale).astype(BF)
-        grad_key[:, at] = (grad_k * scale).astype(BF)
+        for i, grad in enumerate((grad_v, grad_q * scale, grad_k * scale)):
+            grad_all[:, i * width + at.start : i * width + at.stop] = grad.astype(BF)
     half = width // 2
     for h in (0, 1):
         at = slice(h * half, (h + 1) * half)
         left = mm_tn(mixed[:, at], grad_attn).astype(BF)
-        right = mm_tn(normed_one[:, at], grad_value[...]).astype(BF)
-        store_halves(core, h, left, right, keep_1, send_1)
-    for h in (0, 1):
-        at = slice(h * half, (h + 1) * half)
-        left = mm_tn(normed_one[:, at], grad_query[...]).astype(BF)
-        right = mm_tn(normed_one[:, at], grad_key[...]).astype(BF)
-        store_halves(core, h, left, right, keep_2, send_2)
-    send_2.send()
-    keep_2.send()
-    grad_one = mm_nt(grad_value[...], w_value[...])
-    grad_one = grad_one + mm_nt(grad_query[...], w_query[...])
-    grad_one = grad_one + mm_nt(grad_key[...], w_key[...])
+        right = mm_tn(normed_one[:, at], grad_all[...]).astype(BF)
+        store_halves(core, h, left, right[:, :width], keep_1, send_1)
+        store_halves(core, h, right[:, width : 2 * width], right[:, 2 * width :], keep_2, send_2)
+    for out in (send_1, keep_1, send_2, keep_2):
+        out.send(half)
+    grad_one = mm_nt(grad_all[:, :width], w_value[...])
+    grad_one = grad_one + mm_nt(grad_all[:, width : 2 * width], w_query[...])
+    grad_one = grad_one + mm_nt(grad_all[:, 2 * width :], w_key[...])
     inputs = tokens[...].astype(F32)
     scale_one = rms_scale(inputs)
     small[0:1, :] = jnp.sum(grad_one * inputs * scale_one, axis=0, keepdims=True)
@@ -874,7 +875,7 @@
         *returned,
         smem=1,
         early=4,
-        scratch=[pltpu.VMEM((small_rows, width), F32)] + [pltpu.VMEM((length, width), BF)] * 4,
+        scratch=[pltpu.VMEM((small_rows, width), F32)] + [pltpu.VMEM((length, width), BF), pltpu.VMEM((length, 3 * width), BF)],
         flops=16 * length * width * width + 3 * attn_flops,
     )
 

time: 218 us -> 217 us (level)
  transfers between devices with their start and end apart: 59 -> 59, of which waited for: 28 -> 26; matrix products, arithmetic and copies ran while one was open for 1% -> 1% of each run, Pallas kernels for 16% -> 17%
where the time goes in v5:
time: 217 us
  starting transfers between devices  78.4 us (36%)
  Pallas kernels  65.9 us (30%)
  waiting for transfers between devices  64.1 us (30%)
  local copies, waits for them, and re-layouts  5.12 us (2%)
    pallas_call x22, Pallas kernels, call(): pl.pallas_call(body, out_shape=tuple(outs), in_specs=[pl.BlockSpec(memory...  60.3 us
    ppermute x23, starting transfers between devices, along(): return lax.ppermute(x, 'wide', pairs(n_wide, k))  45.5 us
    ppermute x36, waiting for transfers between devices, across(): return lax.ppermute(x, 'narrow', pairs(n_narrow, k))  33.3 us
    ppermute x36, starting transfers between devices, across(): return lax.ppermute(x, 'narrow', pairs(n_narrow, k))  32.9 us
    ppermute x23, waiting for transfers between devices, along(): return lax.ppermute(x, 'wide', pairs(n_wide, k))  30.8 us
    pallas_call x2, Pallas kernels, finish(): pl.pallas_call(functools.partial(finish_kernel, bool(outs), len(sources))...  5.66 us
  transfers between devices with their start and end apart: 59, of which 26 were waited for; matrix products, arithmetic and copies ran while one was open for 1% of the time, Pallas kernels for 17%

profile of v5, /device:TPU:1, one launch (start us, length us, event | category | flops | bytes accessed | tf_op | source)
XLA Modules:
  0.0 216.7 jit_solution(8928600304075978353)
XLA Ops:
  0.6 11.3 %shard_map.238 = (bf16[256,768]{1,0:T(8,128)(2,1)}, bf16[256,768]{1,0:T(8,128)(2,1)}, bf16[256,768]{1,0:T(8,128)(2,1)}, bf16[256,768]{1,0:T(8,128)(2,1)}, bf16[1...) custom-call(s32[1]{0:T(128)} %bitcast.1.refs_0_, ...), custom_call_target="tpu_custom_call" | custom-call | flops 1409286144 | bytes 11246112 | tf_op jit(solution)/shard_map/pallas_call | solution.py:156
  15.1 2.5 %collective-permute-start.1 = (bf16[80,1536]{1,0:T(8,128)(2,1)S(1)}, bf16[80,1536]{1,0:T(8,128)(2,1)S(1)}, u32[]{:S(2)}, u32[]{:S(2)}) collective-permute-start(bf16[80,1536]{1,0:T(8,128)(2,1)S(1)} %pad_maximum_fusion), channel_id=1, source_target_pairs={{0,2},{1,3},{2,0},{3,1},{4,6},{5,7},{6,4},{7,5},{8,10},{9,11},{10,... | collective-permute-start | bytes 737288 | tf_op jit(solution)/shard_map/ppermute | solution.py:704
  17.6 2.4 %collective-permute-start.3 = (bf16[80,1536]{1,0:T(8,128)(2,1)S(1)}, bf16[80,1536]{1,0:T(8,128)(2,1)S(1)}, u32[]{:S(2)}, u32[]{:S(2)}) collective-permute-start(bf16[80,1536]{1,0:T(8,128)(2,1)S(1)} %pad_maximum_fusion.2), channel_id=1, source_target_pairs={{0,4},{1,5},{2,6},{3,7},{4,0},{5,1},{6,2},{7,3},{8,12},{9,13},{10,... | collective-permute-start | bytes 737288 | tf_op jit(solution)/shard_map/ppermute | solution.py:704
  22.6 5.2 %collective-permute-done.3.refs_2_.refs_1_ = bf16[80,1536]{1,0:T(8,128)(2,1)S(1)} collective-permute-done((bf16[80,1536]{1,0:T(8,128)(2,1)S(1)}, bf16[80,1536]{1,0:T(8,128)(2,1)S(1)}, u32[]{:S(2)}, u32[]{:S(2)}) %collective-permute-start.3) | collective-permute-done | bytes 245792 | tf_op jit(solution)/shard_map/ppermute | solution.py:704
  30.6 5.5 %collective-permute-done.2.refs_2_.refs_9_ = bf16[80,1536]{1,0:T(8,128)(2,1)S(1)} collective-permute-done((bf16[80,1536]{1,0:T(8,128)(2,1)S(1)}, bf16[80,1536]{1,0:T(8,128)(2,1)S(1)}, u32[]{:S(2)}, u32[]{:S(2)}) %collective-permute-start.2) | collective-permute-done | bytes 245792 | tf_op jit(solution)/shard_map/ppermute | solution.py:704
  43.7 2.7 %collective-permute-done.15.refs_9_.refs_7_ = bf16[80,1536]{1,0:T(8,128)(2,1)S(1)} collective-permute-done((bf16[80,1536]{1,0:T(8,128)(2,1)S(1)}, bf16[80,1536]{1,0:T(8,128)(2,1)S(1)}, u32[]{:S(2)}, u32[]{:S(2)}) %collective-permute-start.15) | collective-permute-done | bytes 245792 | tf_op jit(solution)/shard_map/ppermute | solution.py:701
  47.1 7.3 %shard_map.240 = (bf16[320,768]{1,0:T(8,128)(2,1)}, bf16[320,768]{1,0:T(8,128)(2,1)}, bf16[320,768]{1,0:T(8,128)(2,1)}, bf16[320,768]{1,0:T(8,128)(2,1)}, bf16[8...) custom-call(bf16[768,768]{1,0:T(8,128)(2,1)} %bitcast.53, ...), custom_call_target="tpu_custom_call" | custom-call | flops 3019898880 | bytes 8257536 | tf_op jit(solution)/shard_map/pallas_call | solution.py:156
  58.5 7.5 %shard_map.239 = (bf16[320,768]{1,0:T(8,128)(2,1)}, bf16[320,768]{1,0:T(8,128)(2,1)}, bf16[320,768]{1,0:T(8,128)(2,1)}, bf16[320,768]{1,0:T(8,128)(2,1)}, bf16[8...) custom-call(bf16[768,768]{1,0:T(8,128)(2,1)} %bitcast.54, ...), custom_call_target="tpu_custom_call" | custom-call | flops 3019898880 | bytes 8257536 | tf_op jit(solution)/shard_map/pallas_call | solution.py:156
  70.8 4.9 %collective-permute-done.18 = bf16[80,1536]{1,0:T(8,128)(2,1)S(1)} collective-permute-done((bf16[80,1536]{1,0:T(8,128)(2,1)S(1)}, bf16[80,1536]{1,0:T(8,128)(2,1)S(1)}, u32[]{:S(2)}, u32[]{:S(2)}) %collective-permute-start.18) | collective-permute-done | bytes 245792 | tf_op jit(solution)/shard_map/ppermute | solution.py:701
  76.5 12.3 %collective-permute-start.27 = (bf16[40,1536]{1,0:T(8,128)(2,1)S(1)}, bf16[40,1536]{1,0:T(8,128)(2,1)S(1)}, u32[]{:S(2)}, u32[]{:S(2)}) collective-permute-start(bf16[40,1536]{1,0:T(8,128)(2,1)S(1)} %get-tuple-element.266), channel_id=1, source_target_pairs={{0,1},{1,0},{2,3},{3,2},{4,5},{5,4},{6,7},{7,6},{8,9},{9,8},{10,11... | collective-permute-start | bytes 368648 | tf_op jit(solution)/shard_map/ppermute | solution.py:704
  89.0 3.0 %collective-permute-start.23 = (bf16[40,1536]{1,0:T(8,128)(2,1)S(1)}, bf16[40,1536]{1,0:T(8,128)(2,1)S(1)}, u32[]{:S(2)}, u32[]{:S(2)}) collective-permute-start(bf16[40,1536]{1,0:T(8,128)(2,1)S(1)} %get-tuple-element.263), channel_id=1, source_target_pairs={{0,4},{1,5},{2,6},{3,7},{4,0},{5,1},{6,2},{7,3},{8,12},{9,13},{10,... | collective-permute-start | bytes 368648 | tf_op jit(solution)/shard_map/ppermute | solution.py:704
  92.8 4.7 %collective-permute-done.20 = bf16[80,1536]{1,0:T(8,128)(2,1)S(1)} collective-permute-done((bf16[80,1536]{1,0:T(8,128)(2,1)S(1)}, bf16[80,1536]{1,0:T(8,128)(2,1)S(1)}, u32[]{:S(2)}, u32[]{:S(2)}) %collective-permute-start.20) | collective-permute-done | bytes 245792 | tf_op jit(solution)/shard_map/ppermute | solution.py:701
  97.6 3.9 %collective-permute-start.28 = (bf16[40,1536]{1,0:T(8,128)(2,1)S(1)}, bf16[40,1536]{1,0:T(8,128)(2,1)S(1)}, u32[]{:S(2)}, u32[]{:S(2)}) collective-permute-start(bf16[40,1536]{1,0:T(8,128)(2,1)S(1)} %get-tuple-element.264), channel_id=1, source_target_pairs={{0,3},{1,2},{2,1},{3,0},{4,7},{5,6},{6,5},{7,4},{8,11},{9,10},{10,... | collective-permute-start | bytes 368648 | tf_op jit(solution)/shard_map/ppermute | solution.py:704
  106.4 8.5 %shard_map.241 = (f32[1,768,768]{2,1,0:T(8,128)}, f32[1,768,768]{2,1,0:T(8,128)}) custom-call(bf16[80,1536]{1,0:T(8,128)(2,1)} %copy-done.2, bf16[80,1536]{1,0:T(8,128)(2,1)} %copy-done.24, bf16[80,1536]{1,0:T(8,128)(2,1)} %copy-done.25, bf16[80,1536]{1,0:T(8,128)(2,1)} %copy-done.28, bf16[80,1536]{1,0:T(8,128)(2,1)} %copy-done.26, ...), custom_call_target="tpu_custom_call" | custom-call | flops 3019898880 | bytes 12582912 | tf_op jit(solution)/shard_map/pallas_call | solution.py:156
  115.7 15.3 %shard_map.242 = (bf16[256,768]{1,0:T(8,128)(2,1)}, bf16[256,768]{1,0:T(8,128)(2,1)}, bf16[400,1536]{1,0:T(8,128)(2,1)}, bf16[400,1536]{1,0:T(8,128)(2,1)}, bf16...) custom-call(s32[1]{0:T(128)} %bitcast.refs_0_, f32[16,256]{1,0:T(8,128)} %get-tuple-element.134.refs_1_, ...), custom_call_target="tpu_custom_call" | custom-call | flops 3019898880 | bytes 16850944 | tf_op jit(solution)/shard_map/pallas_call | solution.py:156
  131.8 3.5 %collective-permute-done.45.refs_2_ = bf16[384,1536]{1,0:T(8,128)(2,1)} collective-permute-done((bf16[384,1536]{1,0:T(8,128)(2,1)}, bf16[384,1536]{1,0:T(8,128)(2,1)}, u32[]{:S(2)}, u32[]{:S(2)}) %collective-permute-start.45) | collective-permute-done | bytes 1179680 | tf_op jit(solution)/shard_map/ppermute | solution.py:704
  142.1 6.6 %collective-permute-done.33.refs_4_ = bf16[192,768]{1,0:T(8,128)(2,1)S(1)} collective-permute-done((bf16[192,768]{1,0:T(8,128)(2,1)S(1)}, bf16[192,768]{1,0:T(8,128)(2,1)S(1)}, u32[]{:S(2)}, u32[]{:S(2)}) %collective-permute-start.33) | collective-permute-done | bytes 294944 | tf_op jit(solution)/shard_map/ppermute | solution.py:701
  157.2 2.6 %collective-permute-done.47.refs_2_ = bf16[96,768]{1,0:T(8,128)(2,1)S(1)} collective-permute-done((bf16[96,768]{1,0:T(8,128)(2,1)S(1)}, bf16[96,768]{1,0:T(8,128)(2,1)S(1)}, u32[]{:S(2)}, u32[]{:S(2)}) %collective-permute-start.47) | collective-permute-done | bytes 147488 | tf_op jit(solution)/shard_map/ppermute | solution.py:701
  170.8 5.8 %collective-permute-done.37.refs_1_ = bf16[80,768]{1,0:T(8,128)(2,1)S(1)} collective-permute-done((bf16[80,768]{1,0:T(8,128)(2,1)S(1)}, bf16[80,768]{1,0:T(8,128)(2,1)S(1)}, u32[]{:S(2)}, u32[]{:S(2)}) %collective-permute-start.37) | collective-permute-done | bytes 122912 | tf_op jit(solution)/shard_map/ppermute | solution.py:704
  179.8 2.8 %collective-permute-done.38.refs_2_ = bf16[48,768]{1,0:T(8,128)(2,1)S(1)} collective-permute-done((bf16[48,768]{1,0:T(8,128)(2,1)S(1)}, bf16[48,768]{1,0:T(8,128)(2,1)S(1)}, u32[]{:S(2)}, u32[]{:S(2)}) %collective-permute-start.38) | collective-permute-done | bytes 73760 | tf_op jit(solution)/shard_map/ppermute | solution.py:704
  200.3 6.8 %collective-permute-start.58 = (bf16[384,1536]{1,0:T(8,128)(2,1)S(1)}, bf16[384,1536]{1,0:T(8,128)(2,1)S(1)}, u32[]{:S(2)}, u32[]{:S(2)}) collective-permute-start(bf16[384,1536]{1,0:T(8,128)(2,1)S(1)} %shard_map.258.refs_1_), channel_id=1, source_target_pairs={{0,1},{1,0},{2,3},{3,2},{4,5},{5,4},{6,7},{7,6},{8,9},{9,8},{10,11... | collective-permute-start | bytes 3538952 | tf_op jit(solution)/shard_map/ppermute | solution.py:704
  207.7 2.5 %collective-permute-start.44 = (bf16[384,1536]{1,0:T(8,128)(2,1)S(1)}, bf16[384,1536]{1,0:T(8,128)(2,1)S(1)}, u32[]{:S(2)}, u32[]{:S(2)}) collective-permute-start(bf16[384,1536]{1,0:T(8,128)(2,1)S(1)} %shard_map.250.refs_0_), channel_id=1, source_target_pairs={{0,1},{1,0},{2,3},{3,2},{4,5},{5,4},{6,7},{7,6},{8,9},{9,8},{10,11... | collective-permute-start | bytes 3538952 | tf_op jit(solution)/shard_map/ppermute | solution.py:704
  210.9 2.8 %shard_map.259 = (f32[768,768]{1,0:T(8,128)}, f32[768,768]{1,0:T(8,128)}, f32[768,768]{1,0:T(8,128)}, f32[768,768]{1,0:T(8,128)}) custom-call(s32[5]{0:T(128)S(1)} %stack.20.refs_0_.place_ref, bf16[384,1536]{1,0:T(8,128)(2,1)S(1)} %shard_map.250.refs_0_, bf16[384,1536]{1,0:T(8,128)(2,1)S(1)} %shard_map.258.refs_1_), custom_call_target="tpu_custom_call" | custom-call | tf_op jit(solution)/shard_map/pallas_call | solution.py:977
  213.7 2.8 %shard_map.261 = (f32[768,768]{1,0:T(8,128)}, f32[768,768]{1,0:T(8,128)}, f32[768,768]{1,0:T(8,128)}, f32[768,768]{1,0:T(8,128)}) custom-call(s32[5]{0:T(128)S(1)} %stack.20.refs_0_.place_ref, bf16[384,1536]{1,0:T(8,128)(2,1)S(1)} %collective-permute-done.44.refs_0_, ...), custom_call_target="tpu_custom_call", output_to_operand_aliasing={{0}: (3, {}), {1}: (4, {}), {2}: (5, {}), {3}: (6, {})} | custom-call | tf_op jit(solution)/shard_map/pallas_call | solution.py:977
  (214 shorter events, 82.0 us)
Async XLA Ops:
  15.1 14.0 %collective-permute-start.1 = (bf16[80,1536]{1,0:T(8,128)(2,1)S(1)}, bf16[80,1536]{1,0:T(8,128)(2,1)S(1)}, u32[]{:S(2)}, u32[]{:S(2)}) collective-permute-start(bf16[80,1536]{1,0:T(8,128)(2,1)S(1)} %pad_maximum_fusion), channel_id=1, source_target_pairs={{0,2},{1,3},{2,0},{3,1},{4,6},{5,7},{6,4},{7,5},{8,10},{9,11},{10,... | collective-permute-start | bytes 737288 | tf_op jit(solution)/shard_map/ppermute | solution.py:704
  17.6 10.3 %collective-permute-start.3 = (bf16[80,1536]{1,0:T(8,128)(2,1)S(1)}, bf16[80,1536]{1,0:T(8,128)(2,1)S(1)}, u32[]{:S(2)}, u32[]{:S(2)}) collective-permute-start(bf16[80,1536]{1,0:T(8,128)(2,1)S(1)} %pad_maximum_fusion.2), channel_id=1, source_target_pairs={{0,4},{1,5},{2,6},{3,7},{4,0},{5,1},{6,2},{7,3},{8,12},{9,13},{10,... | collective-permute-start | bytes 737288 | tf_op jit(solution)/shard_map/ppermute | solution.py:704
  20.0 10.3 %collective-permute-start.12 = (bf16[80,1536]{1,0:T(8,128)(2,1)S(1)}, bf16[80,1536]{1,0:T(8,128)(2,1)S(1)}, u32[]{:S(2)}, u32[]{:S(2)}) collective-permute-start(bf16[80,1536]{1,0:T(8,128)(2,1)S(1)} %pad_maximum_fusion.3.refs_1_.refs_0_), channel_id=1, source_target_pairs={{0,8},{8,0},{16,24},{24,16},{1,9},{9,1},{17,25},{25,17},{2,10},{10... | collective-permute-start | bytes 737288 | tf_op jit(solution)/shard_map/ppermute | solution.py:701
  21.3 14.8 %collective-permute-start.5 = (bf16[80,1536]{1,0:T(8,128)(2,1)S(1)}, bf16[80,1536]{1,0:T(8,128)(2,1)S(1)}, u32[]{:S(2)}, u32[]{:S(2)}) collective-permute-start(bf16[80,1536]{1,0:T(8,128)(2,1)S(1)} %pad_maximum_fusion.3.refs_1_.refs_0_), channel_id=1, source_target_pairs={{0,16},{8,24},{16,0},{24,8},{1,17},{9,25},{17,1},{25,9},{2,18},{10... | collective-permute-start | bytes 737288 | tf_op jit(solution)/shard_map/ppermute | solution.py:701
  22.6 13.5 %collective-permute-start.2 = (bf16[80,1536]{1,0:T(8,128)(2,1)S(1)}, bf16[80,1536]{1,0:T(8,128)(2,1)S(1)}, u32[]{:S(2)}, u32[]{:S(2)}) collective-permute-start(bf16[80,1536]{1,0:T(8,128)(2,1)S(1)} %pad_maximum_fusion.1), channel_id=1, source_target_pairs={{0,6},{1,7},{2,4},{3,5},{4,2},{5,3},{6,0},{7,1},{8,14},{9,15},{10,... | collective-permute-start | bytes 737288 | tf_op jit(solution)/shard_map/ppermute | solution.py:704
  38.9 16.8 %collective-permute-start.8 = (bf16[80,1536]{1,0:T(8,128)(2,1)S(1)}, bf16[80,1536]{1,0:T(8,128)(2,1)S(1)}, u32[]{:S(2)}, u32[]{:S(2)}) collective-permute-start(bf16[80,1536]{1,0:T(8,128)(2,1)S(1)} %collective-permute-done.1.refs_1_.refs_8_), channel_id=1, source_target_pairs={{0,16},{8,24},{16,0},{24,8},{1,17},{9,25},{17,1},{25,9},{2,18},{10... | collective-permute-start | bytes 737288 | tf_op jit(solution)/shard_map/ppermute | solution.py:701
  39.1 17.9 %collective-permute-start.7 = (bf16[80,1536]{1,0:T(8,128)(2,1)S(1)}, bf16[80,1536]{1,0:T(8,128)(2,1)S(1)}, u32[]{:S(2)}, u32[]{:S(2)}) collective-permute-start(bf16[80,1536]{1,0:T(8,128)(2,1)S(1)} %collective-permute-done.2.refs_2_.refs_9_), channel_id=1, source_target_pairs={{0,8},{8,0},{16,24},{24,16},{1,9},{9,1},{17,25},{25,17},{2,10},{10... | collective-permute-start | bytes 737288 | tf_op jit(solution)/shard_map/ppermute | solution.py:701
  41.2 15.8 %collective-permute-start.10 = (bf16[80,1536]{1,0:T(8,128)(2,1)S(1)}, bf16[80,1536]{1,0:T(8,128)(2,1)S(1)}, u32[]{:S(2)}, u32[]{:S(2)}) collective-permute-start(bf16[80,1536]{1,0:T(8,128)(2,1)S(1)} %collective-permute-done.6.refs_3_.refs_10_), channel_id=1, source_target_pairs={{0,16},{8,24},{16,0},{24,8},{1,17},{9,25},{17,1},{25,9},{2,18},{10... | collective-permute-start | bytes 737288 | tf_op jit(solution)/shard_map/ppermute | solution.py:701
  42.7 14.3 %collective-permute-start.11 = (bf16[80,1536]{1,0:T(8,128)(2,1)S(1)}, bf16[80,1536]{1,0:T(8,128)(2,1)S(1)}, u32[]{:S(2)}, u32[]{:S(2)}) collective-permute-start(bf16[80,1536]{1,0:T(8,128)(2,1)S(1)} %collective-permute-done.9.refs_7_.refs_13_), channel_id=1, source_target_pairs={{0,8},{8,0},{16,24},{24,16},{1,9},{9,1},{17,25},{25,17},{2,10},{10... | collective-permute-start | bytes 737288 | tf_op jit(solution)/shard_map/ppermute | solution.py:701
  54.4 13.2 %collective-permute-start.16 = (bf16[2,80,1536]{2,1,0:T(8,128)(2,1)}, bf16[2,80,1536]{2,1,0:T(8,128)(2,1)S(1)}, u32[]{:S(2)}, u32[]{:S(2)}) collective-permute-start(bf16[2,80,1536]{2,1,0:T(8,128)(2,1)} %get-tuple-element.164), channel_id=1, source_target_pairs={{0,8},{8,0},{16,24},{24,16},{1,9},{9,1},{17,25},{25,17},{2,10},{10... | collective-permute-start | bytes 1474568 | tf_op jit(solution)/shard_map/ppermute | solution.py:701
  55.7 12.0 %collective-permute-start.17 = (bf16[2,80,1536]{2,1,0:T(8,128)(2,1)}, bf16[2,80,1536]{2,1,0:T(8,128)(2,1)S(1)}, u32[]{:S(2)}, u32[]{:S(2)}) collective-permute-start(bf16[2,80,1536]{2,1,0:T(8,128)(2,1)} %get-tuple-element.165), channel_id=1, source_target_pairs={{0,16},{8,24},{16,0},{24,8},{1,17},{9,25},{17,1},{25,9},{2,18},{10... | collective-permute-start | bytes 1474568 | tf_op jit(solution)/shard_map/ppermute | solution.py:701
  69.1 19.6 %collective-permute-start.22 = (bf16[80,1536]{1,0:T(8,128)(2,1)S(1)}, bf16[80,1536]{1,0:T(8,128)(2,1)S(1)}, u32[]{:S(2)}, u32[]{:S(2)}) collective-permute-start(bf16[80,1536]{1,0:T(8,128)(2,1)S(1)} %fusion.10), channel_id=1, source_target_pairs={{0,8},{8,0},{16,24},{24,16},{1,9},{9,1},{17,25},{25,17},{2,10},{10... | collective-permute-start | bytes 737288 | tf_op jit(solution)/shard_map/ppermute | solution.py:701
  70.3 21.6 %collective-permute-start.19 = (bf16[2,80,1536]{2,1,0:T(8,128)(2,1)S(1)}, bf16[2,80,1536]{2,1,0:T(8,128)(2,1)S(1)}, u32[]{:S(2)}, u32[]{:S(2)}) collective-permute-start(bf16[2,80,1536]{2,1,0:T(8,128)(2,1)S(1)} %copy-done.22), channel_id=1, source_target_pairs={{0,8},{8,0},{16,24},{24,16},{1,9},{9,1},{17,25},{25,17},{2,10},{10... | collective-permute-start | bytes 1474568 | tf_op jit(solution)/shard_map/ppermute | solution.py:701
  70.6 22.0 %collective-permute-start.24 = (bf16[2,80,1536]{2,1,0:T(8,128)(2,1)S(1)}, bf16[2,80,1536]{2,1,0:T(8,128)(2,1)S(1)}, u32[]{:S(2)}, u32[]{:S(2)}) collective-permute-start(bf16[2,80,1536]{2,1,0:T(8,128)(2,1)S(1)} %copy-done.21), channel_id=1, source_target_pairs={{0,16},{8,24},{16,0},{24,8},{1,17},{9,25},{17,1},{25,9},{2,18},{10... | collective-permute-start | bytes 1474568 | tf_op jit(solution)/shard_map/ppermute | solution.py:701
  76.5 26.3 %collective-permute-start.27 = (bf16[40,1536]{1,0:T(8,128)(2,1)S(1)}, bf16[40,1536]{1,0:T(8,128)(2,1)S(1)}, u32[]{:S(2)}, u32[]{:S(2)}) collective-permute-start(bf16[40,1536]{1,0:T(8,128)(2,1)S(1)} %get-tuple-element.266), channel_id=1, source_target_pairs={{0,1},{1,0},{2,3},{3,2},{4,5},{5,4},{6,7},{7,6},{8,9},{9,8},{10,11... | collective-permute-start | bytes 368648 | tf_op jit(solution)/shard_map/ppermute | solution.py:704
  88.9 15.8 %collective-permute-start.29 = (bf16[40,1536]{1,0:T(8,128)(2,1)S(1)}, bf16[40,1536]{1,0:T(8,128)(2,1)S(1)}, u32[]{:S(2)}, u32[]{:S(2)}) collective-permute-start(bf16[40,1536]{1,0:T(8,128)(2,1)S(1)} %get-tuple-element.262), channel_id=1, source_target_pairs={{0,5},{1,4},{2,7},{3,6},{4,1},{5,0},{6,3},{7,2},{8,13},{9,12},{10,... | collective-permute-start | bytes 368648 | tf_op jit(solution)/shard_map/ppermute | solution.py:704
  89.0 25.9 %collective-permute-start.23 = (bf16[40,1536]{1,0:T(8,128)(2,1)S(1)}, bf16[40,1536]{1,0:T(8,128)(2,1)S(1)}, u32[]{:S(2)}, u32[]{:S(2)}) collective-permute-start(bf16[40,1536]{1,0:T(8,128)(2,1)S(1)} %get-tuple-element.263), channel_id=1, source_target_pairs={{0,4},{1,5},{2,6},{3,7},{4,0},{5,1},{6,2},{7,3},{8,12},{9,13},{10,... | collective-permute-start | bytes 368648 | tf_op jit(solution)/shard_map/ppermute | solution.py:704
  97.6 17.3 %collective-permute-start.28 = (bf16[40,1536]{1,0:T(8,128)(2,1)S(1)}, bf16[40,1536]{1,0:T(8,128)(2,1)S(1)}, u32[]{:S(2)}, u32[]{:S(2)}) collective-permute-start(bf16[40,1536]{1,0:T(8,128)(2,1)S(1)} %get-tuple-element.264), channel_id=1, source_target_pairs={{0,3},{1,2},{2,1},{3,0},{4,7},{5,6},{6,5},{7,4},{8,11},{9,10},{10,... | collective-permute-start | bytes 368648 | tf_op jit(solution)/shard_map/ppermute | solution.py:704
  101.4 13.5 %collective-permute-start.21 = (bf16[40,1536]{1,0:T(8,128)(2,1)S(1)}, bf16[40,1536]{1,0:T(8,128)(2,1)S(1)}, u32[]{:S(2)}, u32[]{:S(2)}) collective-permute-start(bf16[40,1536]{1,0:T(8,128)(2,1)S(1)} %get-tuple-element.265), channel_id=1, source_target_pairs={{0,2},{1,3},{2,0},{3,1},{4,6},{5,7},{6,4},{7,5},{8,10},{9,11},{10,... | collective-permute-start | bytes 368648 | tf_op jit(solution)/shard_map/ppermute | solution.py:704
  102.8 12.1 %collective-permute-start.30 = (bf16[40,1536]{1,0:T(8,128)(2,1)S(1)}, bf16[40,1536]{1,0:T(8,128)(2,1)S(1)}, u32[]{:S(2)}, u32[]{:S(2)}) collective-permute-start(bf16[40,1536]{1,0:T(8,128)(2,1)S(1)} %get-tuple-element.260), channel_id=1, source_target_pairs={{0,7},{1,6},{2,5},{3,4},{4,3},{5,2},{6,1},{7,0},{8,15},{9,14},{10,... | collective-permute-start | bytes 368648 | tf_op jit(solution)/shard_map/ppermute | solution.py:704
  138.1 15.1 %collective-permute-start.46 = (bf16[192,1536]{1,0:T(8,128)(2,1)S(1)}, bf16[192,1536]{1,0:T(8,128)(2,1)S(1)}, u32[]{:S(2)}, u32[]{:S(2)}) collective-permute-start(bf16[192,1536]{1,0:T(8,128)(2,1)S(1)} %get-tuple-element.217), channel_id=1, source_target_pairs={{0,2},{1,3},{2,0},{3,1},{4,6},{5,7},{6,4},{7,5},{8,10},{9,11},{10,... | collective-permute-start | bytes 1769480 | tf_op jit(solution)/shard_map/ppermute | solution.py:704
  193.4 13.7 %collective-permute-start.42 = (bf16[192,768]{1,0:T(8,128)(2,1)S(1)}, bf16[192,768]{1,0:T(8,128)(2,1)S(1)}, u32[]{:S(2)}, u32[]{:S(2)}) collective-permute-start(bf16[192,768]{1,0:T(8,128)(2,1)S(1)} %get-tuple-element.212.refs_1_), channel_id=1, source_target_pairs={{0,8},{8,0},{16,24},{24,16},{1,9},{9,1},{17,25},{25,17},{2,10},{10... | collective-permute-start | bytes 884744 | tf_op jit(solution)/shard_map/ppermute | solution.py:701
  194.4 12.6 %collective-permute-start.43 = (bf16[192,768]{1,0:T(8,128)(2,1)S(1)}, bf16[192,768]{1,0:T(8,128)(2,1)S(1)}, u32[]{:S(2)}, u32[]{:S(2)}) collective-permute-start(bf16[192,768]{1,0:T(8,128)(2,1)S(1)} %get-tuple-element.213.refs_3_), channel_id=1, source_target_pairs={{0,16},{8,24},{16,0},{24,8},{1,17},{9,25},{17,1},{25,9},{2,18},{10... | collective-permute-start | bytes 884744 | tf_op jit(solution)/shard_map/ppermute | solution.py:701
  200.3 13.4 %collective-permute-start.58 = (bf16[384,1536]{1,0:T(8,128)(2,1)S(1)}, bf16[384,1536]{1,0:T(8,128)(2,1)S(1)}, u32[]{:S(2)}, u32[]{:S(2)}) collective-permute-start(bf16[384,1536]{1,0:T(8,128)(2,1)S(1)} %shard_map.258.refs_1_), channel_id=1, source_target_pairs={{0,1},{1,0},{2,3},{3,2},{4,5},{5,4},{6,7},{7,6},{8,9},{9,8},{10,11... | collective-permute-start | bytes 3538952 | tf_op jit(solution)/shard_map/ppermute | solution.py:704
  (73 other events, 569.6 us)

commit v6 on v5

--- a/solution.py
+++ b/solution.py
@@ -198,14 +198,12 @@
     buckets,
     choices,
     levels,
-    normed_one_out,
     query_out,
     key_out,
     value_out,
     probs_out,
     mixed_out,
     residual_out,
-    normed_two_out,
     packed_out,
     *slots_out,
 ):
@@ -215,8 +213,6 @@
     flat_slots = sum(out.shape[0] for out in slots_out)
     inputs = tokens[...].astype(F32)
     normed = (inputs * rms_scale(inputs) * as_row(gain_attn)).astype(BF)
-    normed_one_out[...] = normed
-    normed_one_out.send()
     query_out[...] = mm(normed, w_query[...]).astype(BF)
     key_out[...] = mm(normed, w_key[...]).astype(BF)
     value_out[...] = mm(normed, w_value[...]).astype(BF)
@@ -258,8 +254,6 @@
     residual_out[...] = residual
     residual_out.send()
     normed_two = (residual * rms_scale(residual) * as_row(gain_ffn)).astype(BF)
-    normed_two_out[...] = normed_two
-    normed_two_out.send()
     logits = mm_nt(w_router[...], normed_two) + 0.25 * as_column(levels).astype(F32)
     logit_exp = jnp.exp(logits - jnp.max(logits, axis=0, keepdims=True))
     router = logit_exp / jnp.sum(logit_exp, axis=0, keepdims=True)
@@ -385,15 +379,13 @@
     w_output,
     value,
     probs_ref,
-    normed_two,
     key,
     query,
     mixed,
-    normed_one,
+    tokens,
     w_value,
     w_query,
     w_key,
-    tokens,
     gain_attn,
     *refs,
 ):
@@ -441,7 +433,8 @@
     small[1:2, :] = jnp.sum(grad_two * residual * scale_two, axis=0, keepdims=True)
     grad_attn = grad_residual.astype(BF)
     grad_mixed_out[...] = mm_nt(grad_attn, w_output[...]).astype(BF)
-    small[2 : 2 + experts, :] = mm_tn(grad_logits, normed_two[...])
+    normed_two = (residual * scale_two * as_row(gain_ffn)).astype(BF)
+    small[2 : 2 + experts, :] = mm_tn(grad_logits, normed_two)
     pair = 2 * width // heads
     masks = half_masks(length, pair)
     sums = []
@@ -470,6 +463,9 @@
         )
         for i, grad in enumerate((grad_v, grad_q * scale, grad_k * scale)):
             grad_all[:, i * width + at.start : i * width + at.stop] = grad.astype(BF)
+    inputs = tokens[...].astype(F32)
+    scale_one = rms_scale(inputs)
+    normed_one = (inputs * scale_one * as_row(gain_attn)).astype(BF)
     half = width // 2
     for h in (0, 1):
         at = slice(h * half, (h + 1) * half)
@@ -482,8 +478,6 @@
     grad_one = mm_nt(grad_all[:, :width], w_value[...])
     grad_one = grad_one + mm_nt(grad_all[:, width : 2 * width], w_query[...])
     grad_one = grad_one + mm_nt(grad_all[:, 2 * width :], w_key[...])
-    inputs = tokens[...].astype(F32)
-    scale_one = rms_scale(inputs)
     small[0:1, :] = jnp.sum(grad_one * inputs * scale_one, axis=0, keepdims=True)
     weighted = grad_one * as_row(gain_attn)
     input_grad[...] = (
@@ -704,14 +698,12 @@
         return lax.ppermute(x, "wide", pairs(n_wide, k))
 
     (
-        normed_one,
         query,
         key,
         value,
         probs,
         mixed,
         residual,
-        normed_two,
         packed,
         *slots,
     ) = call(
@@ -720,11 +712,9 @@
             rows_bf,
             rows_bf,
             rows_bf,
-            rows_bf,
             shaped((heads, length, length)),
             rows_bf,
             shaped((length, width), F32),
-            rows_bf,
             shaped((8 + experts, length), F32),
         ]
         + [shaped((n, 2 * width)) for n in slot_counts],
@@ -862,15 +852,13 @@
         w_output,
         value,
         probs,
-        normed_two,
         key,
         query,
         mixed,
-        normed_one,
+        tokens,
         w_value,
         w_query,
         w_key,
-        tokens,
         gain_attn,
         *returned,
         smem=1,
@@ -1007,10 +995,11 @@
         scratch=[pltpu.VMEM((small_rows, width), F32)],
         stream=False,
     )
+    part_2, small = lax.optimization_barrier((part_2, small))
     part_1, part_2 = spread_out(part_1, 1), spread_out(part_2, 2)
     far_1, far_2 = along(part_1, 1), along(part_2, 1)
     near = finish((part_1, part_2))
-    far_1, far_2, near, small = lax.optimization_barrier((far_1, far_2, near, small))
+    far_1, far_2, near = lax.optimization_barrier((far_1, far_2, near))
     grad_w_output, grad_w_value, grad_w_query, grad_w_key = finish((far_1, far_2), near)
     return (
         layer_output,

time: 217 us -> 217 us (level)
  starting transfers between devices: 78.4 us -> 81.1 us
  waiting for transfers between devices: 64.1 us -> 61.8 us
    ppermute x23, starting transfers between devices: 45.5 us -> 48.5 us  [along(): return lax.ppermute(x, 'wide', pairs(n_wide, k))]
    ppermute x23, waiting for transfers between devices: 30.8 us -> 28 us  [along(): return lax.ppermute(x, 'wide', pairs(n_wide, k))]
where the time goes in v6:
time: 217 us; the launch traced here: 216 us
  starting transfers between devices  81.1 us (37%)
  Pallas kernels  65 us (30%)
  waiting for transfers between devices  61.8 us (28%)
  local copies, waits for them, and re-layouts  5.15 us (2%)
    pallas_call x22, Pallas kernels, call(): pl.pallas_call(body, out_shape=tuple(outs), in_specs=[pl.BlockSpec(memory...  59.4 us
    ppermute x23, starting transfers between devices, along(): return lax.ppermute(x, 'wide', pairs(n_wide, k))  48.5 us
    ppermute x36, waiting for transfers between devices, across(): return lax.ppermute(x, 'narrow', pairs(n_narrow, k))  33.8 us
    ppermute x36, starting transfers between devices, across(): return lax.ppermute(x, 'narrow', pairs(n_narrow, k))  32.6 us
    ppermute x23, waiting for transfers between devices, along(): return lax.ppermute(x, 'wide', pairs(n_wide, k))  28 us
    pallas_call x2, Pallas kernels, finish(): pl.pallas_call(functools.partial(finish_kernel, bool(outs), len(sources))...  5.66 us
  transfers between devices with their start and end apart: 59, of which 26 were waited for; matrix products, arithmetic and copies ran while one was open for 1% of the time, Pallas kernels for 17%

profile of v6, /device:TPU:1, one launch (start us, length us, event | category | flops | bytes accessed | tf_op | source)
XLA Modules:
  0.0 216.2 jit_solution(13106366434877376360)
XLA Ops:
  0.6 11.1 %shard_map.238 = (bf16[256,768]{1,0:T(8,128)(2,1)}, bf16[256,768]{1,0:T(8,128)(2,1)}, bf16[256,768]{1,0:T(8,128)(2,1)}, bf16[12,256,256]{2,1,0:T(8,128)(2,1)}, b...) custom-call(s32[1]{0:T(128)} %bitcast.1.refs_0_, ...), custom_call_target="tpu_custom_call" | custom-call | flops 1409286144 | bytes 10459680 | tf_op jit(solution)/shard_map/pallas_call | solution.py:156
  14.9 2.5 %collective-permute-start.1 = (bf16[80,1536]{1,0:T(8,128)(2,1)S(1)}, bf16[80,1536]{1,0:T(8,128)(2,1)S(1)}, u32[]{:S(2)}, u32[]{:S(2)}) collective-permute-start(bf16[80,1536]{1,0:T(8,128)(2,1)S(1)} %pad_maximum_fusion), channel_id=1, source_target_pairs={{0,2},{1,3},{2,0},{3,1},{4,6},{5,7},{6,4},{7,5},{8,10},{9,11},{10,... | collective-permute-start | bytes 737288 | tf_op jit(solution)/shard_map/ppermute | solution.py:698
  22.5 5.2 %collective-permute-done.3.refs_2_.refs_1_ = bf16[80,1536]{1,0:T(8,128)(2,1)S(1)} collective-permute-done((bf16[80,1536]{1,0:T(8,128)(2,1)S(1)}, bf16[80,1536]{1,0:T(8,128)(2,1)S(1)}, u32[]{:S(2)}, u32[]{:S(2)}) %collective-permute-start.3) | collective-permute-done | bytes 245792 | tf_op jit(solution)/shard_map/ppermute | solution.py:698
  30.4 5.5 %collective-permute-done.2.refs_2_.refs_9_ = bf16[80,1536]{1,0:T(8,128)(2,1)S(1)} collective-permute-done((bf16[80,1536]{1,0:T(8,128)(2,1)S(1)}, bf16[80,1536]{1,0:T(8,128)(2,1)S(1)}, u32[]{:S(2)}, u32[]{:S(2)}) %collective-permute-start.2) | collective-permute-done | bytes 245792 | tf_op jit(solution)/shard_map/ppermute | solution.py:698
  43.5 2.7 %collective-permute-done.15.refs_9_.refs_7_ = bf16[80,1536]{1,0:T(8,128)(2,1)S(1)} collective-permute-done((bf16[80,1536]{1,0:T(8,128)(2,1)S(1)}, bf16[80,1536]{1,0:T(8,128)(2,1)S(1)}, u32[]{:S(2)}, u32[]{:S(2)}) %collective-permute-start.15) | collective-permute-done | bytes 245792 | tf_op jit(solution)/shard_map/ppermute | solution.py:695
  46.9 7.3 %shard_map.240 = (bf16[320,768]{1,0:T(8,128)(2,1)}, bf16[320,768]{1,0:T(8,128)(2,1)}, bf16[320,768]{1,0:T(8,128)(2,1)}, bf16[320,768]{1,0:T(8,128)(2,1)}, bf16[8...) custom-call(bf16[768,768]{1,0:T(8,128)(2,1)} %bitcast.53, ...), custom_call_target="tpu_custom_call" | custom-call | flops 3019898880 | bytes 8257536 | tf_op jit(solution)/shard_map/pallas_call | solution.py:156
  58.4 7.5 %shard_map.239 = (bf16[320,768]{1,0:T(8,128)(2,1)}, bf16[320,768]{1,0:T(8,128)(2,1)}, bf16[320,768]{1,0:T(8,128)(2,1)}, bf16[320,768]{1,0:T(8,128)(2,1)}, bf16[8...) custom-call(bf16[768,768]{1,0:T(8,128)(2,1)} %bitcast.54, ...), custom_call_target="tpu_custom_call" | custom-call | flops 3019898880 | bytes 8257536 | tf_op jit(solution)/shard_map/pallas_call | solution.py:156
  70.7 4.9 %collective-permute-done.18 = bf16[80,1536]{1,0:T(8,128)(2,1)S(1)} collective-permute-done((bf16[80,1536]{1,0:T(8,128)(2,1)S(1)}, bf16[80,1536]{1,0:T(8,128)(2,1)S(1)}, u32[]{:S(2)}, u32[]{:S(2)}) %collective-permute-start.18) | collective-permute-done | bytes 245792 | tf_op jit(solution)/shard_map/ppermute | solution.py:695
  76.4 12.2 %collective-permute-start.27 = (bf16[40,1536]{1,0:T(8,128)(2,1)S(1)}, bf16[40,1536]{1,0:T(8,128)(2,1)S(1)}, u32[]{:S(2)}, u32[]{:S(2)}) collective-permute-start(bf16[40,1536]{1,0:T(8,128)(2,1)S(1)} %get-tuple-element.264), channel_id=1, source_target_pairs={{0,1},{1,0},{2,3},{3,2},{4,5},{5,4},{6,7},{7,6},{8,9},{9,8},{10,11... | collective-permute-start | bytes 368648 | tf_op jit(solution)/shard_map/ppermute | solution.py:698
  88.8 3.0 %collective-permute-start.23 = (bf16[40,1536]{1,0:T(8,128)(2,1)S(1)}, bf16[40,1536]{1,0:T(8,128)(2,1)S(1)}, u32[]{:S(2)}, u32[]{:S(2)}) collective-permute-start(bf16[40,1536]{1,0:T(8,128)(2,1)S(1)} %get-tuple-element.261), channel_id=1, source_target_pairs={{0,4},{1,5},{2,6},{3,7},{4,0},{5,1},{6,2},{7,3},{8,12},{9,13},{10,... | collective-permute-start | bytes 368648 | tf_op jit(solution)/shard_map/ppermute | solution.py:698
  92.6 4.7 %collective-permute-done.20 = bf16[80,1536]{1,0:T(8,128)(2,1)S(1)} collective-permute-done((bf16[80,1536]{1,0:T(8,128)(2,1)S(1)}, bf16[80,1536]{1,0:T(8,128)(2,1)S(1)}, u32[]{:S(2)}, u32[]{:S(2)}) %collective-permute-start.20) | collective-permute-done | bytes 245792 | tf_op jit(solution)/shard_map/ppermute | solution.py:695
  97.4 3.9 %collective-permute-start.28 = (bf16[40,1536]{1,0:T(8,128)(2,1)S(1)}, bf16[40,1536]{1,0:T(8,128)(2,1)S(1)}, u32[]{:S(2)}, u32[]{:S(2)}) collective-permute-start(bf16[40,1536]{1,0:T(8,128)(2,1)S(1)} %get-tuple-element.262), channel_id=1, source_target_pairs={{0,3},{1,2},{2,1},{3,0},{4,7},{5,6},{6,5},{7,4},{8,11},{9,10},{10,... | collective-permute-start | bytes 368648 | tf_op jit(solution)/shard_map/ppermute | solution.py:698
  106.2 8.5 %shard_map.241 = (f32[1,768,768]{2,1,0:T(8,128)}, f32[1,768,768]{2,1,0:T(8,128)}) custom-call(bf16[80,1536]{1,0:T(8,128)(2,1)} %copy-done.2, bf16[80,1536]{1,0:T(8,128)(2,1)} %copy-done.17, bf16[80,1536]{1,0:T(8,128)(2,1)} %copy-done.18, bf16[80,1536]{1,0:T(8,128)(2,1)} %copy-done.21, bf16[80,1536]{1,0:T(8,128)(2,1)} %copy-done.19, ...), custom_call_target="tpu_custom_call" | custom-call | flops 3019898880 | bytes 12582912 | tf_op jit(solution)/shard_map/pallas_call | solution.py:156
  115.6 14.6 %shard_map.242 = (bf16[256,768]{1,0:T(8,128)(2,1)}, bf16[256,768]{1,0:T(8,128)(2,1)}, bf16[400,1536]{1,0:T(8,128)(2,1)}, bf16[400,1536]{1,0:T(8,128)(2,1)}, bf16...) custom-call(s32[1]{0:T(128)} %bitcast.refs_0_, f32[16,256]{1,0:T(8,128)} %get-tuple-element.133.refs_1_, ...), custom_call_target="tpu_custom_call" | custom-call | flops 3019898880 | bytes 16064512 | tf_op jit(solution)/shard_map/pallas_call | solution.py:156
  130.9 3.5 %collective-permute-done.45.refs_2_ = bf16[384,1536]{1,0:T(8,128)(2,1)} collective-permute-done((bf16[384,1536]{1,0:T(8,128)(2,1)}, bf16[384,1536]{1,0:T(8,128)(2,1)}, u32[]{:S(2)}, u32[]{:S(2)}) %collective-permute-start.45) | collective-permute-done | bytes 1179680 | tf_op jit(solution)/shard_map/ppermute | solution.py:698
  141.2 6.6 %collective-permute-done.33.refs_4_ = bf16[192,768]{1,0:T(8,128)(2,1)S(1)} collective-permute-done((bf16[192,768]{1,0:T(8,128)(2,1)S(1)}, bf16[192,768]{1,0:T(8,128)(2,1)S(1)}, u32[]{:S(2)}, u32[]{:S(2)}) %collective-permute-start.33) | collective-permute-done | bytes 294944 | tf_op jit(solution)/shard_map/ppermute | solution.py:695
  156.3 2.5 %collective-permute-done.47.refs_2_ = bf16[96,768]{1,0:T(8,128)(2,1)S(1)} collective-permute-done((bf16[96,768]{1,0:T(8,128)(2,1)S(1)}, bf16[96,768]{1,0:T(8,128)(2,1)S(1)}, u32[]{:S(2)}, u32[]{:S(2)}) %collective-permute-start.47) | collective-permute-done | bytes 147488 | tf_op jit(solution)/shard_map/ppermute | solution.py:695
  169.3 4.5 %collective-permute-done.37.refs_1_ = bf16[80,768]{1,0:T(8,128)(2,1)S(1)} collective-permute-done((bf16[80,768]{1,0:T(8,128)(2,1)S(1)}, bf16[80,768]{1,0:T(8,128)(2,1)S(1)}, u32[]{:S(2)}, u32[]{:S(2)}) %collective-permute-start.37) | collective-permute-done | bytes 122912 | tf_op jit(solution)/shard_map/ppermute | solution.py:698
  181.4 3.1 %collective-permute-done.39.refs_2_ = bf16[48,1536]{1,0:T(8,128)(2,1)S(1)} collective-permute-done((bf16[48,1536]{1,0:T(8,128)(2,1)S(1)}, bf16[48,1536]{1,0:T(8,128)(2,1)S(1)}, u32[]{:S(2)}, u32[]{:S(2)}) %collective-permute-start.39) | collective-permute-done | bytes 147488 | tf_op jit(solution)/shard_map/ppermute | solution.py:698
  195.5 3.2 %collective-permute-done.42.refs_2_ = bf16[192,768]{1,0:T(8,128)(2,1)S(1)} collective-permute-done((bf16[192,768]{1,0:T(8,128)(2,1)S(1)}, bf16[192,768]{1,0:T(8,128)(2,1)S(1)}, u32[]{:S(2)}, u32[]{:S(2)}) %collective-permute-start.42) | collective-permute-done | bytes 294944 | tf_op jit(solution)/shard_map/ppermute | solution.py:695
  199.8 7.4 %collective-permute-start.44 = (bf16[384,1536]{1,0:T(8,128)(2,1)S(1)}, bf16[384,1536]{1,0:T(8,128)(2,1)S(1)}, u32[]{:S(2)}, u32[]{:S(2)}) collective-permute-start(bf16[384,1536]{1,0:T(8,128)(2,1)S(1)} %shard_map.250.refs_0_), channel_id=1, source_target_pairs={{0,1},{1,0},{2,3},{3,2},{4,5},{5,4},{6,7},{7,6},{8,9},{9,8},{10,11... | collective-permute-start | bytes 3538952 | tf_op jit(solution)/shard_map/ppermute | solution.py:698
  207.8 2.5 %collective-permute-start.58 = (bf16[384,1536]{1,0:T(8,128)(2,1)S(1)}, bf16[384,1536]{1,0:T(8,128)(2,1)S(1)}, u32[]{:S(2)}, u32[]{:S(2)}) collective-permute-start(bf16[384,1536]{1,0:T(8,128)(2,1)S(1)} %shard_map.259.refs_1_), channel_id=1, source_target_pairs={{0,1},{1,0},{2,3},{3,2},{4,5},{5,4},{6,7},{7,6},{8,9},{9,8},{10,11... | collective-permute-start | bytes 3538952 | tf_op jit(solution)/shard_map/ppermute | solution.py:698
  210.3 2.8 %shard_map.260 = (f32[768,768]{1,0:T(8,128)}, f32[768,768]{1,0:T(8,128)}, f32[768,768]{1,0:T(8,128)}, f32[768,768]{1,0:T(8,128)}) custom-call(s32[5]{0:T(128)S(1)} %stack.20.refs_0_.place_ref, bf16[384,1536]{1,0:T(8,128)(2,1)S(1)} %shard_map.250.refs_0_, bf16[384,1536]{1,0:T(8,128)(2,1)S(1)} %shard_map.259.refs_1_), custom_call_target="tpu_custom_call" | custom-call | tf_op jit(solution)/shard_map/pallas_call | solution.py:965
  213.2 2.8 %shard_map.261 = (f32[768,768]{1,0:T(8,128)}, f32[768,768]{1,0:T(8,128)}, f32[768,768]{1,0:T(8,128)}, f32[768,768]{1,0:T(8,128)}) custom-call(s32[5]{0:T(128)S(1)} %stack.20.refs_0_.place_ref, bf16[384,1536]{1,0:T(8,128)(2,1)S(1)} %collective-permute-done.44.refs_0_, ...), custom_call_target="tpu_custom_call", output_to_operand_aliasing={{0}: (3, {}), {1}: (4, {}), {2}: (5, {}), {3}: (6, {})} | custom-call | tf_op jit(solution)/shard_map/pallas_call | solution.py:965
  (214 shorter events, 82.2 us)
Async XLA Ops:
  14.9 14.0 %collective-permute-start.1 = (bf16[80,1536]{1,0:T(8,128)(2,1)S(1)}, bf16[80,1536]{1,0:T(8,128)(2,1)S(1)}, u32[]{:S(2)}, u32[]{:S(2)}) collective-permute-start(bf16[80,1536]{1,0:T(8,128)(2,1)S(1)} %pad_maximum_fusion), channel_id=1, source_target_pairs={{0,2},{1,3},{2,0},{3,1},{4,6},{5,7},{6,4},{7,5},{8,10},{9,11},{10,... | collective-permute-start | bytes 737288 | tf_op jit(solution)/shard_map/ppermute | solution.py:698
  17.5 10.3 %collective-permute-start.3 = (bf16[80,1536]{1,0:T(8,128)(2,1)S(1)}, bf16[80,1536]{1,0:T(8,128)(2,1)S(1)}, u32[]{:S(2)}, u32[]{:S(2)}) collective-permute-start(bf16[80,1536]{1,0:T(8,128)(2,1)S(1)} %pad_maximum_fusion.2), channel_id=1, source_target_pairs={{0,4},{1,5},{2,6},{3,7},{4,0},{5,1},{6,2},{7,3},{8,12},{9,13},{10,... | collective-permute-start | bytes 737288 | tf_op jit(solution)/shard_map/ppermute | solution.py:698
  19.9 10.3 %collective-permute-start.12 = (bf16[80,1536]{1,0:T(8,128)(2,1)S(1)}, bf16[80,1536]{1,0:T(8,128)(2,1)S(1)}, u32[]{:S(2)}, u32[]{:S(2)}) collective-permute-start(bf16[80,1536]{1,0:T(8,128)(2,1)S(1)} %pad_maximum_fusion.3.refs_1_.refs_0_), channel_id=1, source_target_pairs={{0,8},{8,0},{16,24},{24,16},{1,9},{9,1},{17,25},{25,17},{2,10},{10... | collective-permute-start | bytes 737288 | tf_op jit(solution)/shard_map/ppermute | solution.py:695
  21.1 14.8 %collective-permute-start.5 = (bf16[80,1536]{1,0:T(8,128)(2,1)S(1)}, bf16[80,1536]{1,0:T(8,128)(2,1)S(1)}, u32[]{:S(2)}, u32[]{:S(2)}) collective-permute-start(bf16[80,1536]{1,0:T(8,128)(2,1)S(1)} %pad_maximum_fusion.3.refs_1_.refs_0_), channel_id=1, source_target_pairs={{0,16},{8,24},{16,0},{24,8},{1,17},{9,25},{17,1},{25,9},{2,18},{10... | collective-permute-start | bytes 737288 | tf_op jit(solution)/shard_map/ppermute | solution.py:695
  22.4 13.5 %collective-permute-start.2 = (bf16[80,1536]{1,0:T(8,128)(2,1)S(1)}, bf16[80,1536]{1,0:T(8,128)(2,1)S(1)}, u32[]{:S(2)}, u32[]{:S(2)}) collective-permute-start(bf16[80,1536]{1,0:T(8,128)(2,1)S(1)} %pad_maximum_fusion.1), channel_id=1, source_target_pairs={{0,6},{1,7},{2,4},{3,5},{4,2},{5,3},{6,0},{7,1},{8,14},{9,15},{10,... | collective-permute-start | bytes 737288 | tf_op jit(solution)/shard_map/ppermute | solution.py:698
  38.7 16.8 %collective-permute-start.8 = (bf16[80,1536]{1,0:T(8,128)(2,1)S(1)}, bf16[80,1536]{1,0:T(8,128)(2,1)S(1)}, u32[]{:S(2)}, u32[]{:S(2)}) collective-permute-start(bf16[80,1536]{1,0:T(8,128)(2,1)S(1)} %collective-permute-done.1.refs_1_.refs_8_), channel_id=1, source_target_pairs={{0,16},{8,24},{16,0},{24,8},{1,17},{9,25},{17,1},{25,9},{2,18},{10... | collective-permute-start | bytes 737288 | tf_op jit(solution)/shard_map/ppermute | solution.py:695
  38.9 18.0 %collective-permute-start.7 = (bf16[80,1536]{1,0:T(8,128)(2,1)S(1)}, bf16[80,1536]{1,0:T(8,128)(2,1)S(1)}, u32[]{:S(2)}, u32[]{:S(2)}) collective-permute-start(bf16[80,1536]{1,0:T(8,128)(2,1)S(1)} %collective-permute-done.2.refs_2_.refs_9_), channel_id=1, source_target_pairs={{0,8},{8,0},{16,24},{24,16},{1,9},{9,1},{17,25},{25,17},{2,10},{10... | collective-permute-start | bytes 737288 | tf_op jit(solution)/shard_map/ppermute | solution.py:695
  41.0 15.9 %collective-permute-start.10 = (bf16[80,1536]{1,0:T(8,128)(2,1)S(1)}, bf16[80,1536]{1,0:T(8,128)(2,1)S(1)}, u32[]{:S(2)}, u32[]{:S(2)}) collective-permute-start(bf16[80,1536]{1,0:T(8,128)(2,1)S(1)} %collective-permute-done.6.refs_3_.refs_10_), channel_id=1, source_target_pairs={{0,16},{8,24},{16,0},{24,8},{1,17},{9,25},{17,1},{25,9},{2,18},{10... | collective-permute-start | bytes 737288 | tf_op jit(solution)/shard_map/ppermute | solution.py:695
  42.5 14.4 %collective-permute-start.11 = (bf16[80,1536]{1,0:T(8,128)(2,1)S(1)}, bf16[80,1536]{1,0:T(8,128)(2,1)S(1)}, u32[]{:S(2)}, u32[]{:S(2)}) collective-permute-start(bf16[80,1536]{1,0:T(8,128)(2,1)S(1)} %collective-permute-done.9.refs_7_.refs_13_), channel_id=1, source_target_pairs={{0,8},{8,0},{16,24},{24,16},{1,9},{9,1},{17,25},{25,17},{2,10},{10... | collective-permute-start | bytes 737288 | tf_op jit(solution)/shard_map/ppermute | solution.py:695
  54.2 13.2 %collective-permute-start.16 = (bf16[2,80,1536]{2,1,0:T(8,128)(2,1)}, bf16[2,80,1536]{2,1,0:T(8,128)(2,1)S(1)}, u32[]{:S(2)}, u32[]{:S(2)}) collective-permute-start(bf16[2,80,1536]{2,1,0:T(8,128)(2,1)} %get-tuple-element.161), channel_id=1, source_target_pairs={{0,8},{8,0},{16,24},{24,16},{1,9},{9,1},{17,25},{25,17},{2,10},{10... | collective-permute-start | bytes 1474568 | tf_op jit(solution)/shard_map/ppermute | solution.py:695
  55.5 12.0 %collective-permute-start.17 = (bf16[2,80,1536]{2,1,0:T(8,128)(2,1)}, bf16[2,80,1536]{2,1,0:T(8,128)(2,1)S(1)}, u32[]{:S(2)}, u32[]{:S(2)}) collective-permute-start(bf16[2,80,1536]{2,1,0:T(8,128)(2,1)} %get-tuple-element.162), channel_id=1, source_target_pairs={{0,16},{8,24},{16,0},{24,8},{1,17},{9,25},{17,1},{25,9},{2,18},{10... | collective-permute-start | bytes 1474568 | tf_op jit(solution)/shard_map/ppermute | solution.py:695
  68.9 19.7 %collective-permute-start.22 = (bf16[80,1536]{1,0:T(8,128)(2,1)S(1)}, bf16[80,1536]{1,0:T(8,128)(2,1)S(1)}, u32[]{:S(2)}, u32[]{:S(2)}) collective-permute-start(bf16[80,1536]{1,0:T(8,128)(2,1)S(1)} %fusion.10), channel_id=1, source_target_pairs={{0,8},{8,0},{16,24},{24,16},{1,9},{9,1},{17,25},{25,17},{2,10},{10... | collective-permute-start | bytes 737288 | tf_op jit(solution)/shard_map/ppermute | solution.py:695
  70.2 21.6 %collective-permute-start.19 = (bf16[2,80,1536]{2,1,0:T(8,128)(2,1)S(1)}, bf16[2,80,1536]{2,1,0:T(8,128)(2,1)S(1)}, u32[]{:S(2)}, u32[]{:S(2)}) collective-permute-start(bf16[2,80,1536]{2,1,0:T(8,128)(2,1)S(1)} %copy-done.15), channel_id=1, source_target_pairs={{0,8},{8,0},{16,24},{24,16},{1,9},{9,1},{17,25},{25,17},{2,10},{10... | collective-permute-start | bytes 1474568 | tf_op jit(solution)/shard_map/ppermute | solution.py:695
  70.4 22.1 %collective-permute-start.24 = (bf16[2,80,1536]{2,1,0:T(8,128)(2,1)S(1)}, bf16[2,80,1536]{2,1,0:T(8,128)(2,1)S(1)}, u32[]{:S(2)}, u32[]{:S(2)}) collective-permute-start(bf16[2,80,1536]{2,1,0:T(8,128)(2,1)S(1)} %copy-done.14), channel_id=1, source_target_pairs={{0,16},{8,24},{16,0},{24,8},{1,17},{9,25},{17,1},{25,9},{2,18},{10... | collective-permute-start | bytes 1474568 | tf_op jit(solution)/shard_map/ppermute | solution.py:695
  76.4 26.3 %collective-permute-start.27 = (bf16[40,1536]{1,0:T(8,128)(2,1)S(1)}, bf16[40,1536]{1,0:T(8,128)(2,1)S(1)}, u32[]{:S(2)}, u32[]{:S(2)}) collective-permute-start(bf16[40,1536]{1,0:T(8,128)(2,1)S(1)} %get-tuple-element.264), channel_id=1, source_target_pairs={{0,1},{1,0},{2,3},{3,2},{4,5},{5,4},{6,7},{7,6},{8,9},{9,8},{10,11... | collective-permute-start | bytes 368648 | tf_op jit(solution)/shard_map/ppermute | solution.py:698
  88.7 15.9 %collective-permute-start.29 = (bf16[40,1536]{1,0:T(8,128)(2,1)S(1)}, bf16[40,1536]{1,0:T(8,128)(2,1)S(1)}, u32[]{:S(2)}, u32[]{:S(2)}) collective-permute-start(bf16[40,1536]{1,0:T(8,128)(2,1)S(1)} %get-tuple-element.260), channel_id=1, source_target_pairs={{0,5},{1,4},{2,7},{3,6},{4,1},{5,0},{6,3},{7,2},{8,13},{9,12},{10,... | collective-permute-start | bytes 368648 | tf_op jit(solution)/shard_map/ppermute | solution.py:698
  88.8 25.9 %collective-permute-start.23 = (bf16[40,1536]{1,0:T(8,128)(2,1)S(1)}, bf16[40,1536]{1,0:T(8,128)(2,1)S(1)}, u32[]{:S(2)}, u32[]{:S(2)}) collective-permute-start(bf16[40,1536]{1,0:T(8,128)(2,1)S(1)} %get-tuple-element.261), channel_id=1, source_target_pairs={{0,4},{1,5},{2,6},{3,7},{4,0},{5,1},{6,2},{7,3},{8,12},{9,13},{10,... | collective-permute-start | bytes 368648 | tf_op jit(solution)/shard_map/ppermute | solution.py:698
  97.4 17.4 %collective-permute-start.28 = (bf16[40,1536]{1,0:T(8,128)(2,1)S(1)}, bf16[40,1536]{1,0:T(8,128)(2,1)S(1)}, u32[]{:S(2)}, u32[]{:S(2)}) collective-permute-start(bf16[40,1536]{1,0:T(8,128)(2,1)S(1)} %get-tuple-element.262), channel_id=1, source_target_pairs={{0,3},{1,2},{2,1},{3,0},{4,7},{5,6},{6,5},{7,4},{8,11},{9,10},{10,... | collective-permute-start | bytes 368648 | tf_op jit(solution)/shard_map/ppermute | solution.py:698
  101.3 13.5 %collective-permute-start.21 = (bf16[40,1536]{1,0:T(8,128)(2,1)S(1)}, bf16[40,1536]{1,0:T(8,128)(2,1)S(1)}, u32[]{:S(2)}, u32[]{:S(2)}) collective-permute-start(bf16[40,1536]{1,0:T(8,128)(2,1)S(1)} %get-tuple-element.263), channel_id=1, source_target_pairs={{0,2},{1,3},{2,0},{3,1},{4,6},{5,7},{6,4},{7,5},{8,10},{9,11},{10,... | collective-permute-start | bytes 368648 | tf_op jit(solution)/shard_map/ppermute | solution.py:698
  102.7 12.1 %collective-permute-start.30 = (bf16[40,1536]{1,0:T(8,128)(2,1)S(1)}, bf16[40,1536]{1,0:T(8,128)(2,1)S(1)}, u32[]{:S(2)}, u32[]{:S(2)}) collective-permute-start(bf16[40,1536]{1,0:T(8,128)(2,1)S(1)} %get-tuple-element.258), channel_id=1, source_target_pairs={{0,7},{1,6},{2,5},{3,4},{4,3},{5,2},{6,1},{7,0},{8,15},{9,14},{10,... | collective-permute-start | bytes 368648 | tf_op jit(solution)/shard_map/ppermute | solution.py:698
  137.3 15.0 %collective-permute-start.46 = (bf16[192,1536]{1,0:T(8,128)(2,1)S(1)}, bf16[192,1536]{1,0:T(8,128)(2,1)S(1)}, u32[]{:S(2)}, u32[]{:S(2)}) collective-permute-start(bf16[192,1536]{1,0:T(8,128)(2,1)S(1)} %get-tuple-element.214), channel_id=1, source_target_pairs={{0,2},{1,3},{2,0},{3,1},{4,6},{5,7},{6,4},{7,5},{8,10},{9,11},{10,... | collective-permute-start | bytes 1769480 | tf_op jit(solution)/shard_map/ppermute | solution.py:698
  193.4 13.7 %collective-permute-start.56 = (bf16[192,768]{1,0:T(8,128)(2,1)S(1)}, bf16[192,768]{1,0:T(8,128)(2,1)S(1)}, u32[]{:S(2)}, u32[]{:S(2)}) collective-permute-start(bf16[192,768]{1,0:T(8,128)(2,1)S(1)} %get-tuple-element.232.refs_1_), channel_id=1, source_target_pairs={{0,8},{8,0},{16,24},{24,16},{1,9},{9,1},{17,25},{25,17},{2,10},{10... | collective-permute-start | bytes 884744 | tf_op jit(solution)/shard_map/ppermute | solution.py:695
  193.8 13.3 %collective-permute-start.57 = (bf16[192,768]{1,0:T(8,128)(2,1)S(1)}, bf16[192,768]{1,0:T(8,128)(2,1)S(1)}, u32[]{:S(2)}, u32[]{:S(2)}) collective-permute-start(bf16[192,768]{1,0:T(8,128)(2,1)S(1)} %get-tuple-element.233.refs_3_), channel_id=1, source_target_pairs={{0,16},{8,24},{16,0},{24,8},{1,17},{9,25},{17,1},{25,9},{2,18},{10... | collective-permute-start | bytes 884744 | tf_op jit(solution)/shard_map/ppermute | solution.py:695
  199.8 13.4 %collective-permute-start.44 = (bf16[384,1536]{1,0:T(8,128)(2,1)S(1)}, bf16[384,1536]{1,0:T(8,128)(2,1)S(1)}, u32[]{:S(2)}, u32[]{:S(2)}) collective-permute-start(bf16[384,1536]{1,0:T(8,128)(2,1)S(1)} %shard_map.250.refs_0_), channel_id=1, source_target_pairs={{0,1},{1,0},{2,3},{3,2},{4,5},{5,4},{6,7},{7,6},{8,9},{9,8},{10,11... | collective-permute-start | bytes 3538952 | tf_op jit(solution)/shard_map/ppermute | solution.py:698
  (73 other events, 563.8 us)
